TPU v7x, 32 devices: a whole 2x2x4 slice. The times are simulated.
32 devices in a mesh: fsdp: 32 (over z, y, x, core).
Axes of the slice: x: 2, y: 2, z: 4, core: 2. Of those that a mesh axis runs over, the one named last changes fastest.
Arguments:
- src_tokens: bfloat16 [32768, 512], P('fsdp'), may hold values from -6 to 6
- tgt_tokens: bfloat16 [32768, 512], P('fsdp'), may hold values from -6 to 6
- src_lengths: int32 [32, 16], P('fsdp'), may hold values from 0 to 128, as said below
- tgt_lengths: int32 [32, 16], P('fsdp'), may hold values from 0 to 128, as said below
- enc_weights: bfloat16 [3147776], P('fsdp'), may hold values from -2 to 2
- dec_weights: bfloat16 [4197376], P('fsdp'), may hold values from -2 to 2
- cotangent: bfloat16 [32768, 512], P('fsdp'), may hold values from -6 to 6, as said below
Outputs:
- decoder_out: bfloat16 [32768, 512], P('fsdp')
- src_grad: float32 [32768, 512], P('fsdp')
- tgt_grad: float32 [32768, 512], P('fsdp')
- enc_grad: float32 [3147776], P('fsdp')
- dec_grad: float32 [4197376], P('fsdp')
Inputs may be any that keep to these rules, and one draw needn't show every extreme that they name: `src_lengths`: in each row the sentences fill the first slots and later slots hold 0; a row's lengths sum to at most 1024. A source row and the target row of the same index hold the same number c of sentences, 8 to 16, each of 1024 // c minus at most a quarter of that tokens. Some row holds 16 sentences and some sentence has 128 tokens. `tgt_lengths`: as for src_lengths, with the same count of sentences in each row. `cotangent`: zero at every slot of a target row at or past the sum of that row's tgt_lengths.
All inputs are finite; a program needn't handle non-finite values.
Results may differ from a plain program's by a relative error of at most 0.017.
Values may be sent and summed in bfloat16 or wider, within the bound.
No kernel may reach another device: no remote copies, remote signals or barrier semaphores. Data moves between devices by JAX's collectives and lax.ppermute only.
A program may use at most 384 MiB of HBM per device.

v0:
```python
import math

import jax
import jax.numpy as jnp
from jax import lax
from jax.sharding import PartitionSpec as P

D = 512
HEADS = 8
FF = 2048


EPSILON = 1e-05
MASKED = -1e30


def product(left, right):
    return jnp.dot(left, right, preferred_element_type=jnp.float32)


def outer_sum(left, right):
    return lax.dot_general(
        left, right, (((0,), (0,)), ((), ())), preferred_element_type=jnp.float32
    )


def back_product(left, right):
    return lax.dot_general(
        left, right, (((1,), (1,)), ((), ())), preferred_element_type=jnp.float32
    )


def encoder_layout():
    return [(D, D)] * 4 + [(D, FF), (FF, D)] + [(D,)] * 4


def decoder_layout():
    return [(D, D)] * 8 + [(D, FF), (FF, D)] + [(D,)] * 6


def unpack(flat, layout):
    pieces = []
    offset = 0
    for extents in layout:
        amount = math.prod(extents)
        pieces.append(flat[offset : offset + amount].reshape(extents))
        offset = offset + amount
    return pieces


def segments(lengths, width):
    ends = jnp.cumsum(lengths)
    places = jnp.arange(width, dtype=jnp.int32)
    return jnp.sum((places[:, None] >= ends[None, :]).astype(jnp.int32), axis=1)


def allowed_of(seg_query, seg_keys, causal):
    allowed = seg_query[:, None] == seg_keys[None, :]
    if causal:
        places = jnp.arange(seg_query.shape[0], dtype=jnp.int32)
        allowed = allowed & (places[:, None] >= places[None, :])
    return allowed


def norm(values, gain, bias):
    center = jnp.mean(values, axis=-1, keepdims=True)
    shifted = values - center
    spread = jnp.mean(shifted * shifted, axis=-1, keepdims=True)
    return shifted * lax.rsqrt(spread + EPSILON) * gain + bias


def gelu_exact(values):
    return jax.nn.gelu(values, approximate=False)


def split_heads(block):
    return block.reshape(block.shape[0], HEADS, block.shape[1] // HEADS)


def shares_of(heads_query, heads_keys, allowed):
    temper = heads_query.shape[-1] ** (-0.5)
    products = jnp.einsum(
        "qhd,khd->hqk", heads_query, heads_keys, preferred_element_type=jnp.float32
    )
    return (jnp.where(allowed[None], products * temper, MASKED), temper)


def attend_forward(query, keys, values, seg_query, seg_keys, causal):
    heads_query = split_heads(query)
    scores, temper = shares_of(
        heads_query, split_heads(keys), allowed_of(seg_query, seg_keys, causal)
    )
    highest = jnp.max(scores, axis=-1, keepdims=True)
    weights = jnp.exp(scores - highest)
    totals = jnp.sum(weights, axis=-1, keepdims=True)
    shares = (weights / totals).astype(jnp.bfloat16)
    mixed = jnp.einsum(
        "hqk,khd->qhd", shares, split_heads(values), preferred_element_type=jnp.float32
    )
    return (mixed.reshape(query.shape[0], -1).astype(jnp.bfloat16), highest, totals)


def attend_backward(query, keys, values, grad_mixed, highest, totals, seg_query, seg_keys, causal):
    heads_query = split_heads(query)
    heads_keys = split_heads(keys)
    heads_grad = split_heads(grad_mixed)
    allowed = allowed_of(seg_query, seg_keys, causal)
    scores, temper = shares_of(heads_query, heads_keys, allowed)
    shares = jnp.exp(scores - highest) / totals
    grad_shares = jnp.einsum(
        "qhd,khd->hqk", heads_grad, split_heads(values), preferred_element_type=jnp.float32
    )
    inner = jnp.sum(shares * grad_shares, axis=-1, keepdims=True)
    grad_scores = (jnp.where(allowed[None], shares * (grad_shares - inner), 0.0) * temper).astype(
        jnp.bfloat16
    )
    grad_query = jnp.einsum(
        "hqk,khd->qhd", grad_scores, heads_keys, preferred_element_type=jnp.float32
    )
    grad_keys = jnp.einsum(
        "hqk,qhd->khd", grad_scores, heads_query, preferred_element_type=jnp.float32
    )
    grad_values = jnp.einsum(
        "hqk,qhd->khd", shares.astype(jnp.bfloat16), heads_grad, preferred_element_type=jnp.float32
    )
    count_query = query.shape[0]
    count_keys = keys.shape[0]
    return (
        grad_query.reshape(count_query, -1).astype(jnp.bfloat16),
        grad_keys.reshape(count_keys, -1).astype(jnp.bfloat16),
        grad_values.reshape(count_keys, -1).astype(jnp.bfloat16),
    )


def attend_rows(query, keys, values, seg_query, seg_keys, causal):

    def one_row(items):
        return attend_forward(items[0], items[1], items[2], items[3], items[4], causal)

    return lax.map(one_row, (query, keys, values, seg_query, seg_keys))


def attend_back_rows(query, keys, values, grad_mixed, highest, totals, seg_query, seg_keys, causal):

    def one_row(items):
        return attend_backward(
            items[0], items[1], items[2], items[3], items[4], items[5], items[6], items[7], causal
        )

    return lax.map(one_row, (query, keys, values, grad_mixed, highest, totals, seg_query, seg_keys))


def on_device(
    src_tokens, tgt_tokens, src_lengths, tgt_lengths, enc_weights, dec_weights, cotangent
):
    batch = src_lengths.shape[0]
    length = src_tokens.shape[0] // batch

    def row_segments(lengths):
        return segments(lengths, length)

    def to_rows(block):
        return block.reshape(batch, length, block.shape[-1])

    def to_tokens(block):
        return block.reshape(batch * length, block.shape[-1])

    src_segment = jax.vmap(row_segments)(src_lengths)
    tgt_segment = jax.vmap(row_segments)(tgt_lengths)
    enc_flat = lax.all_gather(enc_weights, "fsdp", axis=0, tiled=True)
    w_query, w_key, w_value, w_out, w_up, w_down, gain_attn, bias_attn, gain_ffn, bias_ffn = unpack(
        enc_flat, encoder_layout()
    )
    enc_query = product(src_tokens, w_query).astype(jnp.bfloat16)
    enc_keys = product(src_tokens, w_key).astype(jnp.bfloat16)
    enc_values = product(src_tokens, w_value).astype(jnp.bfloat16)
    enc_attn, enc_highest, enc_totals = attend_rows(
        to_rows(enc_query), to_rows(enc_keys), to_rows(enc_values), src_segment, src_segment, False
    )
    enc_attn = to_tokens(enc_attn)
    enc_mid, back_mid = jax.vjp(
        norm,
        src_tokens.astype(jnp.float32) + product(enc_attn, w_out),
        gain_attn.astype(jnp.float32),
        bias_attn.astype(jnp.float32),
    )
    enc_mid_low = enc_mid.astype(jnp.bfloat16)
    enc_act, back_enc_act = jax.vjp(gelu_exact, product(enc_mid_low, w_up))
    enc_hidden = enc_act.astype(jnp.bfloat16)
    encoded, back_encoded = jax.vjp(
        norm,
        enc_mid + product(enc_hidden, w_down) + src_tokens.astype(jnp.float32),
        gain_ffn.astype(jnp.float32),
        bias_ffn.astype(jnp.float32),
    )
    encoded_low = encoded.astype(jnp.bfloat16)
    dec_flat = lax.all_gather(dec_weights, "fsdp", axis=0, tiled=True)
    (
        self_query,
        self_key,
        self_value,
        self_out,
        cross_query,
        cross_key,
        cross_value,
        cross_out,
        dec_up,
        dec_down,
        gain_self,
        bias_self,
        gain_cross,
        bias_cross,
        gain_last,
        bias_last,
    ) = unpack(dec_flat, decoder_layout())
    dec_query = product(tgt_tokens, self_query).astype(jnp.bfloat16)
    dec_keys = product(tgt_tokens, self_key).astype(jnp.bfloat16)
    dec_values = product(tgt_tokens, self_value).astype(jnp.bfloat16)
    dec_attn, dec_highest, dec_totals = attend_rows(
        to_rows(dec_query), to_rows(dec_keys), to_rows(dec_values), tgt_segment, tgt_segment, True
    )
    dec_attn = to_tokens(dec_attn)
    first_norm, back_first = jax.vjp(
        norm,
        tgt_tokens.astype(jnp.float32) + product(dec_attn, self_out),
        gain_self.astype(jnp.float32),
        bias_self.astype(jnp.float32),
    )
    first_low = first_norm.astype(jnp.bfloat16)
    query_cross = product(first_low, cross_query).astype(jnp.bfloat16)
    keys_cross = product(encoded_low, cross_key).astype(jnp.bfloat16)
    values_cross = product(encoded_low, cross_value).astype(jnp.bfloat16)
    attn_cross, cross_highest, cross_totals = attend_rows(
        to_rows(query_cross),
        to_rows(keys_cross),
        to_rows(values_cross),
        tgt_segment,
        src_segment,
        False,
    )
    attn_cross = to_tokens(attn_cross)
    second_norm, back_second = jax.vjp(
        norm,
        first_norm + product(attn_cross, cross_out),
        gain_cross.astype(jnp.float32),
        bias_cross.astype(jnp.float32),
    )
    second_low = second_norm.astype(jnp.bfloat16)
    dec_act, back_dec_act = jax.vjp(gelu_exact, product(second_low, dec_up))
    dec_hidden = dec_act.astype(jnp.bfloat16)
    final, back_final = jax.vjp(
        norm,
        second_norm + product(dec_hidden, dec_down) + tgt_tokens.astype(jnp.float32),
        gain_last.astype(jnp.float32),
        bias_last.astype(jnp.float32),
    )
    dec_flat = lax.all_gather(dec_weights, "fsdp", axis=0, tiled=True)
    (
        self_query,
        self_key,
        self_value,
        self_out,
        cross_query,
        cross_key,
        cross_value,
        cross_out,
        dec_up,
        dec_down,
        gain_self,
        bias_self,
        gain_cross,
        bias_cross,
        gain_last,
        bias_last,
    ) = unpack(dec_flat, decoder_layout())
    grad_sum_last, grad_gain_last, grad_bias_last = back_final(cotangent.astype(jnp.float32))
    grad_branch = grad_sum_last.astype(jnp.bfloat16)
    grad_dec_down = outer_sum(dec_hidden, grad_branch)
    (grad_dec_pre,) = back_dec_act(back_product(grad_branch, dec_down))
    grad_dec_pre_low = grad_dec_pre.astype(jnp.bfloat16)
    grad_dec_up = outer_sum(second_low, grad_dec_pre_low)
    grad_second = grad_sum_last + back_product(grad_dec_pre_low, dec_up)
    grad_sum_cross, grad_gain_cross, grad_bias_cross = back_second(grad_second)
    grad_cross_branch = grad_sum_cross.astype(jnp.bfloat16)
    grad_cross_out = outer_sum(attn_cross, grad_cross_branch)
    grad_attn_cross = back_product(grad_cross_branch, cross_out).astype(jnp.bfloat16)
    grad_q_cross, grad_k_cross, grad_v_cross = attend_back_rows(
        to_rows(query_cross),
        to_rows(keys_cross),
        to_rows(values_cross),
        to_rows(grad_attn_cross),
        cross_highest,
        cross_totals,
        tgt_segment,
        src_segment,
        False,
    )
    grad_q_cross = to_tokens(grad_q_cross)
    grad_k_cross = to_tokens(grad_k_cross)
    grad_v_cross = to_tokens(grad_v_cross)
    grad_cross_query = outer_sum(first_low, grad_q_cross)
    grad_cross_key = outer_sum(encoded_low, grad_k_cross)
    grad_cross_value = outer_sum(encoded_low, grad_v_cross)
    grad_first = grad_sum_cross + back_product(grad_q_cross, cross_query)
    grad_encoded = back_product(grad_k_cross, cross_key) + back_product(grad_v_cross, cross_value)
    grad_sum_self, grad_gain_self, grad_bias_self = back_first(grad_first)
    grad_self_branch = grad_sum_self.astype(jnp.bfloat16)
    grad_self_out = outer_sum(dec_attn, grad_self_branch)
    grad_dec_attn = back_product(grad_self_branch, self_out).astype(jnp.bfloat16)
    grad_q_self, grad_k_self, grad_v_self = attend_back_rows(
        to_rows(dec_query),
        to_rows(dec_keys),
        to_rows(dec_values),
        to_rows(grad_dec_attn),
        dec_highest,
        dec_totals,
        tgt_segment,
        tgt_segment,
        True,
    )
    grad_q_self = to_tokens(grad_q_self)
    grad_k_self = to_tokens(grad_k_self)
    grad_v_self = to_tokens(grad_v_self)
    grad_self_query = outer_sum(tgt_tokens, grad_q_self)
    grad_self_key = outer_sum(tgt_tokens, grad_k_self)
    grad_self_value = outer_sum(tgt_tokens, grad_v_self)
    tgt_grad = (
        grad_sum_last
        + grad_sum_self
        + back_product(grad_q_self, self_query)
        + back_product(grad_k_self, self_key)
        + back_product(grad_v_self, self_value)
    )
    dec_terms = jnp.concatenate(
        [
            piece.reshape(-1)
            for piece in (
                grad_self_query,
                grad_self_key,
                grad_self_value,
                grad_self_out,
                grad_cross_query,
                grad_cross_key,
                grad_cross_value,
                grad_cross_out,
                grad_dec_up,
                grad_dec_down,
                grad_gain_self,
                grad_bias_self,
                grad_gain_cross,
                grad_bias_cross,
                grad_gain_last,
                grad_bias_last,
            )
        ]
    )
    dec_grad = lax.psum_scatter(dec_terms, "fsdp", scatter_dimension=0, tiled=True)
    enc_flat = lax.all_gather(enc_weights, "fsdp", axis=0, tiled=True)
    w_query, w_key, w_value, w_out, w_up, w_down, gain_attn, bias_attn, gain_ffn, bias_ffn = unpack(
        enc_flat, encoder_layout()
    )
    grad_sum_ffn, grad_gain_ffn, grad_bias_ffn = back_encoded(grad_encoded)
    grad_ffn_branch = grad_sum_ffn.astype(jnp.bfloat16)
    grad_w_down = outer_sum(enc_hidden, grad_ffn_branch)
    (grad_enc_pre,) = back_enc_act(back_product(grad_ffn_branch, w_down))
    grad_enc_pre_low = grad_enc_pre.astype(jnp.bfloat16)
    grad_w_up = outer_sum(enc_mid_low, grad_enc_pre_low)
    grad_mid = grad_sum_ffn + back_product(grad_enc_pre_low, w_up)
    grad_sum_attn, grad_gain_attn, grad_bias_attn = back_mid(grad_mid)
    grad_attn_branch = grad_sum_attn.astype(jnp.bfloat16)
    grad_w_out = outer_sum(enc_attn, grad_attn_branch)
    grad_enc_attn = back_product(grad_attn_branch, w_out).astype(jnp.bfloat16)
    grad_q_enc, grad_k_enc, grad_v_enc = attend_back_rows(
        to_rows(enc_query),
        to_rows(enc_keys),
        to_rows(enc_values),
        to_rows(grad_enc_attn),
        enc_highest,
        enc_totals,
        src_segment,
        src_segment,
        False,
    )
    grad_q_enc = to_tokens(grad_q_enc)
    grad_k_enc = to_tokens(grad_k_enc)
    grad_v_enc = to_tokens(grad_v_enc)
    grad_w_query = outer_sum(src_tokens, grad_q_enc)
    grad_w_key = outer_sum(src_tokens, grad_k_enc)
    grad_w_value = outer_sum(src_tokens, grad_v_enc)
    src_grad = (
        grad_sum_ffn
        + grad_sum_attn
        + back_product(grad_q_enc, w_query)
        + back_product(grad_k_enc, w_key)
        + back_product(grad_v_enc, w_value)
    )
    enc_terms = jnp.concatenate(
        [
            piece.reshape(-1)
            for piece in (
                grad_w_query,
                grad_w_key,
                grad_w_value,
                grad_w_out,
                grad_w_up,
                grad_w_down,
                grad_gain_attn,
                grad_bias_attn,
                grad_gain_ffn,
                grad_bias_ffn,
            )
        ]
    )
    enc_grad = lax.psum_scatter(enc_terms, "fsdp", scatter_dimension=0, tiled=True)
    return (final.astype(jnp.bfloat16), src_grad, tgt_grad, enc_grad, dec_grad)


def solution(mesh):
    return jax.shard_map(
        on_device,
        mesh=mesh,
        in_specs=(
            P("fsdp", None),
            P("fsdp", None),
            P("fsdp", None),
            P("fsdp", None),
            P("fsdp"),
            P("fsdp"),
            P("fsdp", None),
        ),
        out_specs=(P("fsdp", None), P("fsdp", None), P("fsdp", None), P("fsdp"), P("fsdp")),
        check_vma=False,
    )
```

profile of v0, /device:TPU:9, one launch (start us, length us, event | category | flops | bytes accessed | tf_op | source)
XLA Modules:
  0.0 1492.2 jit_solution(15113192295286663552)
XLA Ops:
  7.2 3.9 broadcast.449
  11.2 5.3 dynamic-update-slice
  16.4 3.2 broadcast.450
  19.6 4.6 dynamic-update-slice.1
  29.3 3.2 fusion.69
  32.6 248.3 %all-reduce.11.cloned.1.call-done = (bf16[4197376]{0:T(1024)(128)(2,1)}, bf16[3147776]{0:T(1024)(128)(2,1)}) async-done(((bf16[4197376]{0:T(1024)(128)(2,1)}, bf16[3147776]{0:T(1024)(128)(2,1)}), (bf16[4197376]{0:T(1024)(128)(2,1)}, bf16[3147776]{0:T(1024)(128)(2,1)})) %all-reduce.11.cloned.1.call-update) | async-done | bytes 14690320
  280.9 3.8 fusion.159
  290.4 4.5 fusion.158
  295.2 3.2 convolution_convert_fusion.10
  298.7 3.2 convolution_convert_fusion.9
  308.0 19.7 %fusion.165 = (f32[8,1024]{1,0:T(8,128)S(1)}, f32[8,1024,1024]{1,2,0:T(8,128)}) fusion(pred[1024,1024]{0,1:T(8,128)(4,1)} %get-tuple-element.262, bf16[1024,8,64]{0,2,1:T(8,128)(2,1)} %bitcast.288, bf16[1024,8,64]{0,2,1:T(8,128)(2,1)} %bitcast.290), kind=kOutput, calls=%fused_computation.281 | convolution fusion | flops 1107297280 | bytes 36732928 | tf_op jit(solution)/shard_map/while/body/eval_jaxpr/sub | solution.py:94
  327.8 12.9 fusion.84
  348.8 3.2 convolution_convert_fusion.6
  356.7 19.4 %fusion.162 = (f32[8,1024]{1,0:T(8,128)S(1)}, f32[8,1024,1024]{1,2,0:T(8,128)}) fusion(pred[1024,1024]{0,1:T(8,128)(4,1)} %get-tuple-element.264, bf16[1024,8,64]{0,2,1:T(8,128)(2,1)S(1)} %bitcast.284, bf16[1024,8,64]{0,2,1:T(8,128)(2,1)} %bitcast.286), kind=kOutput, calls=%fused_computation.278 | convolution fusion | flops 1107297280 | bytes 36732928 | tf_op jit(solution)/shard_map/while/body/eval_jaxpr/sub | solution.py:94
  376.1 12.6 fusion.90
  390.9 4.2 slice.265
  395.0 4.3 slice.267
  399.4 24.7 %multiply_convert_fusion.4 = (bf16[1024,2048]{1,0:T(8,128)(2,1)S(1)}, f32[1024,2048]{1,0:T(8,128)}, f32[1024,2048]{1,0:T(8,128)}) fusion(bf16[512,2048]{1,0:T(8,128)(2,1)} %slice.265, f32[1024,512]{0,1:T(8,128)S(1)} %get-tuple-element.268, f32[512]{0:T(512)S(1)} %copy-done.146, f32[512]{0:T(512)S(1)} %copy-done.131, f32[1024]{0:T(1024)S(1)} %fusion.121, ...), kind=kOutput, calls=%fused_computation.65 | convolution fusion | flops 2286419968 | bytes 25178112 | tf_op jit(solution)/shard_map/dot_general | solution.py:18
  424.2 5.8 fusion.164
  440.6 3.5 convolution_convert_fusion.4
  444.1 20.0 %fusion.167 = (f32[8,1024]{1,0:T(8,128)S(1)}, f32[8,1024,1024]{1,2,0:T(8,128)}) fusion(pred[1024,1024]{0,1:T(8,128)(4,1)} %get-tuple-element.263, bf16[1024,8,64]{0,2,1:T(8,128)(2,1)} %bitcast.294, bf16[1024,8,64]{0,2,1:T(8,128)(2,1)} %bitcast.292), kind=kOutput, calls=%fused_computation.283 | convolution fusion | flops 1107297280 | bytes 36732928 | tf_op jit(solution)/shard_map/while/body/eval_jaxpr/sub | solution.py:94
  464.1 12.5 fusion.96
  477.9 4.2 reshape.779
  482.1 4.3 slice.282
  486.5 23.5 %multiply_convert_fusion.3 = (bf16[1024,2048]{1,0:T(8,128)(2,1)S(1)}, f32[1024,2048]{1,0:T(8,128)S(1)}, f32[1024,2048]{1,0:T(8,128)}) fusion(bf16[512,2048]{1,0:T(8,128)(2,1)} %reshape.779, f32[1024,512]{0,1:T(8,128)S(1)} %get-tuple-element.279, f32[512]{0:T(512)S(1)} %copy-done.141, f32[512]{0:T(512)S(1)} %copy-done.127, f32[1024]{0:T(1024)S(1)} %fusion.123, ...), kind=kOutput, calls=%fused_computation.48 | convolution fusion | flops 2286419968 | bytes 25178112 | tf_op jit(solution)/shard_map/dot_general | solution.py:18
  516.4 8.2 add_convert_fusion.1
  524.7 4.5 convolution_bitcast_fusion.1
  529.2 3.7 multiply_reduce_fusion.3
  535.9 13.1 fusion.170
  549.1 14.5 fusion.99
  563.6 44.1 %fusion.117 = bf16[8,64,1024]{2,1,0:T(8,128)(2,1)} fusion(bf16[1024,8,64]{0,2,1:T(8,128)(2,1)S(1)} %bitcast.293, f32[8,1024,1024]{1,2,0:T(8,128)} %fusion.170, pred[1024,1024]{0,1:T(8,128)(4,1)S(1)} %copy-done.66, f32[8,1024,1024]{1,2,0:T(8,128)} %get-tuple-element.277, f32[8,1024]{1,0:T(8,128)S(1)} %get-tuple-element.276), kind=kOutput, calls=%fused_computation.159 | convolution fusion | flops 1141384192 | bytes 70287360 | tf_op jit(solution)/shard_map/while/body/eval_jaxpr/hqk,khd->qhd/dot_general | solution.py:117
  607.7 44.8 %fusion.114 = bf16[8,64,1024]{2,1,0:T(8,128)(2,1)} fusion(bf16[1024,8,64]{0,2,1:T(8,128)(2,1)} %bitcast.295, f32[8,1024,1024]{1,2,0:T(8,128)} %fusion.170, pred[1024,1024]{0,1:T(8,128)(4,1)} %get-tuple-element.263, f32[8,1024,1024]{1,2,0:T(8,128)} %get-tuple-element.277, f32[8,1024]{1,0:T(8,128)S(1)} %get-tuple-element.276), kind=kOutput, calls=%fused_computation.158 | convolution fusion | flops 1141384192 | bytes 70287360 | tf_op jit(solution)/shard_map/while/body/eval_jaxpr/hqk,qhd->khd/dot_general | solution.py:120
  652.6 3.1 convolution_bitcast_fusion.7
  655.7 3.8 multiply_reduce_fusion.4
  662.9 9.3 add_convert_fusion
  672.3 3.6 multiply_reduce_fusion.6
  675.9 3.2 fusion.151
  681.6 13.3 fusion.172
  694.9 43.7 %fusion.102 = bf16[8,64,1024]{2,1,0:T(8,128)(2,1)} fusion(bf16[1024,8,64]{0,2,1:T(8,128)(2,1)} %bitcast.291, f32[8,1024,1024]{1,2,0:T(8,128)} %fusion.172, pred[1024,1024]{0,1:T(8,128)(4,1)S(1)} %copy-done.65, f32[8,1024,1024]{1,2,0:T(8,128)} %get-tuple-element.273, f32[8,1024]{1,0:T(8,128)S(1)} %copy-done.164), kind=kOutput, calls=%fused_computation.154 | convolution fusion | flops 1141384192 | bytes 70287360 | tf_op jit(solution)/shard_map/while/body/eval_jaxpr/hqk,khd->qhd/dot_general | solution.py:117
  738.6 43.2 %fusion.105 = bf16[8,64,1024]{2,1,0:T(8,128)(2,1)} fusion(bf16[1024,8,64]{0,2,1:T(8,128)(2,1)S(1)} %bitcast.289, f32[8,1024,1024]{1,2,0:T(8,128)} %fusion.172, pred[1024,1024]{0,1:T(8,128)(4,1)S(1)} %copy-done.65, f32[8,1024,1024]{1,2,0:T(8,128)} %get-tuple-element.273, f32[8,1024]{1,0:T(8,128)S(1)} %copy-done.164), kind=kOutput, calls=%fused_computation.155 | convolution fusion | flops 1141384192 | bytes 70287360 | tf_op jit(solution)/shard_map/while/body/eval_jaxpr/hqk,qhd->khd/dot_general | solution.py:120
  781.8 14.9 fusion.87
  796.7 3.2 convolution_bitcast_fusion.6
  799.9 3.4 convolution_bitcast_fusion.5
  803.3 6.6 convolution_bitcast_fusion
  810.0 4.5 convolution_bitcast_fusion.2
  814.6 4.6 convolution_bitcast_fusion.3
  821.7 13.3 fusion.171
  835.1 43.7 %fusion.108 = bf16[8,64,1024]{2,1,0:T(8,128)(2,1)} fusion(bf16[1024,8,64]{0,2,1:T(8,128)(2,1)} %bitcast.287, f32[8,1024,1024]{1,2,0:T(8,128)} %fusion.171, pred[1024,1024]{0,1:T(8,128)(4,1)S(1)} %copy-done.64, f32[8,1024,1024]{1,2,0:T(8,128)} %get-tuple-element.266, f32[8,1024]{1,0:T(8,128)S(1)} %copy-done.162), kind=kOutput, calls=%fused_computation.156 | convolution fusion | flops 1141384192 | bytes 70287360 | tf_op jit(solution)/shard_map/while/body/eval_jaxpr/hqk,khd->qhd/dot_general | solution.py:117
  878.8 43.1 %fusion.111 = bf16[8,64,1024]{2,1,0:T(8,128)(2,1)} fusion(bf16[1024,8,64]{0,2,1:T(8,128)(2,1)S(1)} %bitcast.285, f32[8,1024,1024]{1,2,0:T(8,128)} %fusion.171, pred[1024,1024]{0,1:T(8,128)(4,1)S(1)} %copy-done.64, f32[8,1024,1024]{1,2,0:T(8,128)} %get-tuple-element.266, f32[8,1024]{1,0:T(8,128)S(1)} %copy-done.162), kind=kOutput, calls=%fused_computation.157 | convolution fusion | flops 1141384192 | bytes 70287360 | tf_op jit(solution)/shard_map/while/body/eval_jaxpr/hqk,qhd->khd/dot_general | solution.py:120
  921.9 14.5 fusion.93
  936.5 5.4 copy.183
  948.3 3.3 convolution_bitcast_fusion.10
  954.4 3.3 convolution_bitcast_fusion.9
  960.6 3.2 copy.180
  966.3 3.1 copy.184
  969.4 3.1 copy.174
  972.5 2.9 copy.173
  982.6 3.2 convolution_bitcast_fusion.14
  990.8 3.3 convolution_bitcast_fusion.13
  1040.8 3.8 add_add_fusion.5
  1044.6 3.0 copy.145
  1051.7 3.8 add_add_fusion.6
  1055.6 2.9 copy.144
  1059.8 421.4 %all-reduce.9.cloned.1.call-done = (f32[3147776]{0:T(1024)}, f32[4197376]{0:T(1024)}) async-done(((f32[3147776]{0:T(1024)}, f32[4197376]{0:T(1024)}), (f32[3147776]{0:T(1024)}, f32[4197376]{0:T(1024)})) %all-reduce.9.cloned.1.call-update) | async-done | bytes 29380624
  (456 shorter events, 144.5 us)
Async XLA Ops:
  7.2 12.4 copy-start.87
  7.2 273.7 %all-reduce.11.cloned.1.call-start = ((), (), s32[]{:S(2)}) async-start(), calls=%async_computation.1 | async-start | bytes 29380608
  24.2 1456.9 %all-reduce.9.cloned.1.call-start = ((), (), s32[]{:S(2)}) async-start(), calls=%async_computation | async-start | bytes 58761216
  25.2 315.5 %copy-start.32 = (bf16[1024,512]{0,1:T(8,128)(2,1)}, bf16[1024,512]{0,1:T(8,128)(2,1)S(1)}, u32[]{:S(2)}) copy-start(bf16[1024,512]{0,1:T(8,128)(2,1)S(1)} %copy.111) | copy-start | bytes 3145732
  303.3 24.5 %copy-start.43 = (bf16[512,512]{1,0:T(8,128)(2,1)}, bf16[512,512]{1,0:T(8,128)(2,1)S(1)}, u32[]{:S(2)}) copy-start(bf16[512,512]{1,0:T(8,128)(2,1)S(1)} %slice.245) | copy-start | bytes 1572868
  305.5 22.3 %copy-start.37 = (bf16[512,1024]{1,0:T(8,128)(2,1)}, bf16[512,1024]{1,0:T(8,128)(2,1)S(1)}, u32[]{:S(2)}) copy-start(bf16[512,1024]{1,0:T(8,128)(2,1)S(1)} %convolution_convert_fusion.11) | copy-start | bytes 3145732
  327.7 12.9 copy-start.163
  327.7 13.0 copy-start.60
  341.5 14.0 copy-start.62
  341.5 34.5 %copy-start.90 = (f32[1024]{0:T(1024)}, f32[1024]{0:T(1024)S(1)}, u32[]{:S(2)}) copy-start(f32[1024]{0:T(1024)S(1)} %broadcast_multiply_fusion.4) | copy-start | bytes 12292
  343.2 32.9 %copy-start.100 = (f32[1024]{0:T(1024)}, f32[1024]{0:T(1024)S(1)}, u32[]{:S(2)}) copy-start(f32[1024]{0:T(1024)S(1)} %multiply_reduce_fusion.15) | copy-start | bytes 12292
  348.4 27.6 %copy-start.150 = (bf16[512,1024]{1,0:T(8,128)(2,1)}, bf16[512,1024]{1,0:T(8,128)(2,1)S(1)}, u32[]{:S(2)}) copy-start(bf16[512,1024]{1,0:T(8,128)(2,1)S(1)} %convolution_convert_fusion.7) | copy-start | bytes 3145732
  353.3 22.7 %copy-start.48 = (bf16[512,512]{1,0:T(8,128)(2,1)}, bf16[512,512]{1,0:T(8,128)(2,1)S(1)}, u32[]{:S(2)}) copy-start(bf16[512,512]{1,0:T(8,128)(2,1)S(1)} %slice.255) | copy-start | bytes 1572868
  355.5 20.5 %copy-start.35 = (bf16[512,1024]{1,0:T(8,128)(2,1)}, bf16[512,1024]{1,0:T(8,128)(2,1)S(1)}, u32[]{:S(2)}) copy-start(bf16[512,1024]{1,0:T(8,128)(2,1)S(1)} %convolution_convert_fusion.8) | copy-start | bytes 3145732
  376.1 12.6 copy-start.161
  376.1 12.7 copy-start.34
  376.1 12.7 copy-start.58
  388.7 10.7 copy-start.131
  388.7 10.7 copy-start.146
  389.7 34.4 %copy-start.5 = (f32[1024,512]{0,1:T(8,128)}, f32[1024,512]{0,1:T(8,128)S(1)}, u32[]{:S(2)}) copy-start(f32[1024,512]{0,1:T(8,128)S(1)} %get-tuple-element.268) | copy-start | bytes 6291460
  389.7 34.4 %copy-start.95 = (f32[1024]{0:T(1024)}, f32[1024]{0:T(1024)S(1)}, u32[]{:S(2)}) copy-start(f32[1024]{0:T(1024)S(1)} %broadcast_multiply_fusion.3) | copy-start | bytes 12292
  390.9 33.3 %copy-start.121 = (f32[1024]{0:T(1024)}, f32[1024]{0:T(1024)S(1)}, u32[]{:S(2)}) copy-start(f32[1024]{0:T(1024)S(1)} %fusion.121) | copy-start | bytes 12292
  399.4 24.7 %copy-start.54 = (bf16[2048,512]{1,0:T(8,128)(2,1)S(1)}, bf16[2048,512]{1,0:T(8,128)(2,1)}, u32[]{:S(2)}) copy-start(bf16[2048,512]{1,0:T(8,128)(2,1)} %slice.267) | copy-start | bytes 6291460
  424.1 10.3 copy-start.106
  424.2 10.3 copy-start.134
  430.0 14.2 copy-start
  430.0 10.6 copy-start.91
  430.0 10.6 copy-start.98
  430.0 10.6 copy-start.109
  430.0 10.6 copy-start.139
  464.1 12.5 copy-start.3
  464.1 12.5 copy-start.84
  486.4 23.6 %copy-start.33 = (bf16[1024,512]{0,1:T(8,128)(2,1)S(1)}, bf16[1024,512]{0,1:T(8,128)(2,1)}, u32[]{:S(2)}) copy-start(bf16[1024,512]{0,1:T(8,128)(2,1)} %copy-done.32) | copy-start | bytes 3145732
  486.5 23.6 %copy-start.57 = (bf16[2048,512]{1,0:T(8,128)(2,1)S(1)}, bf16[2048,512]{1,0:T(8,128)(2,1)}, u32[]{:S(2)}) copy-start(bf16[2048,512]{1,0:T(8,128)(2,1)} %slice.282) | copy-start | bytes 6291460
  516.4 12.7 copy-start.16
  516.4 12.7 copy-start.111
  549.1 14.5 copy-start.66
  549.1 14.5 copy-start.153
  607.7 44.8 %copy-start.4 = (f32[1024,512]{0,1:T(8,128)S(1)}, f32[1024,512]{0,1:T(8,128)}, u32[]{:S(2)}) copy-start(f32[1024,512]{0,1:T(8,128)} %copy-done.2) | copy-start | bytes 6291460
  607.7 44.8 %copy-start.92 = (f32[1024]{0:T(1024)S(1)}, f32[1024]{0:T(1024)}, u32[]{:S(2)}) copy-start(f32[1024]{0:T(1024)} %copy-done.90) | copy-start | bytes 12292
  607.7 44.8 %copy-start.99 = (f32[1024]{0:T(1024)S(1)}, f32[1024]{0:T(1024)}, u32[]{:S(2)}) copy-start(f32[1024]{0:T(1024)} %fusion.120) | copy-start | bytes 12292
  607.7 44.8 %copy-start.110 = (f32[512]{0:T(512)S(1)}, f32[512]{0:T(512)}, u32[]{:S(2)}) copy-start(f32[512]{0:T(512)} %get-tuple-element.239) | copy-start | bytes 6148
  607.7 44.8 %copy-start.140 = (f32[512]{0:T(512)S(1)}, f32[512]{0:T(512)}, u32[]{:S(2)}) copy-start(f32[512]{0:T(512)} %get-tuple-element.238) | copy-start | bytes 6148
  607.7 48.0 %copy-start.49 = (bf16[512,512]{1,0:T(8,128)(2,1)S(1)}, bf16[512,512]{1,0:T(8,128)(2,1)}, u32[]{:S(2)}) copy-start(bf16[512,512]{1,0:T(8,128)(2,1)} %slice.273) | copy-start | bytes 1572868
  607.7 48.0 %copy-start.126 = (f32[1024]{0:T(1024)S(1)}, f32[1024]{0:T(1024)}, u32[]{:S(2)}) copy-start(f32[1024]{0:T(1024)} %copy-done.125) | copy-start | bytes 12292
  681.6 13.3 copy-start.65
  681.6 13.3 copy-start.164
  694.9 43.7 %copy-start.152 = (bf16[512,1024]{1,0:T(8,128)(2,1)S(1)}, bf16[512,1024]{1,0:T(8,128)(2,1)}, u32[]{:S(2)}) copy-start(bf16[512,1024]{1,0:T(8,128)(2,1)} %convolution_convert_fusion.10) | copy-start | bytes 3145732
  781.8 21.6 %copy-start.17 = (f32[1024,512]{0,1:T(8,128)S(1)}, f32[1024,512]{0,1:T(8,128)}, u32[]{:S(2)}) copy-start(f32[1024,512]{0,1:T(8,128)} %copy-done.16) | copy-start | bytes 6291460
  781.8 21.6 %copy-start.112 = (f32[1024]{0:T(1024)S(1)}, f32[1024]{0:T(1024)}, u32[]{:S(2)}) copy-start(f32[1024]{0:T(1024)} %copy-done.111) | copy-start | bytes 12292
  799.9 10.0 copy-start.14
  799.9 10.0 copy-start.115
  799.9 10.0 copy-start.157
  821.7 13.3 copy-start.64
  821.7 13.3 copy-start.162
  835.1 43.7 %copy-start.151 = (bf16[512,1024]{1,0:T(8,128)(2,1)S(1)}, bf16[512,1024]{1,0:T(8,128)(2,1)}, u32[]{:S(2)}) copy-start(bf16[512,1024]{1,0:T(8,128)(2,1)} %copy-done.150) | copy-start | bytes 3145732
  959.3 10.1 copy-start.26
  996.6 11.1 copy-start.29
  996.6 13.2 copy-start.10
  1009.9 10.3 copy-start.136
  1009.9 11.6 copy-start.135
  1009.9 12.9 copy-start.28
  1012.3 13.7 copy-start.9
  1014.7 13.5 copy-start.8
  (103 other events, 560.9 us)
Sparse Core Ops, SparseCore 0:
  24.3 256.4 all-reduce.10
  1035.8 445.2 all-reduce.8
where the time goes:
time: 1500 us; the launch traced here: 1490 us
  waiting for transfers between devices  670 us (45%)
  matrix products  626 us (42%)
  local copies, waits for them, and re-layouts  164 us (11%)
  between operations  16.2 us (1%)
  other arithmetic  16 us (1%)
    unnamed x4, waiting for transfers between devices  670 us
    dot_general x3, matrix products, attend_backward(): jnp.einsum('hqk,khd->qhd', grad_scores, heads_keys, preferred_element_typ...  131 us
    dot_general x3, matrix products, attend_backward(): jnp.einsum('hqk,qhd->khd', grad_scores, heads_query, preferred_element_ty...  131 us
    unnamed x382, local copies, waits for them, and re-layouts  104 us
    dot_general x16, matrix products, product(): return jnp.dot(left, right, preferred_element_type=jnp.float32)  82.3 us
    sub x3, matrix products, attend_forward(): weights = jnp.exp(scores - highest)  59.1 us
    dot_general x16, matrix products, outer_sum(): lax.dot_general(left, right, (((0,), (0,)), ((), ())), preferred_element_...  51.7 us
    dot_general x16, matrix products, back_product(): lax.dot_general(left, right, (((1,), (1,)), ((), ())), preferred_element_...  49 us
  transfers between devices with their start and end apart: 2, of which 2 were waited for; matrix products, arithmetic and copies ran while one was open for 2% of the time, Pallas kernels for 0%

commit v1 on v0

v1 whole, which is shorter than its diff:
```python
import functools
import math

import jax
import jax.numpy as jnp
from jax import lax
from jax.experimental import pallas as pl
from jax.experimental.pallas import tpu as pltpu
from jax.sharding import PartitionSpec as P

D=512; TILE=128; SENTS=16; LOWEST=-1e30
NT=(((1,),(1,)),((),())); TN=(((0,),(0,)),((),()))
BF=jnp.bfloat16; F32=jnp.float32

def aligned(at):
    return at if isinstance(at,int) else pl.multiple_of(at,TILE)

def ends_of(ref):
    ends=[]; total=ref[0,0]
    ends.append(total)
    for j in range(1,SENTS):
        total=total+ref[0,j]; ends.append(total)
    return ends

def seg_iota(ends, shape, dim, base=0):
    place=lax.broadcasted_iota(jnp.int32, shape, dim)+base
    seg=jnp.zeros(shape,jnp.int32)
    for e in ends: seg=seg+(place>=e).astype(jnp.int32)
    return seg

def start_of(pos, ends_q, ends_k):
    at=jnp.int32(0)
    for eq,ek in zip(ends_q,ends_k): at=jnp.where(pos>=eq, ek, at)
    return at

def half_lanes(rows):
    return lax.broadcasted_iota(jnp.int32,(rows,TILE),1)<TILE//2

def two_heads(block, low):
    zero=jnp.zeros_like(block)
    return jnp.concatenate([jnp.where(low,block,zero),jnp.where(low,zero,block)],axis=0)

def window_start(kind, tile, blocks, ends_q, ends_k, width):
    if kind=="cross":
        first=start_of(tile*TILE, ends_q, ends_k)//TILE
    else:
        first=tile-1
    return pl.multiple_of(jnp.clip(first,0,blocks-width//TILE)*TILE,TILE)

WIDTH={"full":384,"causal":256,"cross":512}

VM=pl.BlockSpec(memory_space=pltpu.VMEM); SM=pl.BlockSpec(memory_space=pltpu.SMEM)
FF = 2048
EPSILON = 1e-05

def dot(a, b, dims=(((1,), (0,)), ((), ()))):
    return lax.dot_general(a, b, dims, preferred_element_type=F32)


def row_tile(i, size):
    return pl.ds(pl.multiple_of(i * size, size), size)


class Moves:
    def __init__(self, sems):
        self.sems, self.used, self.coming, self.going = sems, 0, [], []

    def copy(self, source, target):
        made = pltpu.make_async_copy(source, target, self.sems.at[self.used])
        self.used += 1
        made.start()
        return made

    def fetch(self, source, target, tile=None):
        self.coming.append((target, tile, self.copy(source, target if tile is None else target.at[rows_of(tile)])))

    def ready(self, *refs, tile=None):
        left = []
        for entry in self.coming:
            if any(entry[0] is ref for ref in refs) and (tile is None or entry[1] in (None, tile)):
                entry[2].wait()
            else:
                left.append(entry)
        self.coming = left

    def ready_all(self):
        for entry in self.coming:
            entry[2].wait()
        self.coming = []

    def send(self, source, target):
        self.going.append(self.copy(source, target))

    def finish(self):
        self.ready_all()
        for made in self.going:
            made.wait()


ROWS = 256


def rows_of(tile):
    return slice(tile * ROWS, (tile + 1) * ROWS)


def call(body, scalars, ins, outs, raw_outs, scratch, micros, raw_ins=(), alias=False, tiled=0):
    ins = [a if isinstance(a, tuple) else (a, 0, a.shape[0]) for a in ins]
    tall = [(count, *a.shape[1:]) for a, _, count in ins]
    tiles = tall[0][0] // ROWS if tiled else 1

    def kernel(*refs):
        refs = list(refs)

        def cut(count):
            taken = refs[:count]
            del refs[:count]
            return taken

        words, sources, raw_in, targets, raw = (
            cut(len(scalars)), cut(len(ins)), cut(len(raw_ins)), cut(len(outs)), cut(len(raw_outs))
        )
        in_refs, out_refs, own = cut(len(ins)), cut(len(outs)), cut(len(scratch))
        moves = Moves(refs[0])
        pairs = list(zip(sources, in_refs, ins))
        for tile in range(tiles):
            for source, target, _ in pairs[:tiled]:
                moves.fetch(source.at[rows_of(tile)], target, tile)
            if tile == 0:
                for source, target, (_, first, count) in pairs[tiled:]:
                    moves.fetch(source.at[pl.ds(first, count)], target)
        place = {id(ref): target for ref, target in zip(out_refs, targets)}

        def emit(*done, tile=None):
            for ref in done:
                part = (lambda r: r) if tile is None else (lambda r: r.at[rows_of(tile)])
                moves.send(part(ref), part(place[id(ref)]))

        body(moves, emit, words, in_refs, raw_in, out_refs, raw, own)
        moves.finish()

    anywhere = pl.BlockSpec(memory_space=pl.ANY)
    held = [*((s, a.dtype) for s, (a, _, _) in zip(tall, ins)), *outs]
    room = sum(math.prod(s) * jnp.dtype(d).itemsize for s, d in held)
    room += sum(math.prod(s.shape) * jnp.dtype(s.dtype).itemsize for s in scratch)
    return pl.pallas_call(
        kernel,
        out_shape=tuple(jax.ShapeDtypeStruct(s, d) for s, d in (*outs, *raw_outs)),
        in_specs=[SM] * len(scalars) + [anywhere] * (len(ins) + len(raw_ins)),
        out_specs=(anywhere,) * (len(outs) + len(raw_outs)),
        scratch_shapes=[
            *(pltpu.VMEM(s, d) for s, d in held),
            *scratch,
            pltpu.SemaphoreType.DMA((len(ins) + tiled * (tiles - 1) + len(outs) * tiles + 8,)),
        ],
        input_output_aliases={len(scalars) + len(ins): len(outs)} if alias else {},
        cost_estimate=pl.CostEstimate(flops=int(micros * 1e10), bytes_accessed=2**20, transcendentals=0),
        compiler_params=pltpu.CompilerParams(vmem_limit_bytes=max(room + 8 * 2**20, 56 * 2**20)),
    )(*scalars, *(a for a, _, _ in ins), *raw_ins)


class Plain:
    def __init__(self, base, ref):
        self.base, self.ref = base, ref

    def put(self, first, value):
        if first - self.base < self.ref.shape[0]:
            self.ref[first - self.base : first - self.base + value.shape[0], :] = value


class Laid:
    def __init__(self, rows, base, ref):
        self.rows, self.base, self.ref = rows, base, ref

    def put(self, first, value):
        last = first + value.shape[0]
        for owner in range(first // self.rows, (last - 1) // self.rows + 1):
            low, high = max(first, owner * self.rows), min(last, (owner + 1) * self.rows)
            self.store(owner, low - owner * self.rows, value[low - first : high - first])
            if low == owner * self.rows:
                self.store(owner - 1, self.rows, value[low - first : low - first + 16])

    def store(self, owner, at, value):
        if 0 <= owner - self.base < self.ref.shape[0]:
            self.ref[owner - self.base, at : at + value.shape[0], :] = value


class Owned(Laid):
    def __init__(self, rows, base, kept, sent):
        self.rows, self.base, self.kept, self.sent = rows, base, kept, sent
        self.core = lax.axis_index("fsdp") % 2

    def store(self, owner, at, value):
        pair = (owner - self.base) // 2
        if not 0 <= pair < self.kept.shape[0]:
            return

        @pl.when(self.core == owner % 2)
        def _():
            self.kept[pair, at : at + value.shape[0], :] = value

        @pl.when(self.core != owner % 2)
        def _():
            self.sent[pair, at : at + value.shape[0], :] = value


def sinks_of(plan, refs):
    if plan[0] == "plain":
        return [Plain(plan[1], refs[0])]
    if plan[0] == "laid":
        return [Laid(plan[1], plan[2], refs[0])]
    return [Owned(plan[1], base, refs[2 * i], refs[2 * i + 1]) for i, (base, _) in enumerate(plan[2])]


def sink_shapes(plan):
    if plan[0] == "plain":
        return [((plan[2], D), BF)]
    if plan[0] == "laid":
        return [((plan[3], plan[1] + 16, D), BF)]
    return [((owners // 2, plan[1] + 16, D), BF) for _, owners in plan[2] for _ in range(2)]


def send_blocks(moves, sink, whole, seal=None):
    count, base, rows = sink.ref.shape[0], sink.base, sink.rows
    moves.send(sink.ref.at[pl.ds(0, count - 1)], whole.at[pl.ds(base, count - 1)])
    moves.send(sink.ref.at[count - 1, pl.ds(0, rows)], whole.at[base + count - 1, pl.ds(0, rows)])
    if base:
        moves.send(sink.ref.at[0, pl.ds(0, 16)], whole.at[base - 1, pl.ds(rows, 16)])
    if seal is not None:
        moves.send(seal, whole.at[whole.shape[0] - 1, pl.ds(rows, 16)])


def laid_shape(plan, n):
    return ((n, plan[1] + 16, D), BF)


def put_all(sinks, first, value):
    for sink in sinks:
        sink.put(first, value)


def matrix(ref, first, rows):
    if len(ref.shape) == 2:
        return ref[first : first + rows, :]
    each = ref.shape[1] - 16
    return ref[first // each : (first + rows) // each, :each, :].reshape(rows, D)


def part_of(w, first, rows):
    each = 1 if len(w.shape) == 2 else w.shape[1] - 16
    return w, first // each, rows // each


def normed(values, gain, bias):
    center = jnp.mean(values, axis=1, keepdims=True)
    shifted = values - center
    spread = jnp.mean(shifted * shifted, axis=1, keepdims=True)
    return shifted * lax.rsqrt(spread + EPSILON) * gain + bias


def norm_back(values, gain, upstream):
    center = jnp.mean(values, axis=1, keepdims=True)
    shifted = values - center
    r = lax.rsqrt(jnp.mean(shifted * shifted, axis=1, keepdims=True) + EPSILON)
    hat = shifted * r
    scaled = upstream * gain
    inner = jnp.mean(scaled * hat, axis=1, keepdims=True)
    grad = r * (scaled - jnp.mean(scaled, axis=1, keepdims=True) - hat * inner)
    return grad, jnp.sum(upstream * hat, axis=0, keepdims=True), jnp.sum(upstream, axis=0, keepdims=True)


def gelu_both(u):
    bell = jnp.exp(u * u * -0.5)
    t = 1.0 / (1.0 + jnp.abs(u) * (0.3275911 * 0.7071067811865476))
    poly = 0.5 * 1.061405429 * t - 0.5 * 1.453152027
    for c in (1.421413741, -0.284496736, 0.254829592):
        poly = poly * t + 0.5 * c
    tail = poly * t * bell
    cdf = jnp.where(u >= 0, 1.0 - tail, tail)
    return u * cdf, cdf + u * bell * 0.3989422804014327


def interleave(size):
    out = lax.broadcasted_iota(jnp.int32, (size, size), 0)
    come = lax.broadcasted_iota(jnp.int32, (size, size), 1)
    quarter = size // 4
    return jnp.where((out % quarter) * 4 + out // quarter == come, 1.0, 0.0).astype(BF)


def ffn_fwd_body(at, moves, emit, words, ins, raw_in, outs, raw, own):
    a_ref, res_ref, w_ref, vec_ref = ins
    h_ref, gp_ref, v_ref, low_ref, wup_ref = outs
    tokens = a_ref.shape[0]
    order = interleave(256)
    moves.ready(w_ref)
    for g in range(FF // 256):
        block = dot(order, matrix(w_ref, g * 256, 256)).astype(BF)
        for k in range(4):
            wup_ref[k, g * 64 : (g + 1) * 64, :] = block[k * 64 : (k + 1) * 64]
    emit(wup_ref)
    moves.ready(vec_ref)
    gain, bias = vec_ref[at : at + 1, :], vec_ref[at + 1 : at + 2, :]
    for i in range(tokens // ROWS):
        rows = rows_of(i)
        moves.ready(a_ref, res_ref, tile=i)
        a = a_ref[rows, :]
        low = a.astype(BF)
        total = a + res_ref[rows, :].astype(F32)
        for k in range(4):
            lanes = slice(k * D, (k + 1) * D)
            act, slope = gelu_both(dot(low, wup_ref[k]))
            act = act.astype(BF)
            h_ref[rows, lanes] = act
            gp_ref[rows, lanes] = slope.astype(BF)
            total = total + dot(act, matrix(w_ref, FF + k * D, D))
        v_ref[rows, :] = total
        low_ref[rows, :] = normed(total, gain, bias).astype(BF)
        emit(low_ref, v_ref, h_ref, gp_ref, tile=i)


def ffn_fwd(at, base, a, res, w, vecs):
    t = a.shape[0]
    return call(
        functools.partial(ffn_fwd_body, at),
        (),
        (a, res, part_of(w, base, 2 * FF), vecs),
        [((t, FF), BF), ((t, FF), BF), ((t, D), F32), ((t, D), BF), ((4, D, D), BF)],
        [],
        [],
        12,
        tiled=2,
    )


def ffn_bwd_body(at, before, plan, base, seal, count, moves, emit, words, ins, raw_in, outs, raw, own):
    e_ref, v_ref, gp_ref, pre_ref, down_ref, wup_ref, vec_ref, h_ref, low_ref = ins
    sink_refs, (dgb_ref, ds_ref, dp_ref) = outs[:count], outs[count:]
    du_ref, dsl_ref, dk_ref, *more_own = own
    sink_refs = more_own or sink_refs
    sinks = sinks_of(plan, sink_refs)
    tokens = v_ref.shape[0]
    moves.ready(down_ref, wup_ref, vec_ref)
    gain, gain_pre = vec_ref[at : at + 1, :], vec_ref[before : before + 1, :]

    sums = (jnp.zeros((1, D), F32),) * 4
    for i in range(tokens // ROWS):
        rows = rows_of(i)
        moves.ready(e_ref, v_ref, gp_ref, pre_ref, tile=i)
        grad, dg, db = norm_back(v_ref[rows, :], gain, e_ref[rows, :].astype(F32))
        ds_ref[rows, :] = grad
        gl = grad.astype(BF)
        dsl_ref[rows, :] = gl
        for k in range(4):
            lanes = slice(k * D, (k + 1) * D)
            du = (dot(gl, matrix(down_ref, k * D, D), NT) * gp_ref[rows, lanes].astype(F32)).astype(BF)
            du_ref[rows, lanes] = du
            grad = grad + dot(du, wup_ref[k], NT)
        grad, dg_pre, db_pre = norm_back(pre_ref[rows, :], gain_pre, grad)
        dp_ref[rows, :] = grad
        emit(dp_ref, ds_ref, tile=i)
        sums = tuple(c + d for c, d in zip(sums, (dg_pre, db_pre, dg, db)))

    vectors = jnp.concatenate([*sums, jnp.zeros((12, D), F32)], axis=0)
    dgb_ref[...] = vectors
    if seal is not None:
        put_all(sinks, seal, vectors.astype(BF))
    emit(dgb_ref)
    moves.ready(h_ref, low_ref)
    for k in range(8):
        piece = dot(h_ref[:, k * 256 : (k + 1) * 256], dsl_ref[...], TN).astype(BF)
        put_all(sinks, base + FF + k * 256, piece)
    for k in range(4):
        for half in range(2):
            lanes = slice(half * 256, (half + 1) * 256)
            dk_ref[k, lanes, :] = dot(low_ref[:, lanes], du_ref[:, k * D : (k + 1) * D], TN).astype(BF)
    order = interleave(256)
    for g in range(FF // 256):
        block = jnp.concatenate([dk_ref[k, g * 64 : (g + 1) * 64, :] for k in range(4)], axis=0)
        put_all(sinks, base + g * 256, dot(order, block, TN).astype(BF))
    if raw:
        send_blocks(moves, sinks[0], raw[0])
    else:
        emit(*sink_refs)


def ffn_bwd(at, before, plan, base, e, v, h, gp, low, pre, wup, w, vecs, seal=None):
    t = v.shape[0]
    shapes, raw = ([], [laid_shape(plan, w.shape[0])]) if plan[0] == "laid" else (sink_shapes(plan), [])
    outs = call(
        functools.partial(ffn_bwd_body, at, before, plan, base, seal, len(shapes)),
        (),
        (e, v, gp, pre, part_of(w, base + FF, FF), wup, vecs, h, low),
        [*shapes, ((16, D), F32), ((t, D), F32), ((t, D), F32)],
        raw,
        [pltpu.VMEM((t, FF), BF), pltpu.VMEM((t, D), BF), pltpu.VMEM((4, D, D), BF)]
        + [pltpu.VMEM(*s) for s in (sink_shapes(plan) if raw else [])],
        13,
        tiled=4,
    )
    if raw:
        return outs[3:], *outs[:3]
    return outs[: len(shapes)], *outs[len(shapes) :]


def attn_fwd_body(kind, at, moves, emit, words, ins, raw_in, outs, raw, own):
    lq_ref, lk_ref = words
    xq_ref, xk_ref, w_ref, vec_ref = ins if kind == "cross" else (ins[0], *ins)
    q_ref, k_ref, v_ref, o_ref, pre_ref, out_ref, low_ref = outs
    (segk_ref,) = own
    tokens = q_ref.shape[0]
    blocks, width = tokens // TILE, WIDTH[kind]
    ends_q, ends_k = ends_of(lq_ref), ends_of(lk_ref)
    segk_ref[...] = seg_iota(ends_k, (8, tokens), 1)
    low = half_lanes(TILE)
    moves.ready(w_ref)
    for i in range(tokens // ROWS):
        rows = rows_of(i)
        moves.ready(xq_ref, xk_ref, tile=i)
        xq, xk = xq_ref[rows, :].astype(BF), xk_ref[rows, :].astype(BF)
        q_ref[rows, :] = dot(xq, matrix(w_ref, 0, D)).astype(BF)
        k_ref[rows, :] = dot(xk, matrix(w_ref, D, D)).astype(BF)
        v_ref[rows, :] = dot(xk, matrix(w_ref, 2 * D, D)).astype(BF)
    emit(q_ref, k_ref, v_ref)

    def one(tile, start, width):
        rows = row_tile(tile, TILE)
        seg_q = seg_iota(ends_q, (TILE, TILE), 0, tile * TILE)
        biases = []
        for b in range(width // TILE):
            ok = seg_q == segk_ref[0:1, pl.ds(aligned(start + b * TILE), TILE)]
            if kind == "causal":
                gap = lax.broadcasted_iota(jnp.int32, (TILE, TILE), 0) - lax.broadcasted_iota(jnp.int32, (TILE, TILE), 1)
                ok = ok & (gap >= start + b * TILE - tile * TILE)
            biases.append(jnp.where(ok, 0.0, LOWEST))
        bias_q = jnp.concatenate(biases, axis=1)
        bias_q = jnp.concatenate([bias_q, bias_q], axis=0)
        outs = []
        for p in range(D // TILE):
            lanes = slice(p * TILE, (p + 1) * TILE)
            q2 = two_heads(q_ref[rows, lanes].astype(F32) * 0.125, low).astype(BF)
            s = dot(q2, k_ref[pl.ds(start, width), lanes], NT) + bias_q
            e = jnp.exp(s - jnp.max(s, axis=1, keepdims=True)).astype(BF)
            vx = jnp.concatenate([v_ref[pl.ds(start, width), lanes], jnp.ones((width, TILE), BF)], axis=1)
            o2 = dot(e, vx)
            o2 = o2[:, :TILE] / o2[:, TILE:]
            outs.append(jnp.where(low, o2[:TILE], o2[TILE:]))
        return jnp.concatenate(outs, axis=1)

    def step(tile, _):
        rows = row_tile(tile, TILE)
        start = window_start(kind, tile, blocks, ends_q, ends_k, width)
        o_ref[rows, :] = one(tile, start, width).astype(BF)
        tail = (blocks - 3) * TILE
        if kind == "cross":
            more = ends_q[-1] < (tile + 1) * TILE
        elif kind == "full":
            more = (tile == blocks - 3) & (ends_q[-1] < tail + TILE)
        else:
            more = (tile == blocks - 1) & (ends_q[-1] < tail + TILE)

        @pl.when(more)
        def _():
            o = one(tile, tail, 3 * TILE)
            if kind == "cross":
                mean = jnp.sum(v_ref[...].astype(F32), axis=0, keepdims=True) * (1.0 / tokens)
                o = jnp.where(ends_k[-1] >= tokens, jnp.broadcast_to(mean, o.shape), o)
            pad = lax.broadcasted_iota(jnp.int32, (TILE, D), 0) + tile * TILE >= ends_q[-1]
            o_ref[rows, :] = jnp.where(pad, o, o_ref[rows, :].astype(F32)).astype(BF)

        return 0

    lax.fori_loop(0, blocks, step, 0)
    emit(o_ref)
    moves.ready(vec_ref)
    gain, bias = vec_ref[at : at + 1, :], vec_ref[at + 1 : at + 2, :]

    for i in range(tokens // ROWS):
        rows = rows_of(i)
        total = xq_ref[rows, :].astype(F32) + dot(o_ref[rows, :], matrix(w_ref, 3 * D, D))
        pre_ref[rows, :] = total
        out = normed(total, gain, bias)
        out_ref[rows, :] = out
        low_ref[rows, :] = out.astype(BF)
        emit(out_ref, low_ref, pre_ref, tile=i)


def attn_fwd(kind, at, base, lq, lk, xq, xk, w, vecs):
    t = xq.shape[0]
    low, full = ((t, D), BF), ((t, D), F32)
    return call(
        functools.partial(attn_fwd_body, kind, at),
        (lq, lk),
        ((xq, xk) if kind == "cross" else (xq,)) + (part_of(w, base, 4 * D), vecs),
        [low, low, low, low, full, full, low],
        [],
        [pltpu.VMEM((8, t), jnp.int32)],
        12,
        tiled=2 if kind == "cross" else 1,
    )


def attn_bwd_body(kind, before, plan, base, seal, count, moves, emit, words, ins, raw_in, outs, raw, own):
    cross = kind == "cross"
    lq_ref, lk_ref = words
    if cross:
        ds_ref, w_ref, q_ref, k_ref, v_ref, vec_ref, more_ref, xq_ref, xk_ref, o_ref, dgb_in_ref = ins
        sink_refs, (dgb_ref, dx_ref, dxk_ref) = outs[:count], outs[count:]
    else:
        ds_ref, w_ref, q_ref, k_ref, v_ref, vec_ref, more_ref, xq_ref, o_ref, dgb_in_ref = ins
        xk_ref, dxk_ref = xq_ref, None
        sink_refs, (dx_ref,) = outs[:count], outs[count:]
    segq_ref, segk_ref, dk_acc, dv_acc, dsl_ref, g_ref, dq_ref, dk_ref, dv_ref, *more_own = own
    seal_ref = None
    if raw:
        *sink_refs, seal_ref = more_own
    sinks = sinks_of(plan, sink_refs)
    if not raw:
        for source, target in zip(raw_in, sink_refs):
            pairs = source.shape[0]
            moves.fetch(source, target.at[pl.ds(target.shape[0] - pairs, pairs)])
    tokens = q_ref.shape[0]
    blocks, width = tokens // TILE, WIDTH[kind]
    ends_q, ends_k = ends_of(lq_ref), ends_of(lk_ref)
    segq_ref[...] = seg_iota(ends_q, (8, tokens), 1)
    segk_ref[...] = seg_iota(ends_k, (tokens, TILE), 0)
    dk_acc[...] = jnp.zeros_like(dk_acc)
    dv_acc[...] = jnp.zeros_like(dv_acc)
    low = half_lanes(TILE)
    moves.ready(w_ref)
    for i in range(tokens // ROWS):
        rows = rows_of(i)
        moves.ready(ds_ref, tile=i)
        gl = ds_ref[rows, :].astype(BF)
        dsl_ref[rows, :] = gl
        g_ref[rows, :] = dot(gl, matrix(w_ref, 3 * D, D), NT).astype(BF)
    moves.ready(q_ref, k_ref, v_ref)

    def step(tile, _):
        rows = row_tile(tile, TILE)
        start = window_start(kind, tile, blocks, ends_q, ends_k, width)
        win = pl.ds(start, width)
        ok = segk_ref[win, :] == segq_ref[0:1, rows]
        if kind == "causal":
            gap = lax.broadcasted_iota(jnp.int32, (width, TILE), 1) - lax.broadcasted_iota(jnp.int32, (width, TILE), 0)
            ok = ok & (gap >= start - tile * TILE)
        bias = jnp.where(ok, 0.0, LOWEST)
        bias = jnp.concatenate([bias, bias], axis=1)
        for p in range(D // TILE):
            lanes = slice(p * TILE, (p + 1) * TILE)
            q2 = two_heads(q_ref[rows, lanes].astype(F32) * 0.125, low).astype(BF)
            g2 = two_heads(g_ref[rows, lanes].astype(F32), low).astype(BF)
            kp, vp = k_ref[win, lanes], v_ref[win, lanes]
            s = dot(kp, q2, NT) + bias
            e = jnp.exp(s - jnp.max(s, axis=0, keepdims=True))
            prob = e * (1.0 / jnp.sum(e, axis=0, keepdims=True))
            t = prob * dot(vp, g2, NT)
            ds = (t - prob * jnp.sum(t, axis=0, keepdims=True)).astype(BF)
            dk_acc[win, lanes] += dot(ds, q2)
            dv_acc[win, lanes] += dot(prob.astype(BF), g2)
            dq = dot(ds, kp, TN)
            dq_ref[rows, lanes] = (jnp.where(low, dq[:TILE], dq[TILE:]) * 0.125).astype(BF)
        return 0

    lax.fori_loop(0, blocks, step, 0)
    moves.ready(vec_ref, more_ref)

    sums = (jnp.zeros((1, D), F32),) * 2
    for i in range(tokens // ROWS):
        rows = rows_of(i)
        dk, dv = dk_acc[rows, :].astype(BF), dv_acc[rows, :].astype(BF)
        dk_ref[rows, :], dv_ref[rows, :] = dk, dv
        from_q = ds_ref[rows, :] + dot(dq_ref[rows, :], matrix(w_ref, 0, D), NT)
        from_k = dot(dk, matrix(w_ref, D, D), NT) + dot(dv, matrix(w_ref, 2 * D, D), NT)
        if not cross:
            dx_ref[rows, :] = more_ref[rows, :] + from_q + from_k
            emit(dx_ref, tile=i)
            continue
        dxk_ref[rows, :] = from_k
        grad, dg, db = norm_back(more_ref[rows, :], vec_ref[before : before + 1, :], from_q)
        dx_ref[rows, :] = grad
        emit(dx_ref, dxk_ref, tile=i)
        sums = sums[0] + dg, sums[1] + db
    moves.ready(dgb_in_ref)
    if cross:
        dgb_ref[...] = jnp.concatenate([*sums, dgb_in_ref[:14, :]], axis=0)
        emit(dgb_ref)
    moves.ready_all()
    for m, (left_ref, right_ref) in enumerate(((xq_ref, dq_ref), (xk_ref, dk_ref), (xk_ref, dv_ref), (o_ref, dsl_ref))):
        for half in range(2):
            piece = dot(left_ref[:, half * 256 : (half + 1) * 256], right_ref[...], TN).astype(BF)
            put_all(sinks, base + m * D + half * 256, piece)
    if not raw:
        emit(*sink_refs)
    elif cross:
        send_blocks(moves, sinks[0], raw[0])
    else:
        seal_ref[...] = dgb_in_ref[...].astype(BF)
        send_blocks(moves, sinks[0], raw[0], seal_ref)


def attn_bwd(kind, before, plan, base, lq, lk, ds, q, k, v, o, xq, xk, w, vecs, more, dgb, taken=()):
    t = xq.shape[0]
    low, full = ((t, D), BF), ((t, D), F32)
    vm = pltpu.VMEM
    shapes, raw = ([], [laid_shape(plan, w.shape[0])]) if plan[0] == "laid" else (sink_shapes(plan), [])
    scratch = [vm((8, t), jnp.int32), vm((t, TILE), jnp.int32), vm(*full), vm(*full)] + [vm(*low)] * 5
    if raw:
        scratch += [*(vm(*s) for s in sink_shapes(plan)), vm((16, D), BF)]
    outs = call(
        functools.partial(attn_bwd_body, kind, before, plan, base, None, len(shapes)),
        (lq, lk),
        (ds, part_of(w, base, 4 * D), q, k, v, vecs, more) + ((xq, xk) if kind == "cross" else (xq,)) + (o, dgb),
        [*shapes] + ([((16, D), F32), full, full] if kind == "cross" else [full]),
        raw,
        scratch,
        26,
        raw_ins=taken,
        alias=bool(raw),
        tiled=1,
    )
    if raw:
        return outs[-1:], *outs[:-1]
    return outs[: len(shapes)], *outs[len(shapes) :]


SIDES = {"z": 4, "y": 2, "x": 2, "core": 2}
STRIDE = {"z": 8, "y": 4, "x": 2, "core": 1}


def place_of(name):
    return lax.axis_index("fsdp") // STRIDE[name] % SIDES[name]


def shifted(block, name, step, n=32):
    side, stride = SIDES[name], STRIDE[name]
    pairs = []
    for device in range(n):
        at = device // stride % side
        pairs.append((device, device + ((at + step) % side - at) * stride))
    return lax.ppermute(block, "fsdp", pairs)


def spread(pieces, order):
    for name in order:
        if len(pieces) > 1:
            pieces = [(jnp.concatenate([p for p, _ in pieces]), sum((l for _, l in pieces), []))]
        held, labels = pieces[0]
        spot = "zyx".index(name)
        for step in range(1, SIDES[name]):
            moved = [tuple(v + step * (i == spot) for i, v in enumerate(label)) for label in labels]
            pieces.append((shifted(held, name, step), moved))
    both = [(p, [l + (0,) for l in labels]) for p, labels in pieces]
    both += [(shifted(p, "core", 1), [l + (1,) for l in labels]) for p, labels in pieces]
    return both


def assemble_kernel(spans, labels, counts, vectors, *refs):
    *pieces, rows_ref, vecs_ref, tails, row_sem, tail_sem = refs
    n, rows = counts
    me = lax.axis_index("fsdp")
    z, y, x, core = me // 8, me // 4 % 2, me // 2 % 2, me % 2
    for piece, (first, last), names in zip(pieces, spans, labels):
        for at, (dz, dy, dx, dc) in enumerate(names):
            owner = (((z + 4 - dz) % 4 * 2 + (y + dy) % 2) * 2 + (x + dx) % 2) * 2 + (core + dc) % 2
            whole = min(last, rows) - first
            if whole:
                pltpu.make_async_copy(
                    piece.at[at, pl.ds(0, whole)], rows_ref.at[owner, pl.ds(first, whole)], row_sem
                ).start()
            if last > rows:
                pltpu.make_async_copy(
                    piece.at[at, pl.ds(whole, last - rows)], tails.at[owner], tail_sem
                ).start()
    pltpu.make_async_copy(rows_ref, rows_ref, row_sem).wait()
    pltpu.make_async_copy(tails, tails, tail_sem).wait()
    spill = lax.broadcasted_iota(jnp.int32, (16, D), 0) < vectors
    for owner in range(1, n):
        tail = jnp.where(spill, tails[owner - 1].astype(F32), 0.0)
        rows_ref[owner, 0:16] = (rows_ref[owner, 0:16].astype(F32) + tail).astype(BF)
    vecs_ref[...] = tails[n - 1].astype(F32)


def assemble(parts, n, rows, vectors):
    pieces, spans, labels = [], [], []
    for first, last, held in parts:
        for piece, names in held:
            pieces.append(piece)
            spans.append((first, last))
            labels.append(names)
    return pl.pallas_call(
        functools.partial(assemble_kernel, spans, labels, (n, rows), vectors),
        out_shape=(jax.ShapeDtypeStruct((n, rows, D), BF), jax.ShapeDtypeStruct((16, D), F32)),
        in_specs=[pl.BlockSpec(memory_space=pl.ANY)] * len(pieces),
        out_specs=(VM, VM),
        scratch_shapes=[pltpu.VMEM((n, 16, D), BF), pltpu.SemaphoreType.DMA, pltpu.SemaphoreType.DMA],
        compiler_params=pltpu.CompilerParams(vmem_limit_bytes=16 * 2**20),
    )(*pieces)


def geometry(local, n, vectors):
    rows = (local * n // D - vectors) // n
    return rows, rows + 16


def own_rows(flat, vectors, n):
    local = flat.shape[0]
    rows, block = geometry(local, n, vectors)
    extra = vectors * D // n
    room = jnp.pad(flat, (vectors * D, block * D - local))
    return lax.dynamic_slice(room, (vectors * D - extra * lax.axis_index("fsdp"),), (block * D,)).reshape(block, D)


def gather_whole(own, vectors, n):
    block = own.shape[0]
    rows = block - 16
    full = lax.all_gather(own, "fsdp", axis=0, tiled=True).reshape(n, block, D)
    spill = jnp.arange(16)[:, None] < vectors
    tails = jnp.where(spill, full[:-1, rows:], 0)
    return full.at[1:, :16].add(tails), full[-1, rows:].astype(F32)


def gather_plain(own, vectors, n):
    full, vecs = gather_whole(own, vectors, n)
    return full[:, : own.shape[0] - 16].reshape(-1, D), vecs


def gather_parts(own, vectors, n):
    rows = own.shape[0] - 16
    full, vecs = assemble(three_ways(own), n, rows, vectors)
    return full.reshape(n * rows, D), vecs


def three_ways(own):
    edges = [0, 48, 128, own.shape[0]]
    return [(a, b, spread([(own[None, a:b], [(0, 0, 0)])], order)) for a, b, order in zip(edges, edges[1:], ("xyz", "yzx", "zxy"))]


def pick(array, at, axis):
    return lax.dynamic_index_in_dim(array, at, axis, keepdims=False)


def total_of(terms):
    return sum(t.astype(F32) for t in terms)


def halve(terms, name, axis):
    at = place_of(name)
    away = total_of([pick(t, 1 - at, axis) for t in terms]).astype(BF)
    return [pick(t, at, axis) for t in terms] + [shifted(away, name, 1)]


def reduce_plane(kept, sent, order):
    kept, come = (a.reshape(-1, 2, 2, *a.shape[1:]) for a in (kept, shifted(sent, "core", 1)))
    terms = [kept, come]
    if order == "both":
        half = kept.shape[-2] // 32 * 16
        one = halve(halve([t[..., :half, :] for t in terms], "x", 2), "y", 1)
        two = halve(halve([t[..., half:, :] for t in terms], "y", 1), "x", 1)
        return [jnp.concatenate([a, b], axis=1) for a, b in zip(one, two)]
    if order == "xy":
        return halve(halve(terms, "x", 2), "y", 1)
    return halve(halve(terms, "y", 1), "x", 1)


def reduce_line(planes, base):
    count = planes[0].shape[0]
    z = place_of("z")
    sums = total_of(planes).astype(BF)
    pieces = []
    for step in (1, 2, 3):
        pairs = []
        for device in range(32):
            goal = (device // 8 + step) % 4
            if base <= goal < base + count:
                pairs.append((device, goal * 8 + device % 8))
        away = pick(sums, jnp.clip((z + step) % 4 - base, 0, count - 1), 0)
        pieces.append(lax.ppermute(away, "fsdp", pairs))
    return total_of([pick(t, jnp.clip(z - base, 0, count - 1), 0) for t in planes] + pieces)


def own_part(own, vectors, local, n):
    return lax.dynamic_slice(own.reshape(-1), (vectors * D // n * lax.axis_index("fsdp"),), (local,))


def scatter_plain(matrices, vectors_sum, n):
    rows = matrices.shape[0] // n
    blocks = matrices.reshape(n, rows, D)
    tails = jnp.concatenate([blocks[1:, :16], vectors_sum[None].astype(BF)], axis=0)
    terms = jnp.concatenate([blocks, tails], axis=1).reshape(-1, D)
    return lax.psum_scatter(terms, "fsdp", scatter_dimension=0, tiled=True).astype(F32)


def on_device(src, tgt, ls, lt, enc_weights, dec_weights, cotangent, n):
    split = n == 32
    e_own, d_own = own_rows(enc_weights, 4, n), own_rows(dec_weights, 6, n)
    e_own, d_own = lax.optimization_barrier((e_own, d_own))
    e_all, ev = (gather_parts if split else gather_plain)(e_own, 4, n)
    d_all, dv = (gather_whole if split else gather_plain)(d_own, 6, n)
    q1, k1, v1, o1, pre1, ax, axl = attn_fwd("full", 0, 0, ls, ls, src, src, e_all, ev)
    hx, gpx, sum2, enc, wup_e = ffn_fwd(2, FF, ax, src, e_all, ev)
    q3, k3, v3, o3, pre3, h1, h1l = attn_fwd("causal", 0, 0, lt, lt, tgt, tgt, d_all, dv)
    q4, k4, v4, o4, pre4, h2, h2l = attn_fwd("cross", 2, FF, lt, ls, h1, enc, d_all, dv)
    hy, gpy, sum5, final, wup_d = ffn_fwd(4, 2 * FF, h2, tgt, d_all, dv)
    if split:
        d_plan = [("laid", 256, 16, 16), ("laid", 256, 8, 8), ("laid", 256, 0, 8)]
        e_plan = [("owned", 192, ((16, 16), (10, 6))), ("owned", 192, ((0, 16),))]
        seal = 3 * FF
    else:
        d_plan = [("plain", 2 * FF, 2 * FF), ("plain", FF, FF), ("plain", 0, FF)]
        e_plan = [("plain", FF, 2 * FF), ("plain", 0, FF)]
        seal = None
    g, dgb, ds5, ds4 = ffn_bwd(4, 2, d_plan[0], 2 * FF, cotangent, sum5, hy, gpy, h2l, pre4, wup_d, d_all, dv)
    g3 = g
    g, dgb, ds3, denc = attn_bwd(
        "cross", 0, d_plan[1], FF, lt, ls, ds4, q4, k4, v4, o4, h1l, enc, d_all, dv, pre3, dgb, g3 if split else ()
    )
    g2 = g
    g, tgt_grad = attn_bwd(
        "causal", 0, d_plan[2], 0, lt, lt, ds3, q3, k3, v3, o3, tgt, tgt, d_all, dv, ds5, dgb, g2 if split else ()
    )
    g1 = g
    f, egb, ds2, ds1 = ffn_bwd(2, 0, e_plan[0], FF, denc, sum2, hx, gpx, axl, pre1, wup_e, e_all, ev, seal)
    if split:
        d_sum = lax.psum_scatter(g1[0].reshape(-1, D), "fsdp", scatter_dimension=0, tiled=True).astype(F32)
        high = reduce_line(reduce_plane(*f[:2], "yx"), 2)
        a, src_grad = attn_bwd(
            "full", 0, e_plan[1], 0, ls, ls, ds1, q1, k1, v1, o1, src, src, e_all, ev, ds2, egb, f[2:]
        )
        low = reduce_line(reduce_plane(*a, "both"), 0)
        e_sum = jnp.where(place_of("z") >= 2, high, low)
    else:
        a, src_grad = attn_bwd("full", 0, e_plan[1], 0, ls, ls, ds1, q1, k1, v1, o1, src, src, e_all, ev, ds2, egb)
        vecs = lax.psum(jnp.concatenate([egb, dgb]), "fsdp")
        d_sum = scatter_plain(jnp.concatenate([g1[0], g2[0], g3[0]]), vecs[16:], n)
        e_sum = scatter_plain(jnp.concatenate([a[0], f[0]]), vecs[:16], n)
    enc_grad = own_part(e_sum, 4, enc_weights.shape[0], n)
    dec_grad = own_part(d_sum, 6, dec_weights.shape[0], n)
    return final, src_grad, tgt_grad, enc_grad, dec_grad


def solution(mesh):
    n = mesh.shape["fsdp"]
    return jax.shard_map(
        functools.partial(on_device, n=n),
        mesh=mesh,
        in_specs=(P("fsdp", None),) * 4 + (P("fsdp"),) * 2 + (P("fsdp", None),),
        out_specs=(P("fsdp", None),) * 3 + (P("fsdp"),) * 2,
        check_vma=False,
    )
```

time: 1500 us -> 475 us (0.32)
  matrix products: 626 us -> 0 us
  waiting for transfers between devices: 670 us -> 142 us
  Pallas kernels: 0 us -> 225 us
  local copies, waits for them, and re-layouts: 164 us -> 24.3 us
  starting transfers between devices: 0.08 us -> 52.5 us
    unnamed x4 -> x2, waiting for transfers between devices: 670 us -> 0.03 us
    dot_general x63 -> x0, matrix products: 567 us -> none  [the longest x3 131 us: attend_backward(): jnp.einsum('hqk,khd->qhd', grad_scores, heads_keys, preferred_element_typ...]
    pallas_call x0 -> x11, Pallas kernels: none -> 225 us  [the longest x10 216 us: call(): pl.pallas_call(kernel, out_shape=tuple((jax.ShapeDtypeStruct(s, d) for s,...]
    ppermute x0 -> x37, waiting for transfers between devices: none -> 114 us  [the longest x31 97.2 us: shifted(): return lax.ppermute(block, 'fsdp', pairs)]
    unnamed x382 -> x60, local copies, waits for them, and re-layouts: 104 us -> 12.3 us
    sub x3 -> x0, matrix products: 59.1 us -> none  [attend_forward(): weights = jnp.exp(scores - highest)]
    ppermute x0 -> x37, starting transfers between devices: none -> 52.4 us  [the longest x31 40.9 us: shifted(): return lax.ppermute(block, 'fsdp', pairs)]
    slice x19 -> x4, local copies, waits for them, and re-layouts: 40.8 us -> 3.82 us  [the longest x2 2.39 us: reduce_plane(): one = halve(halve([t[..., :half, :] for t in terms], 'x', 2), 'y', 1)]
  transfers between devices with their start and end apart: 2 -> 39, of which waited for: 2 -> 19; matrix products, arithmetic and copies ran while one was open for 2% -> 2% of each run, Pallas kernels for 0% -> 21%
where the time goes in v1:
time: 475 us; the launch traced here: 467 us
  Pallas kernels  225 us (47%)
  waiting for transfers between devices  142 us (30%)
  starting transfers between devices  52.5 us (11%)
  local copies, waits for them, and re-layouts  24.3 us (5%)
  between operations  15 us (3%)
  other arithmetic  7.78 us (2%)
    pallas_call x10, Pallas kernels, call(): pl.pallas_call(kernel, out_shape=tuple((jax.ShapeDtypeStruct(s, d) for s,...  216 us
    ppermute x31, waiting for transfers between devices, shifted(): return lax.ppermute(block, 'fsdp', pairs)  97.2 us
    ppermute x31, starting transfers between devices, shifted(): return lax.ppermute(block, 'fsdp', pairs)  40.9 us
    all_gather x1, waiting for transfers between devices, gather_whole(): full = lax.all_gather(own, 'fsdp', axis=0, tiled=True).reshape(n, block, D)  28.5 us
    ppermute x6, waiting for transfers between devices, reduce_line(): pieces.append(lax.ppermute(away, 'fsdp', pairs))  16.7 us
    unnamed x60, local copies, waits for them, and re-layouts  12.3 us
    ppermute x6, starting transfers between devices, reduce_line(): pieces.append(lax.ppermute(away, 'fsdp', pairs))  11.5 us
  transfers between devices with their start and end apart: 39, of which 19 were waited for; matrix products, arithmetic and copies ran while one was open for 2% of the time, Pallas kernels for 21%

profile of v1, /device:TPU:9, one launch (start us, length us, event | category | flops | bytes accessed | tf_op | source)
XLA Modules:
  0.0 466.8 jit_solution(6660194903227919687)
XLA Ops:
  7.2 1.2 pad_dynamic-slice_fusion.7
  8.5 1.2 pad_dynamic-slice_fusion.6
  9.7 0.9 reshape.167
  10.6 1.3 collective-permute-start.16
  12.0 1.1 collective-permute-start.17
  13.1 1.4 collective-permute-start.18
  14.5 1.2 collective-permute-start
  15.7 1.2 collective-permute-start.9
  16.9 2.3 collective-permute-done.9
  19.4 3.1 collective-permute-start.11
  23.5 9.8 %collective-permute-done.11 = bf16[2,80,512]{2,1,0:T(8,128)(2,1)S(1)} collective-permute-done((bf16[2,80,512]{2,1,0:T(8,128)(2,1)S(1)}, bf16[2,80,512]{2,1,0:T(8,128)(2,1)S(1)}, u32[]{:S(2)}, u32[]{:S(2)}) %collective-permute-start.11) | collective-permute-done | bytes 163872 | tf_op jit(solution)/shard_map/ppermute | solution.py:640
  33.3 3.3 collective-permute-done.12
  37.0 1.3 collective-permute-start.20
  38.6 15.4 %collective-permute-done.1 = bf16[2,48,512]{2,1,0:T(8,128)(2,1)S(1)} collective-permute-done((bf16[2,48,512]{2,1,0:T(8,128)(2,1)S(1)}, bf16[2,48,512]{2,1,0:T(8,128)(2,1)S(1)}, u32[]{:S(2)}, u32[]{:S(2)}) %collective-permute-start.1) | collective-permute-done | bytes 98336 | tf_op jit(solution)/shard_map/ppermute | solution.py:640
  54.3 1.4 collective-permute-start.4
  55.6 3.1 collective-permute-done.2.refs_1_
  58.7 11.1 %collective-permute-start.5 = (bf16[4,48,512]{2,1,0:T(8,128)(2,1)S(1)}, bf16[4,48,512]{2,1,0:T(8,128)(2,1)S(1)}, u32[]{:S(2)}, u32[]{:S(2)}) collective-permute-start(bf16[4,48,512]{2,1,0:T(8,128)(2,1)S(1)} %pad_maximum_fusion.4.refs_0_), channel_id=1, source_target_pairs={{0,1},{1,0},{2,3},{3,2},{4,5},{5,4},{6,7},{7,6},{8,9},{9,8},{10,11... | collective-permute-start | bytes 589832 | tf_op jit(solution)/shard_map/ppermute | solution.py:640
  69.8 2.1 collective-permute-start.14
  75.1 1.3 collective-permute-done.6.refs_5_
  80.9 0.9 copy-done.1
  81.9 0.9 copy-done.3
  82.8 0.9 copy-done.5
  83.7 0.9 copy-done.7
  84.6 0.9 copy-done.9
  85.6 8.5 %shard_map.111 = (bf16[32,192,512]{2,1,0:T(8,128)(2,1)S(1)}, f32[16,512]{1,0:T(8,128)S(1)}) custom-call(bf16[4,48,512]{2,1,0:T(8,128)(2,1)S(1)} %pad_maximum_fusion.4.refs_0_, bf16[4,48,512]{2,1,0:T(8,128)(2,1)S(1)} %copy-done.1, bf16[4,48,512]{2,1,0:T(8,128)(2,1)S(1)} %copy-done.3, bf16[4,48,512]{2,1,0:T(8,128)(2,1)} %collective-permute-done.4.refs_3_, ...), custom_call_target="tpu_custom_call" | custom-call | tf_op jit(solution)/shard_map/pallas_call | solution.py:690
  94.1 2.6 copy-done.10
  97.3 16.8 %shard_map.112 = (bf16[1024,512]{1,0:T(8,128)(2,1)}, bf16[1024,512]{1,0:T(8,128)(2,1)}, bf16[1024,512]{1,0:T(8,128)(2,1)}, bf16[1024,512]{1,0:T(8,128)(2,1)}, f3...) custom-call(s32[1,16]{1,0:T(1,128)} %refs_1_.14, s32[1,16]{1,0:T(1,128)} %refs_1_.14, ...), custom_call_target="tpu_custom_call" | custom-call | flops 120000004096 | bytes 1048576 | tf_op jit(solution)/shard_map/pallas_call | solution.py:146
  114.1 17.4 %shard_map.113 = (bf16[1024,2048]{1,0:T(8,128)(2,1)}, bf16[1024,2048]{1,0:T(8,128)(2,1)}, f32[1024,512]{1,0:T(8,128)}, bf16[1024,512]{1,0:T(8,128)(2,1)}, bf16[4,512,512]{2,1,0:T(8,128)(2,1)}) custom-call(f32[1024,512]{1,0:T(8,128)} %get-tuple-element.77.refs_0_, bf16[1024,512]{1,0:T(8,128)(2,1)} %refs_9_.2, bf16[6144,512]{1,0:T(8,128)(2,1)} %bitcast.115, ...), custom_call_target="tpu_custom_call" | custom-call | flops 120000004096 | bytes 1048576 | tf_op jit(solution)/shard_map/pallas_call | solution.py:146
  131.5 28.5 %all-gather.2.cloned.1.call-done = bf16[8704,512]{1,0:T(8,128)(2,1)} async-done(((bf16[272,512]{1,0:T(8,128)(2,1)}), bf16[8704,512]{1,0:T(8,128)(2,1)}) %all-gather.2.cloned.1.call-update) | async-done | bytes 8912912 | tf_op jit(solution)/shard_map/all_gather | solution.py:716
  160.1 1.3 fusion.20.refs_4_.refs_5_.refs_3_.refs_6_.refs_7_
  161.4 1.3 fusion.4
  163.6 13.3 %shard_map.110 = (bf16[1024,512]{1,0:T(8,128)(2,1)}, bf16[1024,512]{1,0:T(8,128)(2,1)}, bf16[1024,512]{1,0:T(8,128)(2,1)}, bf16[1024,512]{1,0:T(8,128)(2,1)}, f3...) custom-call(s32[1,16]{1,0:T(1,128)} %refs_1_.15, s32[1,16]{1,0:T(1,128)} %refs_1_.15, ...), custom_call_target="tpu_custom_call" | custom-call | flops 120000004096 | bytes 1048576 | tf_op jit(solution)/shard_map/pallas_call | solution.py:146
  176.9 17.6 %shard_map.114 = (bf16[1024,512]{1,0:T(8,128)(2,1)}, bf16[1024,512]{1,0:T(8,128)(2,1)}, bf16[1024,512]{1,0:T(8,128)(2,1)}, bf16[1024,512]{1,0:T(8,128)(2,1)}, f3...) custom-call(s32[1,16]{1,0:T(1,128)} %refs_1_.15, s32[1,16]{1,0:T(1,128)} %refs_1_.14, ...), custom_call_target="tpu_custom_call" | custom-call | flops 120000004096 | bytes 1048576 | tf_op jit(solution)/shard_map/pallas_call | solution.py:146
  194.5 17.4 %shard_map.115 = (bf16[1024,2048]{1,0:T(8,128)(2,1)}, bf16[1024,2048]{1,0:T(8,128)(2,1)}, f32[1024,512]{1,0:T(8,128)}, bf16[1024,512]{1,0:T(8,128)(2,1)}, bf16[4,512,512]{2,1,0:T(8,128)(2,1)}) custom-call(f32[1024,512]{1,0:T(8,128)} %get-tuple-element.79.refs_0_, bf16[1024,512]{1,0:T(8,128)(2,1)} %refs_9_.3, ...), custom_call_target="tpu_custom_call" | custom-call | flops 120000004096 | bytes 1048576 | tf_op jit(solution)/shard_map/pallas_call | solution.py:146
  211.9 19.0 %shard_map.116 = (f32[16,512]{1,0:T(8,128)}, f32[1024,512]{1,0:T(8,128)}, f32[1024,512]{1,0:T(8,128)}, bf16[32,272,512]{2,1,0:T(8,128)(2,1)}) custom-call(bf16[1024,512]{1,0:T(8,128)(2,1)} %refs_0_.10, f32[1024,512]{1,0:T(8,128)} %get-tuple-element.81.refs_1_, bf16[1024,2048]{1,0:T(8,128)(2,1)} %get-tuple-element.82.refs_2_, ...), custom_call_target="tpu_custom_call" | custom-call | flops 130000003072 | bytes 1048576 | tf_op jit(solution)/shard_map/pallas_call | solution.py:146
  230.9 35.7 %shard_map.117 = (f32[16,512]{1,0:T(8,128)}, f32[1024,512]{1,0:T(8,128)}, f32[1024,512]{1,0:T(8,128)}, bf16[32,272,512]{2,1,0:T(8,128)(2,1)}) custom-call(s32[1,16]{1,0:T(1,128)} %refs_1_.15, s32[1,16]{1,0:T(1,128)} %refs_1_.14, f32[1024,512]{1,0:T(8,128)} %get-tuple-element.87.refs_2_, ...), custom_call_target="tpu_custom_call", output_to_operand_aliasing={{3}: (13, {})} | custom-call | flops 260000006144 | bytes 1048576 | tf_op jit(solution)/shard_map/pallas_call | solution.py:146
  266.6 25.1 %shard_map.120 = (f32[1024,512]{1,0:T(8,128)}, bf16[32,272,512]{2,1,0:T(8,128)(2,1)}) custom-call(s32[1,16]{1,0:T(1,128)} %refs_1_.15, s32[1,16]{1,0:T(1,128)} %refs_1_.15, f32[1024,512]{1,0:T(8,128)} %get-tuple-element.113.refs_2_, ...), custom_call_target="tpu_custom_call", output_to_operand_aliasing={{1}: (12, {})} | custom-call | flops 260000006144 | bytes 1048576 | tf_op jit(solution)/shard_map/pallas_call | solution.py:146
  291.7 22.5 %shard_map.118 = (bf16[8,208,512]{2,1,0:T(8,128)(2,1)}, bf16[8,208,512]{2,1,0:T(8,128)(2,1)}, bf16[3,208,512]{2,1,0:T(8,128)(2,1)}, bf16[3,208,512]{2,1,0:T(8,12...) custom-call(f32[1024,512]{1,0:T(8,128)} %get-tuple-element.96.refs_0_, ...), custom_call_target="tpu_custom_call" | custom-call | flops 130000003072 | bytes 1048576 | tf_op jit(solution)/shard_map/pallas_call | solution.py:146
  314.3 31.4 %shard_map.119 = (bf16[8,208,512]{2,1,0:T(8,128)(2,1)}, bf16[8,208,512]{2,1,0:T(8,128)(2,1)}, f32[1024,512]{1,0:T(8,128)}) custom-call(s32[1,16]{1,0:T(1,128)} %refs_1_.14, s32[1,16]{1,0:T(1,128)} %refs_1_.14, f32[1024,512]{1,0:T(8,128)} %get-tuple-element.103.refs_2_, bf16[6144,512]{1,0:T(8,128)(2,1)} %bitcast.117, ...), custom_call_target="tpu_custom_call" | custom-call | flops 260000006144 | bytes 1048576 | tf_op jit(solution)/shard_map/pallas_call | solution.py:146
  346.3 1.2 slice.70
  347.5 2.2 collective-permute-done.29
  349.7 1.2 slice.72
  351.0 1.4 slice.73
  352.5 3.7 collective-permute-start.30
  356.8 1.5 collective-permute-start.31
  358.4 17.7 %collective-permute-done.30 = bf16[2,2,96,512]{3,2,0,1:T(8,128)(2,1)S(1)} collective-permute-done((bf16[2,2,96,512]{3,2,0,1:T(8,128)(2,1)S(1)}, bf16[2,2,96,512]{3,2,0,1:T(8,128)(2,1)S(1)}, u32[]{:S(2)}, u32[]{:S(2)}) %collective-permute-start.30) | collective-permute-done | bytes 393248 | tf_op jit(solution)/shard_map/ppermute | solution.py:640
  376.3 22.7 %collective-permute-done.31 = bf16[2,2,112,512]{3,2,0,1:T(8,128)(2,1)S(1)} collective-permute-done((bf16[2,2,112,512]{3,2,0,1:T(8,128)(2,1)S(1)}, bf16[2,2,112,512]{3,2,0,1:T(8,128)(2,1)S(1)}, u32[]{:S(2)}, u32[]{:S(2)}) %collective-permute-start.31) | collective-permute-done | bytes 458784 | tf_op jit(solution)/shard_map/ppermute | solution.py:640
  399.1 3.4 collective-permute-start.33
  402.6 3.6 collective-permute-done.32
  406.4 3.3 collective-permute-start.25
  409.7 4.6 collective-permute-done.33
  415.3 1.9 collective-permute-start.36
  417.3 1.3 collective-permute-start.35
  418.6 1.3 collective-permute-start.34
  419.9 8.8 %collective-permute-done.25 = bf16[2,208,512]{2,1,0:T(8,128)(2,1)S(1)} collective-permute-done((bf16[2,208,512]{2,1,0:T(8,128)(2,1)S(1)}, bf16[2,208,512]{2,1,0:T(8,128)(2,1)S(1)}, u32[]{:S(2)}, u32[]{:S(2)}) %collective-permute-start.25) | collective-permute-done | bytes 426016 | tf_op jit(solution)/shard_map/ppermute | solution.py:640
  429.8 1.4 collective-permute-start.28
  431.1 3.7 collective-permute-start.27
  435.5 2.0 collective-permute-start.26
  437.5 12.1 %collective-permute-done.27 = bf16[208,512]{1,0:T(8,128)(2,1)} collective-permute-done((bf16[208,512]{1,0:T(8,128)(2,1)}, bf16[208,512]{1,0:T(8,128)(2,1)}, u32[]{:S(2)}, u32[]{:S(2)}) %collective-permute-start.27) | collective-permute-done | bytes 213024 | tf_op jit(solution)/shard_map/ppermute | solution.py:777
  449.6 4.6 collective-permute-done.26
  454.2 2.1 fusion.12
  456.5 0.9 dynamic_slice.179
  457.4 1.0 convert_bitcast_fusion
  458.6 1.0 dynamic_slice.180
  (129 shorter events, 16.4 us)
Async XLA Ops:
  7.2 152.9 %all-gather.2.cloned.1.call-start = ((), (), s32[]{:S(2)}) async-start(), calls=%async_computation.1 | async-start | bytes 9191424 | tf_op jit(solution)/shard_map/all_gather | solution.py:716
  10.6 8.8 %collective-permute-start.16 = (bf16[1,80,512]{2,1,0:T(8,128)(2,1)S(1)}, bf16[1,80,512]{2,1,0:T(8,128)(2,1)S(1)}, u32[]{:S(2)}, u32[]{:S(2)}) collective-permute-start(bf16[1,80,512]{2,1,0:T(8,128)(2,1)S(1)} %get-tuple-element.133), channel_id=1, source_target_pairs={{0,8},{1,9},{2,10},{3,11},{4,12},{5,13},{6,14},{7,15},{8,16},{9,17... | collective-permute-start | bytes 245768 | tf_op jit(solution)/shard_map/ppermute | solution.py:640
  12.0 10.5 %collective-permute-start.17 = (bf16[1,80,512]{2,1,0:T(8,128)(2,1)S(1)}, bf16[1,80,512]{2,1,0:T(8,128)(2,1)S(1)}, u32[]{:S(2)}, u32[]{:S(2)}) collective-permute-start(bf16[1,80,512]{2,1,0:T(8,128)(2,1)S(1)} %get-tuple-element.133), channel_id=1, source_target_pairs={{0,16},{1,17},{2,18},{3,19},{4,20},{5,21},{6,22},{7,23},{8,24},{9,... | collective-permute-start | bytes 245768 | tf_op jit(solution)/shard_map/ppermute | solution.py:640
  13.1 9.4 %collective-permute-start.18 = (bf16[1,80,512]{2,1,0:T(8,128)(2,1)S(1)}, bf16[1,80,512]{2,1,0:T(8,128)(2,1)S(1)}, u32[]{:S(2)}, u32[]{:S(2)}) collective-permute-start(bf16[1,80,512]{2,1,0:T(8,128)(2,1)S(1)} %get-tuple-element.133), channel_id=1, source_target_pairs={{0,24},{1,25},{2,26},{3,27},{4,28},{5,29},{6,30},{7,31},{8,0},{9,1... | collective-permute-start | bytes 245768 | tf_op jit(solution)/shard_map/ppermute | solution.py:640
  14.5 23.9 %collective-permute-start = (bf16[1,48,512]{2,1,0:T(8,128)(2,1)S(1)}, bf16[1,48,512]{2,1,0:T(8,128)(2,1)S(1)}, u32[]{:S(2)}, u32[]{:S(2)}) collective-permute-start(bf16[1,48,512]{2,1,0:T(8,128)(2,1)S(1)} %slice_bitcast_fusion.2), channel_id=1, source_target_pairs={{0,2},{1,3},{2,0},{3,1},{4,6},{5,7},{6,4},{7,5},{8,10},{9,11},{10,... | collective-permute-start | bytes 147464 | tf_op jit(solution)/shard_map/ppermute | solution.py:640
  15.7 3.6 collective-permute-start.9
  19.3 4.2 collective-permute-start.10
  19.4 13.9 %collective-permute-start.11 = (bf16[2,80,512]{2,1,0:T(8,128)(2,1)S(1)}, bf16[2,80,512]{2,1,0:T(8,128)(2,1)S(1)}, u32[]{:S(2)}, u32[]{:S(2)}) collective-permute-start(bf16[2,80,512]{2,1,0:T(8,128)(2,1)S(1)} %pad_maximum_fusion.5), channel_id=1, source_target_pairs={{0,16},{1,17},{2,18},{3,19},{4,20},{5,21},{6,22},{7,23},{8,24},{9,... | collective-permute-start | bytes 491528 | tf_op jit(solution)/shard_map/ppermute | solution.py:640
  22.5 14.2 %collective-permute-start.12 = (bf16[2,80,512]{2,1,0:T(8,128)(2,1)S(1)}, bf16[2,80,512]{2,1,0:T(8,128)(2,1)S(1)}, u32[]{:S(2)}, u32[]{:S(2)}) collective-permute-start(bf16[2,80,512]{2,1,0:T(8,128)(2,1)S(1)} %pad_maximum_fusion.5), channel_id=1, source_target_pairs={{0,24},{1,25},{2,26},{3,27},{4,28},{5,29},{6,30},{7,31},{8,0},{9,1... | collective-permute-start | bytes 491528 | tf_op jit(solution)/shard_map/ppermute | solution.py:640
  22.6 14.4 %collective-permute-start.19 = (bf16[4,80,512]{2,1,0:T(8,128)(2,1)S(1)}, bf16[4,80,512]{2,1,0:T(8,128)(2,1)S(1)}, u32[]{:S(2)}, u32[]{:S(2)}) collective-permute-start(bf16[4,80,512]{2,1,0:T(8,128)(2,1)S(1)} %pad_maximum_fusion.3), channel_id=1, source_target_pairs={{0,2},{1,3},{2,0},{3,1},{4,6},{5,7},{6,4},{7,5},{8,10},{9,11},{10,... | collective-permute-start | bytes 983048 | tf_op jit(solution)/shard_map/ppermute | solution.py:640
  36.7 36.4 %collective-permute-start.13 = (bf16[8,80,512]{2,1,0:T(8,128)(2,1)S(1)}, bf16[8,80,512]{2,1,0:T(8,128)(2,1)S(1)}, u32[]{:S(2)}, u32[]{:S(2)}) collective-permute-start(bf16[8,80,512]{2,1,0:T(8,128)(2,1)S(1)} %constant_dynamic-update-slice_fusion.refs_8_), channel_id=1, source_target_pairs={{0,2},{1,3},{2,0},{3,1},{4,6},{5,7},{6,4},{7,5},{8,10},{9,11},{10,... | collective-permute-start | bytes 1966088 | tf_op jit(solution)/shard_map/ppermute | solution.py:640
  37.0 36.1 %collective-permute-start.20 = (bf16[8,80,512]{2,1,0:T(8,128)(2,1)S(1)}, bf16[8,80,512]{2,1,0:T(8,128)(2,1)S(1)}, u32[]{:S(2)}, u32[]{:S(2)}) collective-permute-start(bf16[8,80,512]{2,1,0:T(8,128)(2,1)S(1)} %constant_dynamic-update-slice_fusion.5.refs_12_), channel_id=1, source_target_pairs={{0,4},{1,5},{2,6},{3,7},{4,0},{5,1},{6,2},{7,3},{8,12},{9,13},{10,... | collective-permute-start | bytes 1966088 | tf_op jit(solution)/shard_map/ppermute | solution.py:640
  38.4 15.7 %collective-permute-start.1 = (bf16[2,48,512]{2,1,0:T(8,128)(2,1)S(1)}, bf16[2,48,512]{2,1,0:T(8,128)(2,1)S(1)}, u32[]{:S(2)}, u32[]{:S(2)}) collective-permute-start(bf16[2,48,512]{2,1,0:T(8,128)(2,1)S(1)} %pad_maximum_fusion.6), channel_id=1, source_target_pairs={{0,4},{1,5},{2,6},{3,7},{4,0},{5,1},{6,2},{7,3},{8,12},{9,13},{10,... | collective-permute-start | bytes 294920 | tf_op jit(solution)/shard_map/ppermute | solution.py:640
  54.1 4.6 collective-permute-start.2
  54.2 15.6 %collective-permute-start.3 = (bf16[4,48,512]{2,1,0:T(8,128)(2,1)S(1)}, bf16[4,48,512]{2,1,0:T(8,128)(2,1)S(1)}, u32[]{:S(2)}, u32[]{:S(2)}) collective-permute-start(bf16[4,48,512]{2,1,0:T(8,128)(2,1)S(1)} %pad_maximum_fusion.4.refs_0_), channel_id=1, source_target_pairs={{0,16},{1,17},{2,18},{3,19},{4,20},{5,21},{6,22},{7,23},{8,24},{9,... | collective-permute-start | bytes 589832 | tf_op jit(solution)/shard_map/ppermute | solution.py:640
  54.3 18.3 %collective-permute-start.4 = (bf16[4,48,512]{2,1,0:T(8,128)(2,1)S(1)}, bf16[4,48,512]{2,1,0:T(8,128)(2,1)}, u32[]{:S(2)}, u32[]{:S(2)}) collective-permute-start(bf16[4,48,512]{2,1,0:T(8,128)(2,1)S(1)} %pad_maximum_fusion.4.refs_0_), channel_id=1, source_target_pairs={{0,24},{1,25},{2,26},{3,27},{4,28},{5,29},{6,30},{7,31},{8,0},{9,1... | collective-permute-start | bytes 589832 | tf_op jit(solution)/shard_map/ppermute | solution.py:640
  58.7 14.9 %collective-permute-start.5 = (bf16[4,48,512]{2,1,0:T(8,128)(2,1)S(1)}, bf16[4,48,512]{2,1,0:T(8,128)(2,1)S(1)}, u32[]{:S(2)}, u32[]{:S(2)}) collective-permute-start(bf16[4,48,512]{2,1,0:T(8,128)(2,1)S(1)} %pad_maximum_fusion.4.refs_0_), channel_id=1, source_target_pairs={{0,1},{1,0},{2,3},{3,2},{4,5},{5,4},{6,7},{7,6},{8,9},{9,8},{10,11... | collective-permute-start | bytes 589832 | tf_op jit(solution)/shard_map/ppermute | solution.py:640
  69.8 11.1 %collective-permute-start.14 = (bf16[8,80,512]{2,1,0:T(8,128)(2,1)S(1)}, bf16[8,80,512]{2,1,0:T(8,128)(2,1)S(1)}, u32[]{:S(2)}, u32[]{:S(2)}) collective-permute-start(bf16[8,80,512]{2,1,0:T(8,128)(2,1)S(1)} %constant_dynamic-update-slice_fusion.refs_8_), channel_id=1, source_target_pairs={{0,1},{1,0},{2,3},{3,2},{4,5},{5,4},{6,7},{7,6},{8,9},{9,8},{10,11... | collective-permute-start | bytes 1966088 | tf_op jit(solution)/shard_map/ppermute | solution.py:640
  72.6 8.3 %collective-permute-start.21 = (bf16[8,80,512]{2,1,0:T(8,128)(2,1)S(1)}, bf16[8,80,512]{2,1,0:T(8,128)(2,1)}, u32[]{:S(2)}, u32[]{:S(2)}) collective-permute-start(bf16[8,80,512]{2,1,0:T(8,128)(2,1)S(1)} %constant_dynamic-update-slice_fusion.5.refs_12_), channel_id=1, source_target_pairs={{0,1},{1,0},{2,3},{3,2},{4,5},{5,4},{6,7},{7,6},{8,9},{9,8},{10,11... | collective-permute-start | bytes 1966088 | tf_op jit(solution)/shard_map/ppermute | solution.py:640
  73.1 7.8 %collective-permute-start.15 = (bf16[8,80,512]{2,1,0:T(8,128)(2,1)S(1)}, bf16[8,80,512]{2,1,0:T(8,128)(2,1)}, u32[]{:S(2)}, u32[]{:S(2)}) collective-permute-start(bf16[8,80,512]{2,1,0:T(8,128)(2,1)S(1)} %collective-permute-done.13.refs_9_), channel_id=1, source_target_pairs={{0,1},{1,0},{2,3},{3,2},{4,5},{5,4},{6,7},{7,6},{8,9},{9,8},{10,11... | collective-permute-start | bytes 1966088 | tf_op jit(solution)/shard_map/ppermute | solution.py:640
  73.1 7.8 %collective-permute-start.22 = (bf16[8,80,512]{2,1,0:T(8,128)(2,1)S(1)}, bf16[8,80,512]{2,1,0:T(8,128)(2,1)}, u32[]{:S(2)}, u32[]{:S(2)}) collective-permute-start(bf16[8,80,512]{2,1,0:T(8,128)(2,1)S(1)} %collective-permute-done.20.refs_13_), channel_id=1, source_target_pairs={{0,1},{1,0},{2,3},{3,2},{4,5},{5,4},{6,7},{7,6},{8,9},{9,8},{10,11... | collective-permute-start | bytes 1966088 | tf_op jit(solution)/shard_map/ppermute | solution.py:640
  73.6 0.7 copy-start.4
  74.3 2.0 collective-permute-start.6
  74.4 0.7 copy-start
  76.3 0.7 copy-start.6
  77.0 1.4 collective-permute-start.7
  77.4 0.7 copy-start.2
  78.5 0.7 copy-start.8
  79.1 1.8 collective-permute-start.8
  79.5 377.9 %reduce-scatter.2.cloned.1.call-start = ((), (), s32[]{:S(2)}) async-start(), calls=%async_computation.2 | async-start | bytes 9191424 | tf_op jit(solution)/shard_map/reduce_scatter | solution.py:824
  80.9 0.9 copy-start.1
  81.9 0.9 copy-start.3
  82.8 0.9 copy-start.5
  83.7 0.9 copy-start.7
  84.6 0.9 copy-start.9
  94.1 2.6 copy-start.10
  96.7 0.6 copy-start.11
  114.1 47.3 %copy-start.24 = (pred[16]{0:T(512)(128)(4,1)S(1)}, pred[16]{0:T(512)(128)(4,1)}, u32[]{:S(2)}) copy-start(pred[16]{0:T(512)(128)(4,1)} %iota_compare_fusion) | copy-start | bytes 52
  345.7 1.8 copy-start.19
  345.7 4.1 collective-permute-start.29
  346.0 10.1 %collective-permute-start.23 = (bf16[8,208,512]{2,1,0:T(8,128)(2,1)}, bf16[8,208,512]{2,1,0:T(8,128)(2,1)S(1)}, u32[]{:S(2)}, u32[]{:S(2)}) collective-permute-start(bf16[8,208,512]{2,1,0:T(8,128)(2,1)} %get-tuple-element.123), channel_id=1, source_target_pairs={{0,1},{1,0},{2,3},{3,2},{4,5},{5,4},{6,7},{7,6},{8,9},{9,8},{10,11... | collective-permute-start | bytes 5111816 | tf_op jit(solution)/shard_map/ppermute | solution.py:640
  350.9 5.2 %copy-start.12 = (bf16[8,208,512]{2,1,0:T(8,128)(2,1)S(1)}, bf16[8,208,512]{2,1,0:T(8,128)(2,1)}, u32[]{:S(2)}) copy-start(bf16[8,208,512]{2,1,0:T(8,128)(2,1)} %get-tuple-element.122) | copy-start | bytes 5111812
  352.5 23.6 %collective-permute-start.30 = (bf16[2,2,96,512]{3,2,0,1:T(8,128)(2,1)S(1)}, bf16[2,2,96,512]{3,2,0,1:T(8,128)(2,1)S(1)}, u32[]{:S(2)}, u32[]{:S(2)}) collective-permute-start(bf16[2,2,96,512]{3,2,0,1:T(8,128)(2,1)S(1)} %fusion.15), channel_id=1, source_target_pairs={{0,2},{1,3},{2,0},{3,1},{4,6},{5,7},{6,4},{7,5},{8,10},{9,11},{10,... | collective-permute-start | bytes 1179656 | tf_op jit(solution)/shard_map/ppermute | solution.py:640
  356.5 49.7 %collective-permute-start.24 = (bf16[2,2,208,512]{3,2,0,1:T(8,128)(2,1)S(1)}, bf16[2,2,208,512]{3,2,0,1:T(8,128)(2,1)S(1)}, u32[]{:S(2)}, u32[]{:S(2)}) collective-permute-start(bf16[2,2,208,512]{3,2,0,1:T(8,128)(2,1)S(1)} %copy.14), channel_id=1, source_target_pairs={{0,4},{1,5},{2,6},{3,7},{4,0},{5,1},{6,2},{7,3},{8,12},{9,13},{10,... | collective-permute-start | bytes 2555912 | tf_op jit(solution)/shard_map/ppermute | solution.py:640
  356.8 42.2 %collective-permute-start.31 = (bf16[2,2,112,512]{3,2,0,1:T(8,128)(2,1)S(1)}, bf16[2,2,112,512]{3,2,0,1:T(8,128)(2,1)S(1)}, u32[]{:S(2)}, u32[]{:S(2)}) collective-permute-start(bf16[2,2,112,512]{3,2,0,1:T(8,128)(2,1)S(1)} %fusion.5), channel_id=1, source_target_pairs={{0,4},{1,5},{2,6},{3,7},{4,0},{5,1},{6,2},{7,3},{8,12},{9,13},{10,... | collective-permute-start | bytes 1376264 | tf_op jit(solution)/shard_map/ppermute | solution.py:640
  358.3 56.0 %copy-start.17 = (bf16[2,96,512]{2,1,0:T(8,128)(2,1)}, bf16[2,96,512]{2,1,0:T(8,128)(2,1)S(1)}, u32[]{:S(2)}) copy-start(bf16[2,96,512]{2,1,0:T(8,128)(2,1)S(1)} %get-tuple-element.144) | copy-start | bytes 589828
  358.3 71.4 %copy-start.16 = (bf16[2,96,512]{2,1,0:T(8,128)(2,1)}, bf16[2,96,512]{2,1,0:T(8,128)(2,1)S(1)}, u32[]{:S(2)}) copy-start(bf16[2,96,512]{2,1,0:T(8,128)(2,1)S(1)} %get-tuple-element.143) | copy-start | bytes 589828
  358.4 71.4 %copy-start.13 = (bf16[2,112,512]{2,1,0:T(8,128)(2,1)}, bf16[2,112,512]{2,1,0:T(8,128)(2,1)S(1)}, u32[]{:S(2)}) copy-start(bf16[2,112,512]{2,1,0:T(8,128)(2,1)S(1)} %get-tuple-element.141) | copy-start | bytes 688132
  358.4 71.4 %copy-start.14 = (bf16[2,112,512]{2,1,0:T(8,128)(2,1)}, bf16[2,112,512]{2,1,0:T(8,128)(2,1)S(1)}, u32[]{:S(2)}) copy-start(bf16[2,112,512]{2,1,0:T(8,128)(2,1)S(1)} %get-tuple-element.142) | copy-start | bytes 688132
  376.2 30.0 %collective-permute-start.32 = (bf16[2,96,512]{2,1,0:T(8,128)(2,1)S(1)}, bf16[2,96,512]{2,1,0:T(8,128)(2,1)S(1)}, u32[]{:S(2)}, u32[]{:S(2)}) collective-permute-start(bf16[2,96,512]{2,1,0:T(8,128)(2,1)S(1)} %fusion.16), channel_id=1, source_target_pairs={{0,4},{1,5},{2,6},{3,7},{4,0},{5,1},{6,2},{7,3},{8,12},{9,13},{10,... | collective-permute-start | bytes 589832 | tf_op jit(solution)/shard_map/ppermute | solution.py:640
  376.3 38.2 %copy-start.18 = (bf16[2,96,512]{2,1,0:T(8,128)(2,1)}, bf16[2,96,512]{2,1,0:T(8,128)(2,1)S(1)}, u32[]{:S(2)}) copy-start(bf16[2,96,512]{2,1,0:T(8,128)(2,1)S(1)} %dynamic-slice_bitcast_fusion.9) | copy-start | bytes 589828
  399.1 15.1 %collective-permute-start.33 = (bf16[2,112,512]{2,1,0:T(8,128)(2,1)S(1)}, bf16[2,112,512]{2,1,0:T(8,128)(2,1)S(1)}, u32[]{:S(2)}, u32[]{:S(2)}) collective-permute-start(bf16[2,112,512]{2,1,0:T(8,128)(2,1)S(1)} %fusion.6), channel_id=1, source_target_pairs={{0,2},{1,3},{2,0},{3,1},{4,6},{5,7},{6,4},{7,5},{8,10},{9,11},{10,... | collective-permute-start | bytes 688136 | tf_op jit(solution)/shard_map/ppermute | solution.py:640
  402.5 28.6 %copy-start.15 = (bf16[2,112,512]{2,1,0:T(8,128)(2,1)}, bf16[2,112,512]{2,1,0:T(8,128)(2,1)S(1)}, u32[]{:S(2)}) copy-start(bf16[2,112,512]{2,1,0:T(8,128)(2,1)S(1)} %dynamic-slice_bitcast_fusion) | copy-start | bytes 688132
  406.2 22.4 %copy-start.21 = (bf16[2,2,208,512]{3,2,0,1:T(8,128)(2,1)}, bf16[2,2,208,512]{3,2,0,1:T(8,128)(2,1)S(1)}, u32[]{:S(2)}) copy-start(bf16[2,2,208,512]{3,2,0,1:T(8,128)(2,1)S(1)} %collective-permute-done.24) | copy-start | bytes 2555908
  406.4 22.2 %collective-permute-start.25 = (bf16[2,208,512]{2,1,0:T(8,128)(2,1)S(1)}, bf16[2,208,512]{2,1,0:T(8,128)(2,1)S(1)}, u32[]{:S(2)}, u32[]{:S(2)}) collective-permute-start(bf16[2,208,512]{2,1,0:T(8,128)(2,1)S(1)} %fusion.3), channel_id=1, source_target_pairs={{0,2},{1,3},{2,0},{3,1},{4,6},{5,7},{6,4},{7,5},{8,10},{9,11},{10,... | collective-permute-start | bytes 1277960 | tf_op jit(solution)/shard_map/ppermute | solution.py:640
  414.3 14.6 %copy-start.20 = (bf16[2,208,512]{2,1,0:T(8,128)(2,1)}, bf16[2,208,512]{2,1,0:T(8,128)(2,1)S(1)}, u32[]{:S(2)}) copy-start(bf16[2,208,512]{2,1,0:T(8,128)(2,1)S(1)} %constant_dynamic-update-slice_fusion.10) | copy-start | bytes 1277956
  415.3 19.5 %collective-permute-start.36 = (bf16[208,512]{1,0:T(8,128)(2,1)S(1)}, bf16[208,512]{1,0:T(8,128)(2,1)S(1)}, u32[]{:S(2)}, u32[]{:S(2)}) collective-permute-start(bf16[208,512]{1,0:T(8,128)(2,1)S(1)} %get-tuple-element.131), channel_id=1, source_target_pairs={{8,0},{9,1},{10,2},{11,3},{12,4},{13,5},{14,6},{15,7},{16,8},{17,9... | collective-permute-start | bytes 638984 | tf_op jit(solution)/shard_map/ppermute | solution.py:777
  417.3 20.2 %collective-permute-start.35 = (bf16[208,512]{1,0:T(8,128)(2,1)}, bf16[208,512]{1,0:T(8,128)(2,1)}, u32[]{:S(2)}, u32[]{:S(2)}) collective-permute-start(bf16[208,512]{1,0:T(8,128)(2,1)} %get-tuple-element.132), channel_id=1, source_target_pairs={{16,0},{17,1},{18,2},{19,3},{20,4},{21,5},{22,6},{23,7},{24,8},{25... | collective-permute-start | bytes 638984 | tf_op jit(solution)/shard_map/ppermute | solution.py:777
  418.6 18.9 %collective-permute-start.34 = (bf16[208,512]{1,0:T(8,128)(2,1)}, bf16[208,512]{1,0:T(8,128)(2,1)}, u32[]{:S(2)}, u32[]{:S(2)}) collective-permute-start(bf16[208,512]{1,0:T(8,128)(2,1)} %get-tuple-element.130), channel_id=1, source_target_pairs={{0,8},{1,9},{2,10},{3,11},{4,12},{5,13},{6,14},{7,15},{24,0},{25,1... | collective-permute-start | bytes 638984 | tf_op jit(solution)/shard_map/ppermute | solution.py:777
  428.6 2.5 copy-start.22
  429.8 7.7 %collective-permute-start.28 = (bf16[208,512]{1,0:T(8,128)(2,1)}, bf16[208,512]{1,0:T(8,128)(2,1)}, u32[]{:S(2)}, u32[]{:S(2)}) collective-permute-start(bf16[208,512]{1,0:T(8,128)(2,1)} %get-tuple-element.128), channel_id=1, source_target_pairs={{0,24},{1,25},{2,26},{3,27},{4,28},{5,29},{6,30},{7,31},{24,16},{2... | collective-permute-start | bytes 638984 | tf_op jit(solution)/shard_map/ppermute | solution.py:777
  431.1 18.5 %collective-permute-start.27 = (bf16[208,512]{1,0:T(8,128)(2,1)}, bf16[208,512]{1,0:T(8,128)(2,1)}, u32[]{:S(2)}, u32[]{:S(2)}) collective-permute-start(bf16[208,512]{1,0:T(8,128)(2,1)} %get-tuple-element.129), channel_id=1, source_target_pairs={{0,16},{1,17},{2,18},{3,19},{4,20},{5,21},{6,22},{7,23},{8,24},{9,... | collective-permute-start | bytes 638984 | tf_op jit(solution)/shard_map/ppermute | solution.py:777
  434.9 0.7 copy-start.23
  435.5 18.7 %collective-permute-start.26 = (bf16[208,512]{1,0:T(8,128)(2,1)}, bf16[208,512]{1,0:T(8,128)(2,1)}, u32[]{:S(2)}, u32[]{:S(2)}) collective-permute-start(bf16[208,512]{1,0:T(8,128)(2,1)} %get-tuple-element.127), channel_id=1, source_target_pairs={{8,16},{9,17},{10,18},{11,19},{12,20},{13,21},{14,22},{15,23},{16,... | collective-permute-start | bytes 638984 | tf_op jit(solution)/shard_map/ppermute | solution.py:777
Sparse Core Ops, SparseCore 0:
  79.6 80.3 all-gather.1
  291.8 137.3 reduce-scatter.1

commit v2 on v1

--- a/solution.py
+++ b/solution.py
@@ -97,7 +97,7 @@
             made.wait()
 
 
-ROWS = 256
+ROWS = 512
 
 
 def rows_of(tile):
@@ -218,20 +218,6 @@
     if plan[0] == "laid":
         return [((plan[3], plan[1] + 16, D), BF)]
     return [((owners // 2, plan[1] + 16, D), BF) for _, owners in plan[2] for _ in range(2)]
-
-
-def send_blocks(moves, sink, whole, seal=None):
-    count, base, rows = sink.ref.shape[0], sink.base, sink.rows
-    moves.send(sink.ref.at[pl.ds(0, count - 1)], whole.at[pl.ds(base, count - 1)])
-    moves.send(sink.ref.at[count - 1, pl.ds(0, rows)], whole.at[base + count - 1, pl.ds(0, rows)])
-    if base:
-        moves.send(sink.ref.at[0, pl.ds(0, 16)], whole.at[base - 1, pl.ds(rows, 16)])
-    if seal is not None:
-        moves.send(seal, whole.at[whole.shape[0] - 1, pl.ds(rows, 16)])
-
-
-def laid_shape(plan, n):
-    return ((n, plan[1] + 16, D), BF)
 
 
 def put_all(sinks, first, value):
@@ -333,10 +319,9 @@
 
 
 def ffn_bwd_body(at, before, plan, base, seal, count, moves, emit, words, ins, raw_in, outs, raw, own):
-    e_ref, v_ref, gp_ref, pre_ref, down_ref, wup_ref, vec_ref, h_ref, low_ref = ins
-    sink_refs, (dgb_ref, ds_ref, dp_ref) = outs[:count], outs[count:]
-    du_ref, dsl_ref, dk_ref, *more_own = own
-    sink_refs = more_own or sink_refs
+    e_ref, v_ref, gp_ref, pre_ref, down_ref, wup_ref, vec_ref, h_ref, low_ref, *others = ins
+    sink_refs, (first_ref, dgb_ref, ds_ref, dp_ref) = outs[:count], outs[count:]
+    du_ref, dsl_ref, dk_ref = own
     sinks = sinks_of(plan, sink_refs)
     tokens = v_ref.shape[0]
     moves.ready(down_ref, wup_ref, vec_ref)
@@ -362,6 +347,9 @@
 
     vectors = jnp.concatenate([*sums, jnp.zeros((12, D), F32)], axis=0)
     dgb_ref[...] = vectors
+    if others:
+        moves.ready(*others)
+        vectors = jnp.concatenate([vectors[:4], others[0][:12, :]], axis=0)
     if seal is not None:
         put_all(sinks, seal, vectors.astype(BF))
     emit(dgb_ref)
@@ -376,36 +364,33 @@
     order = interleave(256)
     for g in range(FF // 256):
         block = jnp.concatenate([dk_ref[k, g * 64 : (g + 1) * 64, :] for k in range(4)], axis=0)
-        put_all(sinks, base + g * 256, dot(order, block, TN).astype(BF))
-    if raw:
-        send_blocks(moves, sinks[0], raw[0])
-    else:
-        emit(*sink_refs)
-
-
-def ffn_bwd(at, before, plan, base, e, v, h, gp, low, pre, wup, w, vecs, seal=None):
+        piece = dot(order, block, TN).astype(BF)
+        put_all(sinks, base + g * 256, piece)
+        if g == 0:
+            first_ref[...] = piece[:16]
+    emit(first_ref, *sink_refs)
+
+
+def ffn_bwd(at, before, plan, base, e, v, h, gp, low, pre, wup, w, vecs, *others, seal=None):
     t = v.shape[0]
-    shapes, raw = ([], [laid_shape(plan, w.shape[0])]) if plan[0] == "laid" else (sink_shapes(plan), [])
+    shapes = sink_shapes(plan)
     outs = call(
         functools.partial(ffn_bwd_body, at, before, plan, base, seal, len(shapes)),
         (),
-        (e, v, gp, pre, part_of(w, base + FF, FF), wup, vecs, h, low),
-        [*shapes, ((16, D), F32), ((t, D), F32), ((t, D), F32)],
-        raw,
-        [pltpu.VMEM((t, FF), BF), pltpu.VMEM((t, D), BF), pltpu.VMEM((4, D, D), BF)]
-        + [pltpu.VMEM(*s) for s in (sink_shapes(plan) if raw else [])],
+        (e, v, gp, pre, part_of(w, base + FF, FF), wup, vecs, h, low, *others),
+        [*shapes, ((16, D), BF), ((16, D), F32), ((t, D), F32), ((t, D), F32)],
+        [],
+        [pltpu.VMEM((t, FF), BF), pltpu.VMEM((t, D), BF), pltpu.VMEM((4, D, D), BF)],
         13,
         tiled=4,
     )
-    if raw:
-        return outs[3:], *outs[:3]
     return outs[: len(shapes)], *outs[len(shapes) :]
 
 
 def attn_fwd_body(kind, at, moves, emit, words, ins, raw_in, outs, raw, own):
     lq_ref, lk_ref = words
     xq_ref, xk_ref, w_ref, vec_ref = ins if kind == "cross" else (ins[0], *ins)
-    q_ref, k_ref, v_ref, o_ref, pre_ref, out_ref, low_ref = outs
+    q_ref, k_ref, v_ref, o_ref, pre_ref, out_ref, low_ref, lse_ref = outs
     (segk_ref,) = own
     tokens = q_ref.shape[0]
     blocks, width = tokens // TILE, WIDTH[kind]
@@ -422,7 +407,7 @@
         v_ref[rows, :] = dot(xk, matrix(w_ref, 2 * D, D)).astype(BF)
     emit(q_ref, k_ref, v_ref)
 
-    def one(tile, start, width):
+    def one(tile, start, width, with_logs):
         rows = row_tile(tile, TILE)
         seg_q = seg_iota(ends_q, (TILE, TILE), 0, tile * TILE)
         biases = []
@@ -435,21 +420,29 @@
         bias_q = jnp.concatenate(biases, axis=1)
         bias_q = jnp.concatenate([bias_q, bias_q], axis=0)
         outs = []
+        lane = lax.broadcasted_iota(jnp.int32, (TILE, TILE), 1)
+        logs = jnp.zeros((TILE, TILE), F32)
         for p in range(D // TILE):
             lanes = slice(p * TILE, (p + 1) * TILE)
             q2 = two_heads(q_ref[rows, lanes].astype(F32) * 0.125, low).astype(BF)
             s = dot(q2, k_ref[pl.ds(start, width), lanes], NT) + bias_q
-            e = jnp.exp(s - jnp.max(s, axis=1, keepdims=True)).astype(BF)
+            top = jnp.max(s, axis=1, keepdims=True)
+            e = jnp.exp(s - top).astype(BF)
             vx = jnp.concatenate([v_ref[pl.ds(start, width), lanes], jnp.ones((width, TILE), BF)], axis=1)
             o2 = dot(e, vx)
+            if with_logs:
+                log = top + jnp.log(o2[:, TILE:])
+                logs = jnp.where(lane == 2 * p, log[:TILE], jnp.where(lane == 2 * p + 1, log[TILE:], logs))
             o2 = o2[:, :TILE] / o2[:, TILE:]
             outs.append(jnp.where(low, o2[:TILE], o2[TILE:]))
+        if with_logs:
+            lse_ref[:, rows] = logs.T[:8, :]
         return jnp.concatenate(outs, axis=1)
 
     def step(tile, _):
         rows = row_tile(tile, TILE)
         start = window_start(kind, tile, blocks, ends_q, ends_k, width)
-        o_ref[rows, :] = one(tile, start, width).astype(BF)
+        o_ref[rows, :] = one(tile, start, width, True).astype(BF)
         tail = (blocks - 3) * TILE
         if kind == "cross":
             more = ends_q[-1] < (tile + 1) * TILE
@@ -460,7 +453,7 @@
 
         @pl.when(more)
         def _():
-            o = one(tile, tail, 3 * TILE)
+            o = one(tile, tail, 3 * TILE, False)
             if kind == "cross":
                 mean = jnp.sum(v_ref[...].astype(F32), axis=0, keepdims=True) * (1.0 / tokens)
                 o = jnp.where(ends_k[-1] >= tokens, jnp.broadcast_to(mean, o.shape), o)
@@ -470,7 +463,7 @@
         return 0
 
     lax.fori_loop(0, blocks, step, 0)
-    emit(o_ref)
+    emit(o_ref, lse_ref)
     moves.ready(vec_ref)
     gain, bias = vec_ref[at : at + 1, :], vec_ref[at + 1 : at + 2, :]
 
@@ -491,7 +484,7 @@
         functools.partial(attn_fwd_body, kind, at),
         (lq, lk),
         ((xq, xk) if kind == "cross" else (xq,)) + (part_of(w, base, 4 * D), vecs),
-        [low, low, low, low, full, full, low],
+        [low, low, low, low, full, full, low, ((8, t), F32)],
         [],
         [pltpu.VMEM((8, t), jnp.int32)],
         12,
@@ -503,21 +496,17 @@
     cross = kind == "cross"
     lq_ref, lk_ref = words
     if cross:
-        ds_ref, w_ref, q_ref, k_ref, v_ref, vec_ref, more_ref, xq_ref, xk_ref, o_ref, dgb_in_ref = ins
-        sink_refs, (dgb_ref, dx_ref, dxk_ref) = outs[:count], outs[count:]
+        ds_ref, o_ref, w_ref, lse_ref, q_ref, k_ref, v_ref, vec_ref, more_ref, xq_ref, xk_ref, dgb_in_ref, next_ref = ins
+        sink_refs, (first_ref, dgb_ref, dx_ref, dxk_ref) = outs[:count], outs[count:]
     else:
-        ds_ref, w_ref, q_ref, k_ref, v_ref, vec_ref, more_ref, xq_ref, o_ref, dgb_in_ref = ins
+        ds_ref, o_ref, w_ref, lse_ref, q_ref, k_ref, v_ref, vec_ref, more_ref, xq_ref, dgb_in_ref, next_ref = ins
         xk_ref, dxk_ref = xq_ref, None
-        sink_refs, (dx_ref,) = outs[:count], outs[count:]
-    segq_ref, segk_ref, dk_acc, dv_acc, dsl_ref, g_ref, dq_ref, dk_ref, dv_ref, *more_own = own
-    seal_ref = None
-    if raw:
-        *sink_refs, seal_ref = more_own
+        sink_refs, (first_ref, dx_ref) = outs[:count], outs[count:]
+    segq_ref, segk_ref, inner_ref, dk_acc, dv_acc, dsl_ref, g_ref, dq_ref, dk_ref, dv_ref = own
     sinks = sinks_of(plan, sink_refs)
-    if not raw:
-        for source, target in zip(raw_in, sink_refs):
-            pairs = source.shape[0]
-            moves.fetch(source, target.at[pl.ds(target.shape[0] - pairs, pairs)])
+    for source, target in zip(raw_in, sink_refs):
+        pairs = source.shape[0]
+        moves.fetch(source, target.at[pl.ds(target.shape[0] - pairs, pairs)])
     tokens = q_ref.shape[0]
     blocks, width = tokens // TILE, WIDTH[kind]
     ends_q, ends_k = ends_of(lq_ref), ends_of(lk_ref)
@@ -527,13 +516,20 @@
     dv_acc[...] = jnp.zeros_like(dv_acc)
     low = half_lanes(TILE)
     moves.ready(w_ref)
+    heads = lax.broadcasted_iota(jnp.int32, (16, D), 1) // (D // 8) == lax.broadcasted_iota(jnp.int32, (16, D), 0)
+    heads = jnp.where(heads, 1.0, 0.0).astype(BF)
     for i in range(tokens // ROWS):
         rows = rows_of(i)
-        moves.ready(ds_ref, tile=i)
+        moves.ready(ds_ref, o_ref, tile=i)
         gl = ds_ref[rows, :].astype(BF)
         dsl_ref[rows, :] = gl
-        g_ref[rows, :] = dot(gl, matrix(w_ref, 3 * D, D), NT).astype(BF)
-    moves.ready(q_ref, k_ref, v_ref)
+        g = dot(gl, matrix(w_ref, 3 * D, D), NT).astype(BF)
+        g_ref[rows, :] = g
+        both = g.astype(F32) * o_ref[rows, :].astype(F32)
+        coarse = both.astype(BF)
+        fine = (both - coarse.astype(F32)).astype(BF)
+        inner_ref[:, rows] = dot(heads, coarse, NT) + dot(heads, fine, NT)
+    moves.ready(q_ref, k_ref, v_ref, lse_ref)
 
     def step(tile, _):
         rows = row_tile(tile, TILE)
@@ -543,22 +539,27 @@
         if kind == "causal":
             gap = lax.broadcasted_iota(jnp.int32, (width, TILE), 1) - lax.broadcasted_iota(jnp.int32, (width, TILE), 0)
             ok = ok & (gap >= start - tile * TILE)
-        bias = jnp.where(ok, 0.0, LOWEST)
-        bias = jnp.concatenate([bias, bias], axis=1)
+        mask = jnp.where(ok, 0.0, LOWEST)
+        mask = jnp.concatenate([mask, mask], axis=1)
+        qs, gs = q_ref[rows, :], g_ref[rows, :]
+        ks, vs = k_ref[win, :], v_ref[win, :]
+        lses, inners = lse_ref[:, rows], inner_ref[:, rows]
+        dks, dvs, dqs = [], [], []
         for p in range(D // TILE):
             lanes = slice(p * TILE, (p + 1) * TILE)
-            q2 = two_heads(q_ref[rows, lanes].astype(F32) * 0.125, low).astype(BF)
-            g2 = two_heads(g_ref[rows, lanes].astype(F32), low).astype(BF)
-            kp, vp = k_ref[win, lanes], v_ref[win, lanes]
-            s = dot(kp, q2, NT) + bias
-            e = jnp.exp(s - jnp.max(s, axis=0, keepdims=True))
-            prob = e * (1.0 / jnp.sum(e, axis=0, keepdims=True))
-            t = prob * dot(vp, g2, NT)
-            ds = (t - prob * jnp.sum(t, axis=0, keepdims=True)).astype(BF)
-            dk_acc[win, lanes] += dot(ds, q2)
-            dv_acc[win, lanes] += dot(prob.astype(BF), g2)
-            dq = dot(ds, kp, TN)
-            dq_ref[rows, lanes] = (jnp.where(low, dq[:TILE], dq[TILE:]) * 0.125).astype(BF)
+            q2 = two_heads(qs[:, lanes].astype(F32) * 0.125, low).astype(BF)
+            g2 = two_heads(gs[:, lanes].astype(F32), low).astype(BF)
+            lse = jnp.concatenate([lses[2 * p : 2 * p + 1], lses[2 * p + 1 : 2 * p + 2]], axis=1)
+            inner = jnp.concatenate([inners[2 * p : 2 * p + 1], inners[2 * p + 1 : 2 * p + 2]], axis=1)
+            prob = jnp.exp(dot(ks[:, lanes], q2, NT) + mask - lse)
+            ds = (prob * (dot(vs[:, lanes], g2, NT) - inner)).astype(BF)
+            dks.append(dot(ds, q2))
+            dvs.append(dot(prob.astype(BF), g2))
+            dq = dot(ds, ks[:, lanes], TN)
+            dqs.append(jnp.where(low, dq[:TILE], dq[TILE:]) * 0.125)
+        dk_acc[win, :] += jnp.concatenate(dks, axis=1)
+        dv_acc[win, :] += jnp.concatenate(dvs, axis=1)
+        dq_ref[rows, :] = jnp.concatenate(dqs, axis=1).astype(BF)
         return 0
 
     lax.fori_loop(0, blocks, step, 0)
@@ -589,37 +590,32 @@
         for half in range(2):
             piece = dot(left_ref[:, half * 256 : (half + 1) * 256], right_ref[...], TN).astype(BF)
             put_all(sinks, base + m * D + half * 256, piece)
-    if not raw:
-        emit(*sink_refs)
-    elif cross:
-        send_blocks(moves, sinks[0], raw[0])
-    else:
-        seal_ref[...] = dgb_in_ref[...].astype(BF)
-        send_blocks(moves, sinks[0], raw[0], seal_ref)
-
-
-def attn_bwd(kind, before, plan, base, lq, lk, ds, q, k, v, o, xq, xk, w, vecs, more, dgb, taken=()):
+            if m == half == 0:
+                first_ref[...] = piece[:16]
+    if plan[0] == "owned" and (base + 4 * D) % plan[1] == 0:
+        sinks[0].store((base + 4 * D) // plan[1] - 1, plan[1], next_ref[...])
+    emit(first_ref, *sink_refs)
+
+
+def attn_bwd(kind, before, plan, base, lq, lk, ds, q, k, v, o, lse, xq, xk, w, vecs, more, dgb, following, taken=()):
     t = xq.shape[0]
     low, full = ((t, D), BF), ((t, D), F32)
     vm = pltpu.VMEM
-    shapes, raw = ([], [laid_shape(plan, w.shape[0])]) if plan[0] == "laid" else (sink_shapes(plan), [])
-    scratch = [vm((8, t), jnp.int32), vm((t, TILE), jnp.int32), vm(*full), vm(*full)] + [vm(*low)] * 5
-    if raw:
-        scratch += [*(vm(*s) for s in sink_shapes(plan)), vm((16, D), BF)]
+    shapes = sink_shapes(plan)
+    scratch = [vm((8, t), jnp.int32), vm((t, TILE), jnp.int32), vm((16, t), F32), vm(*full), vm(*full)] + [vm(*low)] * 5
     outs = call(
         functools.partial(attn_bwd_body, kind, before, plan, base, None, len(shapes)),
         (lq, lk),
-        (ds, part_of(w, base, 4 * D), q, k, v, vecs, more) + ((xq, xk) if kind == "cross" else (xq,)) + (o, dgb),
-        [*shapes] + ([((16, D), F32), full, full] if kind == "cross" else [full]),
-        raw,
+        (ds, o, part_of(w, base, 4 * D), lse, q, k, v, vecs, more)
+        + ((xq, xk) if kind == "cross" else (xq,))
+        + (dgb, following),
+        [*shapes, ((16, D), BF)] + ([((16, D), F32), full, full] if kind == "cross" else [full]),
+        [],
         scratch,
         26,
         raw_ins=taken,
-        alias=bool(raw),
-        tiled=1,
+        tiled=2,
     )
-    if raw:
-        return outs[-1:], *outs[:-1]
     return outs[: len(shapes)], *outs[len(shapes) :]
 
 
@@ -640,60 +636,78 @@
     return lax.ppermute(block, "fsdp", pairs)
 
 
-def spread(pieces, order):
-    for name in order:
-        if len(pieces) > 1:
-            pieces = [(jnp.concatenate([p for p, _ in pieces]), sum((l for _, l in pieces), []))]
-        held, labels = pieces[0]
-        spot = "zyx".index(name)
+def widen(pieces, name):
+    if len(pieces) > 1 and name != "core":
+        pieces = [(jnp.concatenate([p for p, _ in pieces]), sum((l for _, l in pieces), []))]
+    spot = list(SIDES).index(name)
+    more = []
+    for held, labels in pieces:
         for step in range(1, SIDES[name]):
             moved = [tuple(v + step * (i == spot) for i, v in enumerate(label)) for label in labels]
-            pieces.append((shifted(held, name, step), moved))
-    both = [(p, [l + (0,) for l in labels]) for p, labels in pieces]
-    both += [(shifted(p, "core", 1), [l + (1,) for l in labels]) for p, labels in pieces]
-    return both
-
-
-def assemble_kernel(spans, labels, counts, vectors, *refs):
-    *pieces, rows_ref, vecs_ref, tails, row_sem, tail_sem = refs
-    n, rows = counts
+            more.append((shifted(held, name, step), moved))
+    return pieces + more
+
+
+def after(pieces, *others):
+    held = lax.optimization_barrier((*(p for p, _ in pieces), *others))
+    return [(p, l) for p, (_, l) in zip(held, pieces)]
+
+
+def at_home(own):
+    return [(own[None], [(0, 0, 0, 0)])]
+
+
+def assemble_body(spans, labels, rows, vectors, keep, *refs):
+    *pieces, rows_ref, vecs_ref, land, tails, tails32, row_sem, tail_sem, out_sem, vec_sem = refs
+    n = land.shape[0]
     me = lax.axis_index("fsdp")
     z, y, x, core = me // 8, me // 4 % 2, me // 2 % 2, me % 2
     for piece, (first, last), names in zip(pieces, spans, labels):
         for at, (dz, dy, dx, dc) in enumerate(names):
             owner = (((z + 4 - dz) % 4 * 2 + (y + dy) % 2) * 2 + (x + dx) % 2) * 2 + (core + dc) % 2
             whole = min(last, rows) - first
-            if whole:
+            if whole > 0:
                 pltpu.make_async_copy(
-                    piece.at[at, pl.ds(0, whole)], rows_ref.at[owner, pl.ds(first, whole)], row_sem
+                    piece.at[at, pl.ds(0, whole)], land.at[owner, pl.ds(first, whole)], row_sem
                 ).start()
             if last > rows:
                 pltpu.make_async_copy(
                     piece.at[at, pl.ds(whole, last - rows)], tails.at[owner], tail_sem
                 ).start()
-    pltpu.make_async_copy(rows_ref, rows_ref, row_sem).wait()
+    pltpu.make_async_copy(land, land, row_sem).wait()
     pltpu.make_async_copy(tails, tails, tail_sem).wait()
     spill = lax.broadcasted_iota(jnp.int32, (16, D), 0) < vectors
     for owner in range(1, n):
         tail = jnp.where(spill, tails[owner - 1].astype(F32), 0.0)
-        rows_ref[owner, 0:16] = (rows_ref[owner, 0:16].astype(F32) + tail).astype(BF)
-    vecs_ref[...] = tails[n - 1].astype(F32)
-
-
-def assemble(parts, n, rows, vectors):
+        land[owner, 0:16] = (land[owner, 0:16].astype(F32) + tail).astype(BF)
+    tails32[...] = tails[n - 1].astype(F32)
+    target = rows_ref.at[:, pl.ds(0, rows)] if keep else rows_ref
+    out = pltpu.make_async_copy(land, target, out_sem)
+    vec = pltpu.make_async_copy(tails32, vecs_ref, vec_sem)
+    out.start()
+    vec.start()
+    out.wait()
+    vec.wait()
+
+
+def assemble(parts, n, rows, vectors, keep):
     pieces, spans, labels = [], [], []
     for first, last, held in parts:
         for piece, names in held:
             pieces.append(piece)
             spans.append((first, last))
             labels.append(names)
+    anywhere = pl.BlockSpec(memory_space=pl.ANY)
     return pl.pallas_call(
-        functools.partial(assemble_kernel, spans, labels, (n, rows), vectors),
-        out_shape=(jax.ShapeDtypeStruct((n, rows, D), BF), jax.ShapeDtypeStruct((16, D), F32)),
-        in_specs=[pl.BlockSpec(memory_space=pl.ANY)] * len(pieces),
-        out_specs=(VM, VM),
-        scratch_shapes=[pltpu.VMEM((n, 16, D), BF), pltpu.SemaphoreType.DMA, pltpu.SemaphoreType.DMA],
-        compiler_params=pltpu.CompilerParams(vmem_limit_bytes=16 * 2**20),
+        functools.partial(assemble_body, spans, labels, rows, vectors, keep),
+        out_shape=(jax.ShapeDtypeStruct((n, rows + 16 * keep, D), BF), jax.ShapeDtypeStruct((16, D), F32)),
+        in_specs=[anywhere] * len(pieces),
+        out_specs=(anywhere, anywhere),
+        scratch_shapes=[
+            pltpu.VMEM((n, rows, D), BF), pltpu.VMEM((n, 16, D), BF), pltpu.VMEM((16, D), F32)
+        ] + [pltpu.SemaphoreType.DMA] * 4,
+        cost_estimate=pl.CostEstimate(flops=int(8e10), bytes_accessed=2**20, transcendentals=0),
+        compiler_params=pltpu.CompilerParams(vmem_limit_bytes=56 * 2**20),
     )(*pieces)
 
 
@@ -724,17 +738,6 @@
     return full[:, : own.shape[0] - 16].reshape(-1, D), vecs
 
 
-def gather_parts(own, vectors, n):
-    rows = own.shape[0] - 16
-    full, vecs = assemble(three_ways(own), n, rows, vectors)
-    return full.reshape(n * rows, D), vecs
-
-
-def three_ways(own):
-    edges = [0, 48, 128, own.shape[0]]
-    return [(a, b, spread([(own[None, a:b], [(0, 0, 0)])], order)) for a, b, order in zip(edges, edges[1:], ("xyz", "yzx", "zxy"))]
-
-
 def pick(array, at, axis):
     return lax.dynamic_index_in_dim(array, at, axis, keepdims=False)
 
@@ -743,26 +746,36 @@
     return sum(t.astype(F32) for t in terms)
 
 
-def halve(terms, name, axis):
+def hold(value, *others):
+    return lax.optimization_barrier((value, *others))[0]
+
+
+def begin_plane(kept, sent):
+    return [a.reshape(-1, 2, 2, *a.shape[1:]) for a in (kept, shifted(sent, "core", 1))]
+
+
+def halve(terms, name, axis, aways=None):
     at = place_of(name)
     away = total_of([pick(t, 1 - at, axis) for t in terms]).astype(BF)
+    if aways is not None:
+        aways.append(away)
     return [pick(t, at, axis) for t in terms] + [shifted(away, name, 1)]
 
 
-def reduce_plane(kept, sent, order):
-    kept, come = (a.reshape(-1, 2, 2, *a.shape[1:]) for a in (kept, shifted(sent, "core", 1)))
-    terms = [kept, come]
-    if order == "both":
-        half = kept.shape[-2] // 32 * 16
-        one = halve(halve([t[..., :half, :] for t in terms], "x", 2), "y", 1)
-        two = halve(halve([t[..., half:, :] for t in terms], "y", 1), "x", 1)
-        return [jnp.concatenate([a, b], axis=1) for a, b in zip(one, two)]
-    if order == "xy":
-        return halve(halve(terms, "x", 2), "y", 1)
-    return halve(halve(terms, "y", 1), "x", 1)
-
-
-def reduce_line(planes, base):
+def first_ways(terms, aways=None):
+    half = terms[0].shape[-2] // 32 * 16
+    return (
+        halve([t[..., :half, :] for t in terms], "x", 2, aways),
+        halve([t[..., half:, :] for t in terms], "y", 1, aways),
+    )
+
+
+def second_ways(ways):
+    one, two = halve(ways[0], "y", 1), halve(ways[1], "x", 1)
+    return [jnp.concatenate([a, b], axis=1) for a, b in zip(one, two)]
+
+
+def send_line(planes, base):
     count = planes[0].shape[0]
     z = place_of("z")
     sums = total_of(planes).astype(BF)
@@ -775,7 +788,12 @@
                 pairs.append((device, goal * 8 + device % 8))
         away = pick(sums, jnp.clip((z + step) % 4 - base, 0, count - 1), 0)
         pieces.append(lax.ppermute(away, "fsdp", pairs))
-    return total_of([pick(t, jnp.clip(z - base, 0, count - 1), 0) for t in planes] + pieces)
+    return pieces
+
+
+def end_line(planes, pieces, base):
+    at = jnp.clip(place_of("z") - base, 0, planes[0].shape[0] - 1)
+    return total_of([pick(t, at, 0) for t in planes] + pieces)
 
 
 def own_part(own, vectors, local, n):
@@ -793,43 +811,87 @@
 def on_device(src, tgt, ls, lt, enc_weights, dec_weights, cotangent, n):
     split = n == 32
     e_own, d_own = own_rows(enc_weights, 4, n), own_rows(dec_weights, 6, n)
-    e_own, d_own = lax.optimization_barrier((e_own, d_own))
-    e_all, ev = (gather_parts if split else gather_plain)(e_own, 4, n)
-    d_all, dv = (gather_whole if split else gather_plain)(d_own, 6, n)
-    q1, k1, v1, o1, pre1, ax, axl = attn_fwd("full", 0, 0, ls, ls, src, src, e_all, ev)
+    if split:
+        b, c = at_home(e_own[:64]), at_home(e_own[64:])
+        c, b = widen(c, "z"), widen(b, "y")
+        b = widen(b, "z")
+        w = after(at_home(d_own), *(p for p, _ in b))
+        one, two = [(p[:, :64], l) for p, l in c], [(p[:, 64:], l) for p, l in c]
+        one, two, w = widen(one, "x"), widen(two, "y"), widen(w, "z")
+        b, one, two = widen(b, "x"), widen(one, "y"), widen(two, "x")
+        b = after(b, *(p for p, _ in w))
+        ready = [(0, 64, widen(b, "core")), (64, 128, widen(one, "core")), (128, 208, widen(two, "core"))]
+        e_all, ev = assemble(ready, n, 192, 4, 0)
+        e_all = e_all.reshape(-1, D)
+        low, high = [(p[:, :144], l) for p, l in w], [(p[:, 144:], l) for p, l in w]
+        low, high = widen(low, "x"), widen(high, "y")
+        low, high = after(low, ev), after(high, ev)
+        low, high = widen(low, "y"), widen(high, "x")
+    else:
+        e_all, ev = gather_plain(e_own, 4, n)
+        d_all, dv = gather_plain(d_own, 6, n)
+    q1, k1, v1, o1, pre1, ax, axl, lse1 = attn_fwd("full", 0, 0, ls, ls, src, src, e_all, ev)
+    if split:
+        low, high = after(low, axl), after(high, axl)
+        low, high = widen(low, "core"), widen(high, "core")
+        ax = hold(ax, *(p for p, _ in low[:2]), *(p for p, _ in high[:2]))
     hx, gpx, sum2, enc, wup_e = ffn_fwd(2, FF, ax, src, e_all, ev)
-    q3, k3, v3, o3, pre3, h1, h1l = attn_fwd("causal", 0, 0, lt, lt, tgt, tgt, d_all, dv)
-    q4, k4, v4, o4, pre4, h2, h2l = attn_fwd("cross", 2, FF, lt, ls, h1, enc, d_all, dv)
+    if split:
+        low, high = after(low, enc), after(high, enc)
+        d_all, dv = assemble([(0, 144, low), (144, 272, high)], n, 256, 6, 1)
+    q3, k3, v3, o3, pre3, h1, h1l, lse3 = attn_fwd("causal", 0, 0, lt, lt, tgt, tgt, d_all, dv)
+    q4, k4, v4, o4, pre4, h2, h2l, lse4 = attn_fwd("cross", 2, FF, lt, ls, h1, enc, d_all, dv)
     hy, gpy, sum5, final, wup_d = ffn_fwd(4, 2 * FF, h2, tgt, d_all, dv)
     if split:
-        d_plan = [("laid", 256, 16, 16), ("laid", 256, 8, 8), ("laid", 256, 0, 8)]
+        d_plan = [("owned", 256, ((16, 16),)), ("owned", 256, ((8, 8),)), ("owned", 256, ((0, 8),))]
         e_plan = [("owned", 192, ((16, 16), (10, 6))), ("owned", 192, ((0, 16),))]
-        seal = 3 * FF
     else:
         d_plan = [("plain", 2 * FF, 2 * FF), ("plain", FF, FF), ("plain", 0, FF)]
         e_plan = [("plain", FF, 2 * FF), ("plain", 0, FF)]
-        seal = None
-    g, dgb, ds5, ds4 = ffn_bwd(4, 2, d_plan[0], 2 * FF, cotangent, sum5, hy, gpy, h2l, pre4, wup_d, d_all, dv)
-    g3 = g
-    g, dgb, ds3, denc = attn_bwd(
-        "cross", 0, d_plan[1], FF, lt, ls, ds4, q4, k4, v4, o4, h1l, enc, d_all, dv, pre3, dgb, g3 if split else ()
+    g3, first3, dgb, ds5, ds4 = ffn_bwd(4, 2, d_plan[0], 2 * FF, cotangent, sum5, hy, gpy, h2l, pre4, wup_d, d_all, dv)
+    if split:
+        p23 = begin_plane(*g3)
+        p23 = halve(p23, "x", 2)
+        ds4 = hold(ds4, *p23[:-1])
+    g2, first2, dgb, ds3, denc = attn_bwd(
+        "cross", 0, d_plan[1], FF, lt, ls, ds4, q4, k4, v4, o4, lse4, h1l, enc, d_all, dv, pre3, dgb, first3
     )
-    g2 = g
-    g, tgt_grad = attn_bwd(
-        "causal", 0, d_plan[2], 0, lt, lt, ds3, q3, k3, v3, o3, tgt, tgt, d_all, dv, ds5, dgb, g2 if split else ()
+    if split:
+        p23[-1], ds3, *g2 = lax.optimization_barrier((p23[-1], ds3, *g2))
+        p1 = begin_plane(*g2)
+        p23, p1 = halve(p23, "y", 1), halve(p1, "y", 1)
+        ds3 = hold(ds3, *p23[:-1], *p1[:-1])
+    g1, _, tgt_grad = attn_bwd(
+        "causal", 0, d_plan[2], 0, lt, lt, ds3, q3, k3, v3, o3, lse3, tgt, tgt, d_all, dv, ds5, dgb, first2
     )
-    g1 = g
-    f, egb, ds2, ds1 = ffn_bwd(2, 0, e_plan[0], FF, denc, sum2, hx, gpx, axl, pre1, wup_e, e_all, ev, seal)
     if split:
-        d_sum = lax.psum_scatter(g1[0].reshape(-1, D), "fsdp", scatter_dimension=0, tiled=True).astype(F32)
-        high = reduce_line(reduce_plane(*f[:2], "yx"), 2)
-        a, src_grad = attn_bwd(
-            "full", 0, e_plan[1], 0, ls, ls, ds1, q1, k1, v1, o1, src, src, e_all, ev, ds2, egb, f[2:]
-        )
-        low = reduce_line(reduce_plane(*a, "both"), 0)
-        e_sum = jnp.where(place_of("z") >= 2, high, low)
+        p23[-1], p1[-1], denc, *g1 = lax.optimization_barrier((p23[-1], p1[-1], denc, *g1, tgt_grad))[:5]
+        p0 = begin_plane(*g1)
+        p1, p0 = halve(p1, "x", 1), halve(p0, "x", 2)
+        denc = hold(denc, *p1[:-1], *p0[:-1])
+    seal = 3 * FF if split else None
+    f, first, egb, ds2, ds1 = ffn_bwd(2, 0, e_plan[0], FF, denc, sum2, hx, gpx, axl, pre1, wup_e, e_all, ev, dgb, seal=seal)
+    if split:
+        p1[-1], p0[-1], ds1, *f = lax.optimization_barrier((p1[-1], p0[-1], ds1, *f))
+        e23 = begin_plane(*f[:2])
+        p0, e23 = halve(p0, "y", 1), first_ways(e23)
+        ds1 = hold(ds1, *p0[:-1])
+    a, _, src_grad = attn_bwd(
+        "full", 0, e_plan[1], 0, ls, ls, ds1, q1, k1, v1, o1, lse1, src, src, e_all, ev, ds2, egb, first, f[2:]
+    )
+    if split:
+        aways = []
+        e01 = first_ways(begin_plane(*a), aways)
+        p0[-1], e23[0][-1], e23[1][-1] = lax.optimization_barrier((p0[-1], e23[0][-1], e23[1][-1], *aways))[:3]
+        d_planes = [jnp.concatenate(t) for t in zip(p0, p1, p23)]
+        dz = send_line(d_planes, 0)
+        e_planes = [jnp.concatenate(t) for t in zip(second_ways(e01), second_ways(e23))]
+        ez = send_line(e_planes, 0)
+        d_sum = end_line(d_planes, dz, 0)
+        e_sum = end_line(e_planes, ez, 0)
+        tail = jnp.where(lax.axis_index("fsdp") == n - 1, jnp.roll(e_sum[-16:], -4, axis=0), d_sum[-16:])
+        d_sum = jnp.concatenate([d_sum[:-16], tail])
     else:
-        a, src_grad = attn_bwd("full", 0, e_plan[1], 0, ls, ls, ds1, q1, k1, v1, o1, src, src, e_all, ev, ds2, egb)
         vecs = lax.psum(jnp.concatenate([egb, dgb]), "fsdp")
         d_sum = scatter_plain(jnp.concatenate([g1[0], g2[0], g3[0]]), vecs[16:], n)
         e_sum = scatter_plain(jnp.concatenate([a[0], f[0]]), vecs[:16], n)

time: 475 us -> 425 us (0.89)
  the two profiles are of different devices: /device:TPU:9 before, /device:TPU:0 now
where the time goes in v2:
time: 425 us; the launch traced here: 419 us
  Pallas kernels  217 us (51%)
  waiting for transfers between devices  81.5 us (19%)
  starting transfers between devices  72.7 us (17%)
  local copies, waits for them, and re-layouts  33 us (8%)
  other arithmetic  12.6 us (3%)
    pallas_call x10, Pallas kernels, call(): pl.pallas_call(kernel, out_shape=tuple((jax.ShapeDtypeStruct(s, d) for s,...  204 us
    ppermute x48, waiting for transfers between devices, shifted(): return lax.ppermute(block, 'fsdp', pairs)  63.3 us
    ppermute x48, starting transfers between devices, shifted(): return lax.ppermute(block, 'fsdp', pairs)  50 us
    ppermute x6, starting transfers between devices, send_line(): pieces.append(lax.ppermute(away, 'fsdp', pairs))  22.7 us
    ppermute x6, waiting for transfers between devices, send_line(): pieces.append(lax.ppermute(away, 'fsdp', pairs))  18.1 us
    pallas_call x2, Pallas kernels, assemble(): pl.pallas_call(functools.partial(assemble_body, spans, labels, rows, vect...  12.9 us
    squeeze x19, local copies, waits for them, and re-layouts, pick(): return lax.dynamic_index_in_dim(array, at, axis, keepdims=False)  11.4 us
    convert_element_type x14, other arithmetic, halve(): away = total_of([pick(t, 1 - at, axis) for t in terms]).astype(BF)  10.1 us
  transfers between devices with their start and end apart: 54, of which 17 were waited for; matrix products, arithmetic and copies ran while one was open for 7% of the time, Pallas kernels for 33%

profile of v2, /device:TPU:0, one launch (start us, length us, event | category | flops | bytes accessed | tf_op | source)
XLA Modules:
  0.0 418.9 jit_solution(3352605309218217507)
XLA Ops:
  1.8 5.1 %collective-permute-start.13 = (bf16[1,144,512]{2,1,0:T(8,128)(2,1)S(1)}, bf16[1,144,512]{2,1,0:T(8,128)(2,1)S(1)}, u32[]{:S(2)}, u32[]{:S(2)}) collective-permute-start(bf16[1,144,512]{2,1,0:T(8,128)(2,1)S(1)} %broadcast_in_dim.7), channel_id=1, source_target_pairs={{0,24},{1,25},{2,26},{3,27},{4,28},{5,29},{6,30},{7,31},{8,0},{9,1... | collective-permute-start | bytes 442376 | tf_op jit(solution)/shard_map/ppermute | solution.py:636
  9.0 1.5 collective-permute-start
  10.6 1.2 pad_dynamic-slice_fusion
  12.0 1.3 collective-permute-done
  13.4 2.5 collective-permute-start.1
  16.7 1.8 collective-permute-done.11
  18.7 7.0 %collective-permute-done.12 = bf16[1,144,512]{2,1,0:T(8,128)(2,1)S(1)} collective-permute-done((bf16[1,144,512]{2,1,0:T(8,128)(2,1)S(1)}, bf16[1,144,512]{2,1,0:T(8,128)(2,1)S(1)}, u32[]{:S(2)}, u32[]{:S(2)}) %collective-permute-start.12) | collective-permute-done | bytes 147488 | tf_op jit(solution)/shard_map/ppermute | solution.py:636
  25.8 1.6 collective-permute-start.18
  27.5 1.6 collective-permute-start.14
  29.8 4.6 %collective-permute-start.6 = (bf16[1,272,512]{2,1,0:T(8,128)(2,1)S(1)}, bf16[1,272,512]{2,1,0:T(8,128)(2,1)S(1)}, u32[]{:S(2)}, u32[]{:S(2)}) collective-permute-start(bf16[1,272,512]{2,1,0:T(8,128)(2,1)S(1)} %broadcast_in_dim_reshape.3), channel_id=1, source_target_pairs={{0,24},{1,25},{2,26},{3,27},{4,28},{5,29},{6,30},{7,31},{8,0},{9,1... | collective-permute-start | bytes 835592 | tf_op jit(solution)/shard_map/ppermute | solution.py:636
  34.4 1.6 collective-permute-start.19
  36.7 1.6 collective-permute-start.15
  38.2 3.2 collective-permute-done.6
  41.5 9.2 %collective-permute-done.5 = bf16[1,272,512]{2,1,0:T(8,128)(2,1)S(1)} collective-permute-done((bf16[1,272,512]{2,1,0:T(8,128)(2,1)S(1)}, bf16[1,272,512]{2,1,0:T(8,128)(2,1)S(1)}, u32[]{:S(2)}, u32[]{:S(2)}) %collective-permute-start.5) | collective-permute-done | bytes 278560 | tf_op jit(solution)/shard_map/ppermute | solution.py:636
  50.7 1.9 collective-permute-start.4
  52.7 8.2 %collective-permute-done.4 = bf16[1,272,512]{2,1,0:T(8,128)(2,1)S(1)} collective-permute-done((bf16[1,272,512]{2,1,0:T(8,128)(2,1)S(1)}, bf16[1,272,512]{2,1,0:T(8,128)(2,1)S(1)}, u32[]{:S(2)}, u32[]{:S(2)}) %collective-permute-start.4) | collective-permute-done | bytes 278560 | tf_op jit(solution)/shard_map/ppermute | solution.py:636
  63.3 1.6 collective-permute-start.7
  64.8 1.5 collective-permute-start.25
  68.8 5.7 %shard_map.110 = (bf16[32,192,512]{2,1,0:T(8,128)(2,1)}, f32[16,512]{1,0:T(8,128)}) custom-call(bf16[8,64,512]{2,1,0:T(8,128)(2,1)} %copy-done.26, bf16[8,64,512]{2,1,0:T(8,128)(2,1)} %copy-done.34, bf16[8,64,512]{2,1,0:T(8,128)(2,1)} %collective-permute-done.9.refs_2_, bf16[8,64,512]{2,1,0:T(8,128)(2,1)} %copy-done.37, bf16[8,64,512]{2,1,0:T(8,128)(2,1)} %copy-done.25, ...), custom_call_target="tpu_custom_call" | custom-call | flops 80000000000 | bytes 1048576 | tf_op jit(solution)/shard_map/pallas_call | solution.py:701
  74.5 4.4 %collective-permute-done.7 = bf16[4,144,512]{2,1,0:T(8,128)(2,1)S(1)} collective-permute-done((bf16[4,144,512]{2,1,0:T(8,128)(2,1)S(1)}, bf16[4,144,512]{2,1,0:T(8,128)(2,1)S(1)}, u32[]{:S(2)}, u32[]{:S(2)}) %collective-permute-start.7) | collective-permute-done | bytes 589856 | tf_op jit(solution)/shard_map/ppermute | solution.py:636
  79.0 1.6 collective-permute-start.22
  80.7 1.6 collective-permute-start.26
  82.3 16.9 %shard_map.111 = (bf16[1024,512]{1,0:T(8,128)(2,1)}, bf16[1024,512]{1,0:T(8,128)(2,1)}, bf16[1024,512]{1,0:T(8,128)(2,1)}, bf16[1024,512]{1,0:T(8,128)(2,1)}, f3...) custom-call(s32[1,16]{1,0:T(1,128)} %refs_1_.15, s32[1,16]{1,0:T(1,128)} %refs_1_.15, ...), custom_call_target="tpu_custom_call" | custom-call | flops 120000004096 | bytes 1048576 | tf_op jit(solution)/shard_map/pallas_call | solution.py:146
  99.1 6.0 %collective-permute-done.26.refs_5_ = bf16[8,128,512]{2,1,0:T(8,128)(2,1)S(1)} collective-permute-done((bf16[8,128,512]{2,1,0:T(8,128)(2,1)S(1)}, bf16[8,128,512]{2,1,0:T(8,128)(2,1)S(1)}, u32[]{:S(2)}, u32[]{:S(2)}) %collective-permute-start.26) | collective-permute-done | bytes 1048608 | tf_op jit(solution)/shard_map/ppermute | solution.py:636
  107.0 16.4 %shard_map.112 = (bf16[1024,2048]{1,0:T(8,128)(2,1)}, bf16[1024,2048]{1,0:T(8,128)(2,1)}, f32[1024,512]{1,0:T(8,128)}, bf16[1024,512]{1,0:T(8,128)(2,1)}, bf16[4,512,512]{2,1,0:T(8,128)(2,1)}) custom-call(f32[1024,512]{1,0:T(8,128)} %get-tuple-element.126.refs_0_, bf16[1024,512]{1,0:T(8,128)(2,1)} %refs_11_.3, bf16[6144,512]{1,0:T(8,128)(2,1)} %bitcast.197, ...), custom_call_target="tpu_custom_call" | custom-call | flops 120000004096 | bytes 1048576 | tf_op jit(solution)/shard_map/pallas_call | solution.py:146
  125.5 7.2 %shard_map.113 = (bf16[32,272,512]{2,1,0:T(8,128)(2,1)}, f32[16,512]{1,0:T(8,128)}) custom-call(bf16[8,144,512]{2,1,0:T(8,128)(2,1)} %copy-done.20, bf16[8,144,512]{2,1,0:T(8,128)(2,1)} %copy-done.27, bf16[8,144,512]{2,1,0:T(8,128)(2,1)} %copy-done.28, bf16[8,144,512]{2,1,0:T(8,128)(2,1)} %copy-done.29, bf16[8,128,512]{2,1,0:T(8,128)(2,1)} %copy-done.23, ...), custom_call_target="tpu_custom_call" | custom-call | flops 80000000000 | bytes 1048576 | tf_op jit(solution)/shard_map/pallas_call | solution.py:701
  132.7 13.5 %shard_map.114 = (bf16[1024,512]{1,0:T(8,128)(2,1)}, bf16[1024,512]{1,0:T(8,128)(2,1)}, bf16[1024,512]{1,0:T(8,128)(2,1)}, bf16[1024,512]{1,0:T(8,128)(2,1)}, f3...) custom-call(s32[1,16]{1,0:T(1,128)} %refs_1_.14, s32[1,16]{1,0:T(1,128)} %refs_1_.14, ...), custom_call_target="tpu_custom_call" | custom-call | flops 120000004096 | bytes 1048576 | tf_op jit(solution)/shard_map/pallas_call | solution.py:146
  146.2 19.0 %shard_map.115 = (bf16[1024,512]{1,0:T(8,128)(2,1)}, bf16[1024,512]{1,0:T(8,128)(2,1)}, bf16[1024,512]{1,0:T(8,128)(2,1)}, bf16[1024,512]{1,0:T(8,128)(2,1)}, f3...) custom-call(s32[1,16]{1,0:T(1,128)} %refs_1_.14, s32[1,16]{1,0:T(1,128)} %refs_1_.15, ...), custom_call_target="tpu_custom_call" | custom-call | flops 120000004096 | bytes 1048576 | tf_op jit(solution)/shard_map/pallas_call | solution.py:146
  165.2 16.5 %shard_map.116 = (bf16[1024,2048]{1,0:T(8,128)(2,1)}, bf16[1024,2048]{1,0:T(8,128)(2,1)}, f32[1024,512]{1,0:T(8,128)}, bf16[1024,512]{1,0:T(8,128)(2,1)}, bf16[4,512,512]{2,1,0:T(8,128)(2,1)}) custom-call(f32[1024,512]{1,0:T(8,128)} %get-tuple-element.139.refs_0_, bf16[1024,512]{1,0:T(8,128)(2,1)} %refs_11_.2, ...), custom_call_target="tpu_custom_call" | custom-call | flops 120000004096 | bytes 1048576 | tf_op jit(solution)/shard_map/pallas_call | solution.py:146
  181.7 21.6 %shard_map.117 = (bf16[8,272,512]{2,1,0:T(8,128)(2,1)}, bf16[8,272,512]{2,1,0:T(8,128)(2,1)}, bf16[16,512]{1,0:T(8,128)(2,1)}, f32[16,512]{1,0:T(8,128)}, f32[1024,512]{1,0:T(8,128)}, /*index=5*/f32[1024,512]{1,0:T(8,128)}) custom-call(bf16[1024,512]{1,0:T(8,128)(2,1)} %refs_0_.10, f32[1024,512]{1,0:T(8,128)} %get-tuple-element.141.refs_1_, ...), custom_call_target="tpu_custom_call" | custom-call | flops 130000003072 | bytes 1048576 | tf_op jit(solution)/shard_map/pallas_call | solution.py:146
  203.4 4.5 %collective-permute-done.29 = bf16[8,272,512]{2,1,0:T(8,128)(2,1)S(1)} collective-permute-done((bf16[8,272,512]{2,1,0:T(8,128)(2,1)}, bf16[8,272,512]{2,1,0:T(8,128)(2,1)S(1)}, u32[]{:S(2)}, u32[]{:S(2)}) %collective-permute-start.29) | collective-permute-done | bytes 2228256 | tf_op jit(solution)/shard_map/ppermute | solution.py:636
  207.9 3.3 fusion
  211.3 1.5 collective-permute-start.30
  212.8 28.1 %shard_map.118 = (bf16[4,272,512]{2,1,0:T(8,128)(2,1)}, bf16[4,272,512]{2,1,0:T(8,128)(2,1)}, bf16[16,512]{1,0:T(8,128)(2,1)}, f32[16,512]{1,0:T(8,128)}, f32[1024,512]{1,0:T(8,128)}, /*index=5*/f32[1024,512]{1,0:T(8,128)}) custom-call(s32[1,16]{1,0:T(1,128)} %refs_1_.14, s32[1,16]{1,0:T(1,128)} %refs_1_.15, f32[1024,512]{1,0:T(8,128)} %get-tuple-element.149.refs_2_, ...), custom_call_target="tpu_custom_call" | custom-call | flops 260000006144 | bytes 1048576 | tf_op jit(solution)/shard_map/pallas_call | solution.py:146
  241.9 1.9 dynamic-slice_bitcast_fusion.1
  243.8 2.4 fusion.1
  246.2 1.5 collective-permute-start.32
  247.7 1.9 dynamic-slice_bitcast_fusion
  251.3 24.7 %shard_map.119 = (bf16[4,272,512]{2,1,0:T(8,128)(2,1)}, bf16[4,272,512]{2,1,0:T(8,128)(2,1)}, bf16[16,512]{1,0:T(8,128)(2,1)}, f32[1024,512]{1,0:T(8,128)}) custom-call(s32[1,16]{1,0:T(1,128)} %refs_1_.14, s32[1,16]{1,0:T(1,128)} %refs_1_.14, f32[1024,512]{1,0:T(8,128)} %get-tuple-element.167.refs_2_, bf16[1024,512]{1,0:T(8,128)(2,1)} %get-tuple-element.168.refs_3_, ...), custom_call_target="tpu_custom_call" | custom-call | flops 260000006144 | bytes 1048576 | tf_op jit(solution)/shard_map/pallas_call | solution.py:146
  276.8 1.7 dynamic-slice_bitcast_fusion.10
  278.5 1.1 fusion.5
  280.2 1.7 dynamic-slice_bitcast_fusion.9
  282.1 1.6 collective-permute-start.36
  283.7 21.5 %shard_map.120 = (bf16[8,208,512]{2,1,0:T(8,128)(2,1)}, bf16[8,208,512]{2,1,0:T(8,128)(2,1)}, bf16[3,208,512]{2,1,0:T(8,128)(2,1)}, bf16[3,208,512]{2,1,0:T(8,12...) custom-call(f32[1024,512]{1,0:T(8,128)} %get-tuple-element.183.refs_0_, ...), custom_call_target="tpu_custom_call" | custom-call | flops 130000003072 | bytes 1048576 | tf_op jit(solution)/shard_map/pallas_call | solution.py:146
  307.5 25.8 %shard_map.121 = (bf16[8,208,512]{2,1,0:T(8,128)(2,1)}, bf16[8,208,512]{2,1,0:T(8,128)(2,1)}, bf16[16,512]{1,0:T(8,128)(2,1)}, f32[1024,512]{1,0:T(8,128)}) custom-call(s32[1,16]{1,0:T(1,128)} %refs_1_.15, s32[1,16]{1,0:T(1,128)} %refs_1_.15, f32[1024,512]{1,0:T(8,128)} %get-tuple-element.196.refs_2_, bf16[1024,512]{1,0:T(8,128)(2,1)} %get-tuple-element.197.refs_3_, ...), custom_call_target="tpu_custom_call" | custom-call | flops 260000006144 | bytes 1048576 | tf_op jit(solution)/shard_map/pallas_call | solution.py:146
  334.1 1.2 copy-done.11
  335.5 1.3 copy-done.12
  339.0 1.6 collective-permute-start.41
  340.7 1.2 slice.147
  341.9 1.2 slice.148
  343.2 1.2 slice.145
  344.4 1.2 slice.146
  347.5 1.6 collective-permute-start.39
  349.3 1.6 collective-permute-start.40
  351.1 14.4 %collective-permute-done.39 = bf16[2,2,96,512]{3,2,0,1:T(8,128)(2,1)S(1)} collective-permute-done((bf16[2,2,96,512]{3,2,0,1:T(8,128)(2,1)S(1)}, bf16[2,2,96,512]{3,2,0,1:T(8,128)(2,1)S(1)}, u32[]{:S(2)}, u32[]{:S(2)}) %collective-permute-start.39) | collective-permute-done | bytes 393248 | tf_op jit(solution)/shard_map/ppermute | solution.py:636
  367.0 1.3 collective-permute-start.46
  368.4 1.3 collective-permute-done.40
  369.8 2.0 collective-permute-start.45
  373.7 1.8 collective-permute-start.53
  376.9 1.4 collective-permute-start.51
  378.9 2.5 collective-permute-start.50
  382.9 15.4 %collective-permute-start.48 = (bf16[208,512]{1,0:T(8,128)(2,1)S(1)}, bf16[208,512]{1,0:T(8,128)(2,1)S(1)}, u32[]{:S(2)}, u32[]{:S(2)}) collective-permute-start(bf16[208,512]{1,0:T(8,128)(2,1)S(1)} %get-tuple-element.220), channel_id=1, source_target_pairs={{0,8},{1,9},{2,10},{3,11},{4,12},{5,13},{6,14},{7,15},{8,16},{9,17... | collective-permute-start | bytes 638984 | tf_op jit(solution)/shard_map/ppermute | solution.py:790
  398.2 12.4 %collective-permute-done.52 = bf16[272,512]{1,0:T(8,128)(2,1)S(1)} collective-permute-done((bf16[272,512]{1,0:T(8,128)(2,1)S(1)}, bf16[272,512]{1,0:T(8,128)(2,1)S(1)}, u32[]{:S(2)}, u32[]{:S(2)}) %collective-permute-start.52) | collective-permute-done | bytes 278560 | tf_op jit(solution)/shard_map/ppermute | solution.py:790
  411.0 5.0 %collective-permute-done.49 = bf16[208,512]{1,0:T(8,128)(2,1)S(1)} collective-permute-done((bf16[208,512]{1,0:T(8,128)(2,1)S(1)}, bf16[208,512]{1,0:T(8,128)(2,1)S(1)}, u32[]{:S(2)}, u32[]{:S(2)}) %collective-permute-start.49) | collective-permute-done | bytes 213024 | tf_op jit(solution)/shard_map/ppermute | solution.py:790
  (238 shorter events, 36.5 us)
Async XLA Ops:
  1.8 23.9 %collective-permute-start.13 = (bf16[1,144,512]{2,1,0:T(8,128)(2,1)S(1)}, bf16[1,144,512]{2,1,0:T(8,128)(2,1)S(1)}, u32[]{:S(2)}, u32[]{:S(2)}) collective-permute-start(bf16[1,144,512]{2,1,0:T(8,128)(2,1)S(1)} %broadcast_in_dim.7), channel_id=1, source_target_pairs={{0,24},{1,25},{2,26},{3,27},{4,28},{5,29},{6,30},{7,31},{8,0},{9,1... | collective-permute-start | bytes 442376 | tf_op jit(solution)/shard_map/ppermute | solution.py:636
  6.9 18.8 %collective-permute-start.12 = (bf16[1,144,512]{2,1,0:T(8,128)(2,1)S(1)}, bf16[1,144,512]{2,1,0:T(8,128)(2,1)S(1)}, u32[]{:S(2)}, u32[]{:S(2)}) collective-permute-start(bf16[1,144,512]{2,1,0:T(8,128)(2,1)S(1)} %broadcast_in_dim.7), channel_id=1, source_target_pairs={{0,16},{1,17},{2,18},{3,19},{4,20},{5,21},{6,22},{7,23},{8,24},{9,... | collective-permute-start | bytes 442376 | tf_op jit(solution)/shard_map/ppermute | solution.py:636
  6.9 11.6 %collective-permute-start.11 = (bf16[1,144,512]{2,1,0:T(8,128)(2,1)S(1)}, bf16[1,144,512]{2,1,0:T(8,128)(2,1)S(1)}, u32[]{:S(2)}, u32[]{:S(2)}) collective-permute-start(bf16[1,144,512]{2,1,0:T(8,128)(2,1)S(1)} %broadcast_in_dim.7), channel_id=1, source_target_pairs={{0,8},{1,9},{2,10},{3,11},{4,12},{5,13},{6,14},{7,15},{8,16},{9,17... | collective-permute-start | bytes 442376 | tf_op jit(solution)/shard_map/ppermute | solution.py:636
  9.0 4.3 %collective-permute-start = (bf16[1,64,512]{2,1,0:T(8,128)(2,1)S(1)}, bf16[1,64,512]{2,1,0:T(8,128)(2,1)S(1)}, u32[]{:S(2)}, u32[]{:S(2)}) collective-permute-start(bf16[1,64,512]{2,1,0:T(8,128)(2,1)S(1)} %broadcast_in_dim.6), channel_id=1, source_target_pairs={{0,4},{1,5},{2,6},{3,7},{4,0},{5,1},{6,2},{7,3},{8,12},{9,13},{10,... | collective-permute-start | bytes 196616 | tf_op jit(solution)/shard_map/ppermute | solution.py:636
  13.4 15.7 %collective-permute-start.1 = (bf16[2,64,512]{2,1,0:T(8,128)(2,1)S(1)}, bf16[2,64,512]{2,1,0:T(8,128)(2,1)S(1)}, u32[]{:S(2)}, u32[]{:S(2)}) collective-permute-start(bf16[2,64,512]{2,1,0:T(8,128)(2,1)S(1)} %get-tuple-element.240), channel_id=1, source_target_pairs={{0,8},{1,9},{2,10},{3,11},{4,12},{5,13},{6,14},{7,15},{8,16},{9,17... | collective-permute-start | bytes 393224 | tf_op jit(solution)/shard_map/ppermute | solution.py:636
  15.8 13.2 %collective-permute-start.2 = (bf16[2,64,512]{2,1,0:T(8,128)(2,1)S(1)}, bf16[2,64,512]{2,1,0:T(8,128)(2,1)S(1)}, u32[]{:S(2)}, u32[]{:S(2)}) collective-permute-start(bf16[2,64,512]{2,1,0:T(8,128)(2,1)S(1)} %get-tuple-element.240), channel_id=1, source_target_pairs={{0,16},{1,17},{2,18},{3,19},{4,20},{5,21},{6,22},{7,23},{8,24},{9,... | collective-permute-start | bytes 393224 | tf_op jit(solution)/shard_map/ppermute | solution.py:636
  18.5 11.3 %collective-permute-start.3 = (bf16[2,64,512]{2,1,0:T(8,128)(2,1)S(1)}, bf16[2,64,512]{2,1,0:T(8,128)(2,1)S(1)}, u32[]{:S(2)}, u32[]{:S(2)}) collective-permute-start(bf16[2,64,512]{2,1,0:T(8,128)(2,1)S(1)} %get-tuple-element.240), channel_id=1, source_target_pairs={{0,24},{1,25},{2,26},{3,27},{4,28},{5,29},{6,30},{7,31},{8,0},{9,1... | collective-permute-start | bytes 393224 | tf_op jit(solution)/shard_map/ppermute | solution.py:636
  25.8 8.5 %collective-permute-start.18 = (bf16[4,80,512]{2,1,0:T(8,128)(2,1)S(1)}, bf16[4,80,512]{2,1,0:T(8,128)(2,1)S(1)}, u32[]{:S(2)}, u32[]{:S(2)}) collective-permute-start(bf16[4,80,512]{2,1,0:T(8,128)(2,1)S(1)} %pad_maximum_fusion.5), channel_id=1, source_target_pairs={{0,4},{1,5},{2,6},{3,7},{4,0},{5,1},{6,2},{7,3},{8,12},{9,13},{10,... | collective-permute-start | bytes 983048 | tf_op jit(solution)/shard_map/ppermute | solution.py:636
  27.5 9.1 %collective-permute-start.14 = (bf16[4,64,512]{2,1,0:T(8,128)(2,1)S(1)}, bf16[4,64,512]{2,1,0:T(8,128)(2,1)S(1)}, u32[]{:S(2)}, u32[]{:S(2)}) collective-permute-start(bf16[4,64,512]{2,1,0:T(8,128)(2,1)S(1)} %pad_maximum_fusion.6), channel_id=1, source_target_pairs={{0,2},{1,3},{2,0},{3,1},{4,6},{5,7},{6,4},{7,5},{8,10},{9,11},{10,... | collective-permute-start | bytes 786440 | tf_op jit(solution)/shard_map/ppermute | solution.py:636
  29.8 11.7 %collective-permute-start.6 = (bf16[1,272,512]{2,1,0:T(8,128)(2,1)S(1)}, bf16[1,272,512]{2,1,0:T(8,128)(2,1)S(1)}, u32[]{:S(2)}, u32[]{:S(2)}) collective-permute-start(bf16[1,272,512]{2,1,0:T(8,128)(2,1)S(1)} %broadcast_in_dim_reshape.3), channel_id=1, source_target_pairs={{0,24},{1,25},{2,26},{3,27},{4,28},{5,29},{6,30},{7,31},{8,0},{9,1... | collective-permute-start | bytes 835592 | tf_op jit(solution)/shard_map/ppermute | solution.py:636
  34.4 16.4 %collective-permute-start.5 = (bf16[1,272,512]{2,1,0:T(8,128)(2,1)S(1)}, bf16[1,272,512]{2,1,0:T(8,128)(2,1)S(1)}, u32[]{:S(2)}, u32[]{:S(2)}) collective-permute-start(bf16[1,272,512]{2,1,0:T(8,128)(2,1)S(1)} %broadcast_in_dim_reshape.3), channel_id=1, source_target_pairs={{0,16},{1,17},{2,18},{3,19},{4,20},{5,21},{6,22},{7,23},{8,24},{9,... | collective-permute-start | bytes 835592 | tf_op jit(solution)/shard_map/ppermute | solution.py:636
  34.4 28.7 %copy-start.24 = (bf16[8,80,512]{2,1,0:T(8,128)(2,1)}, bf16[8,80,512]{2,1,0:T(8,128)(2,1)S(1)}, u32[]{:S(2)}) copy-start(bf16[8,80,512]{2,1,0:T(8,128)(2,1)S(1)} %constant_dynamic-update-slice_fusion.12.refs_8_) | copy-start | bytes 1966084
  34.4 26.4 %collective-permute-start.19 = (bf16[8,80,512]{2,1,0:T(8,128)(2,1)S(1)}, bf16[8,80,512]{2,1,0:T(8,128)(2,1)S(1)}, u32[]{:S(2)}, u32[]{:S(2)}) collective-permute-start(bf16[8,80,512]{2,1,0:T(8,128)(2,1)S(1)} %constant_dynamic-update-slice_fusion.12.refs_8_), channel_id=1, source_target_pairs={{0,2},{1,3},{2,0},{3,1},{4,6},{5,7},{6,4},{7,5},{8,10},{9,11},{10,... | collective-permute-start | bytes 1966088 | tf_op jit(solution)/shard_map/ppermute | solution.py:636
  36.0 27.1 %copy-start.26 = (bf16[8,64,512]{2,1,0:T(8,128)(2,1)}, bf16[8,64,512]{2,1,0:T(8,128)(2,1)S(1)}, u32[]{:S(2)}) copy-start(bf16[8,64,512]{2,1,0:T(8,128)(2,1)S(1)} %constant_dynamic-update-slice_fusion.2.refs_0_) | copy-start | bytes 1572868
  36.0 25.4 %collective-permute-start.8 = (bf16[8,64,512]{2,1,0:T(8,128)(2,1)S(1)}, bf16[8,64,512]{2,1,0:T(8,128)(2,1)S(1)}, u32[]{:S(2)}, u32[]{:S(2)}) collective-permute-start(bf16[8,64,512]{2,1,0:T(8,128)(2,1)S(1)} %constant_dynamic-update-slice_fusion.2.refs_0_), channel_id=1, source_target_pairs={{0,2},{1,3},{2,0},{3,1},{4,6},{5,7},{6,4},{7,5},{8,10},{9,11},{10,... | collective-permute-start | bytes 1572872 | tf_op jit(solution)/shard_map/ppermute | solution.py:636
  36.7 26.6 %copy-start.25 = (bf16[8,64,512]{2,1,0:T(8,128)(2,1)}, bf16[8,64,512]{2,1,0:T(8,128)(2,1)S(1)}, u32[]{:S(2)}) copy-start(bf16[8,64,512]{2,1,0:T(8,128)(2,1)S(1)} %constant_dynamic-update-slice_fusion.7.refs_4_) | copy-start | bytes 1572868
  36.7 24.8 %collective-permute-start.15 = (bf16[8,64,512]{2,1,0:T(8,128)(2,1)S(1)}, bf16[8,64,512]{2,1,0:T(8,128)(2,1)S(1)}, u32[]{:S(2)}, u32[]{:S(2)}) collective-permute-start(bf16[8,64,512]{2,1,0:T(8,128)(2,1)S(1)} %constant_dynamic-update-slice_fusion.7.refs_4_), channel_id=1, source_target_pairs={{0,4},{1,5},{2,6},{3,7},{4,0},{5,1},{6,2},{7,3},{8,12},{9,13},{10,... | collective-permute-start | bytes 1572872 | tf_op jit(solution)/shard_map/ppermute | solution.py:636
  41.5 20.4 %collective-permute-start.16 = (bf16[8,64,512]{2,1,0:T(8,128)(2,1)S(1)}, bf16[8,64,512]{2,1,0:T(8,128)(2,1)S(1)}, u32[]{:S(2)}, u32[]{:S(2)}) collective-permute-start(bf16[8,64,512]{2,1,0:T(8,128)(2,1)S(1)} %constant_dynamic-update-slice_fusion.7.refs_4_), channel_id=1, source_target_pairs={{0,1},{1,0},{2,3},{3,2},{4,5},{5,4},{6,7},{7,6},{8,9},{9,8},{10,11... | collective-permute-start | bytes 1572872 | tf_op jit(solution)/shard_map/ppermute | solution.py:636
  50.7 10.2 %collective-permute-start.4 = (bf16[1,272,512]{2,1,0:T(8,128)(2,1)S(1)}, bf16[1,272,512]{2,1,0:T(8,128)(2,1)S(1)}, u32[]{:S(2)}, u32[]{:S(2)}) collective-permute-start(bf16[1,272,512]{2,1,0:T(8,128)(2,1)S(1)} %broadcast_in_dim_reshape.3), channel_id=1, source_target_pairs={{0,8},{1,9},{2,10},{3,11},{4,12},{5,13},{6,14},{7,15},{8,16},{9,17... | collective-permute-start | bytes 835592 | tf_op jit(solution)/shard_map/ppermute | solution.py:636
  60.9 2.4 collective-permute-start.20
  60.9 7.1 %collective-permute-start.21 = (bf16[8,80,512]{2,1,0:T(8,128)(2,1)S(1)}, bf16[8,80,512]{2,1,0:T(8,128)(2,1)S(1)}, u32[]{:S(2)}, u32[]{:S(2)}) collective-permute-start(bf16[8,80,512]{2,1,0:T(8,128)(2,1)S(1)} %collective-permute-done.19.refs_9_), channel_id=1, source_target_pairs={{0,1},{1,0},{2,3},{3,2},{4,5},{5,4},{6,7},{7,6},{8,9},{9,8},{10,11... | collective-permute-start | bytes 1966088 | tf_op jit(solution)/shard_map/ppermute | solution.py:636
  61.4 3.4 collective-permute-start.9
  61.5 4.9 %collective-permute-start.10 = (bf16[8,64,512]{2,1,0:T(8,128)(2,1)S(1)}, bf16[8,64,512]{2,1,0:T(8,128)(2,1)S(1)}, u32[]{:S(2)}, u32[]{:S(2)}) collective-permute-start(bf16[8,64,512]{2,1,0:T(8,128)(2,1)S(1)} %collective-permute-done.8.refs_1_), channel_id=1, source_target_pairs={{0,1},{1,0},{2,3},{3,2},{4,5},{5,4},{6,7},{7,6},{8,9},{9,8},{10,11... | collective-permute-start | bytes 1572872 | tf_op jit(solution)/shard_map/ppermute | solution.py:636
  62.7 3.6 collective-permute-start.17
  63.3 15.6 %collective-permute-start.7 = (bf16[4,144,512]{2,1,0:T(8,128)(2,1)S(1)}, bf16[4,144,512]{2,1,0:T(8,128)(2,1)S(1)}, u32[]{:S(2)}, u32[]{:S(2)}) collective-permute-start(bf16[4,144,512]{2,1,0:T(8,128)(2,1)S(1)} %pad_maximum_fusion.3), channel_id=1, source_target_pairs={{0,2},{1,3},{2,0},{3,1},{4,6},{5,7},{6,4},{7,5},{8,10},{9,11},{10,... | collective-permute-start | bytes 1769480 | tf_op jit(solution)/shard_map/ppermute | solution.py:636
  64.8 15.8 %collective-permute-start.25 = (bf16[4,128,512]{2,1,0:T(8,128)(2,1)S(1)}, bf16[4,128,512]{2,1,0:T(8,128)(2,1)S(1)}, u32[]{:S(2)}, u32[]{:S(2)}) collective-permute-start(bf16[4,128,512]{2,1,0:T(8,128)(2,1)S(1)} %pad_maximum_fusion.4), channel_id=1, source_target_pairs={{0,4},{1,5},{2,6},{3,7},{4,0},{5,1},{6,2},{7,3},{8,12},{9,13},{10,... | collective-permute-start | bytes 1572872 | tf_op jit(solution)/shard_map/ppermute | solution.py:636
  79.0 27.5 %copy-start.20 = (bf16[8,144,512]{2,1,0:T(8,128)(2,1)}, bf16[8,144,512]{2,1,0:T(8,128)(2,1)S(1)}, u32[]{:S(2)}) copy-start(bf16[8,144,512]{2,1,0:T(8,128)(2,1)S(1)} %constant_dynamic-update-slice_fusion.17.refs_0_) | copy-start | bytes 3538948
  79.0 27.5 %collective-permute-start.22 = (bf16[8,144,512]{2,1,0:T(8,128)(2,1)S(1)}, bf16[8,144,512]{2,1,0:T(8,128)(2,1)S(1)}, u32[]{:S(2)}, u32[]{:S(2)}) collective-permute-start(bf16[8,144,512]{2,1,0:T(8,128)(2,1)S(1)} %constant_dynamic-update-slice_fusion.17.refs_0_), channel_id=1, source_target_pairs={{0,4},{1,5},{2,6},{3,7},{4,0},{5,1},{6,2},{7,3},{8,12},{9,13},{10,... | collective-permute-start | bytes 3538952 | tf_op jit(solution)/shard_map/ppermute | solution.py:636
  80.7 24.4 %collective-permute-start.26 = (bf16[8,128,512]{2,1,0:T(8,128)(2,1)S(1)}, bf16[8,128,512]{2,1,0:T(8,128)(2,1)S(1)}, u32[]{:S(2)}, u32[]{:S(2)}) collective-permute-start(bf16[8,128,512]{2,1,0:T(8,128)(2,1)S(1)} %constant_dynamic-update-slice_fusion.19.refs_4_), channel_id=1, source_target_pairs={{0,2},{1,3},{2,0},{3,1},{4,6},{5,7},{6,4},{7,5},{8,10},{9,11},{10,... | collective-permute-start | bytes 3145736 | tf_op jit(solution)/shard_map/ppermute | solution.py:636
  105.1 18.3 %collective-permute-start.27 = (bf16[8,128,512]{2,1,0:T(8,128)(2,1)S(1)}, bf16[8,128,512]{2,1,0:T(8,128)(2,1)}, u32[]{:S(2)}, u32[]{:S(2)}) collective-permute-start(bf16[8,128,512]{2,1,0:T(8,128)(2,1)S(1)} %constant_dynamic-update-slice_fusion.19.refs_4_), channel_id=1, source_target_pairs={{0,1},{1,0},{2,3},{3,2},{4,5},{5,4},{6,7},{7,6},{8,9},{9,8},{10,11... | collective-permute-start | bytes 3145736 | tf_op jit(solution)/shard_map/ppermute | solution.py:636
  105.1 18.4 %collective-permute-start.28 = (bf16[8,128,512]{2,1,0:T(8,128)(2,1)S(1)}, bf16[8,128,512]{2,1,0:T(8,128)(2,1)}, u32[]{:S(2)}, u32[]{:S(2)}) collective-permute-start(bf16[8,128,512]{2,1,0:T(8,128)(2,1)S(1)} %collective-permute-done.26.refs_5_), channel_id=1, source_target_pairs={{0,1},{1,0},{2,3},{3,2},{4,5},{5,4},{6,7},{7,6},{8,9},{9,8},{10,11... | collective-permute-start | bytes 3145736 | tf_op jit(solution)/shard_map/ppermute | solution.py:636
  106.5 17.0 %collective-permute-start.23 = (bf16[8,144,512]{2,1,0:T(8,128)(2,1)S(1)}, bf16[8,144,512]{2,1,0:T(8,128)(2,1)S(1)}, u32[]{:S(2)}, u32[]{:S(2)}) collective-permute-start(bf16[8,144,512]{2,1,0:T(8,128)(2,1)S(1)} %constant_dynamic-update-slice_fusion.17.refs_0_), channel_id=1, source_target_pairs={{0,1},{1,0},{2,3},{3,2},{4,5},{5,4},{6,7},{7,6},{8,9},{9,8},{10,11... | collective-permute-start | bytes 3538952 | tf_op jit(solution)/shard_map/ppermute | solution.py:636
  106.5 17.0 %collective-permute-start.24 = (bf16[8,144,512]{2,1,0:T(8,128)(2,1)S(1)}, bf16[8,144,512]{2,1,0:T(8,128)(2,1)S(1)}, u32[]{:S(2)}, u32[]{:S(2)}) collective-permute-start(bf16[8,144,512]{2,1,0:T(8,128)(2,1)S(1)} %collective-permute-done.22.refs_1_), channel_id=1, source_target_pairs={{0,1},{1,0},{2,3},{3,2},{4,5},{5,4},{6,7},{7,6},{8,9},{9,8},{10,11... | collective-permute-start | bytes 3538952 | tf_op jit(solution)/shard_map/ppermute | solution.py:636
  203.3 4.6 %collective-permute-start.29 = (bf16[8,272,512]{2,1,0:T(8,128)(2,1)}, bf16[8,272,512]{2,1,0:T(8,128)(2,1)S(1)}, u32[]{:S(2)}, u32[]{:S(2)}) collective-permute-start(bf16[8,272,512]{2,1,0:T(8,128)(2,1)} %get-tuple-element.148), channel_id=1, source_target_pairs={{0,1},{1,0},{2,3},{3,2},{4,5},{5,4},{6,7},{7,6},{8,9},{9,8},{10,11... | collective-permute-start | bytes 6684680 | tf_op jit(solution)/shard_map/ppermute | solution.py:636
  211.3 29.6 %collective-permute-start.30 = (bf16[2,2,272,512]{3,2,0,1:T(8,128)(2,1)}, bf16[2,2,272,512]{3,2,0,1:T(8,128)(2,1)}, u32[]{:S(2)}, u32[]{:S(2)}) collective-permute-start(bf16[2,2,272,512]{3,2,0,1:T(8,128)(2,1)} %fusion), channel_id=1, source_target_pairs={{0,2},{1,3},{2,0},{3,1},{4,6},{5,7},{6,4},{7,5},{8,10},{9,11},{10,... | collective-permute-start | bytes 3342344 | tf_op jit(solution)/shard_map/ppermute | solution.py:636
  212.8 28.3 %copy-start.9 = (bf16[8,272,512]{2,1,0:T(8,128)(2,1)S(1)}, bf16[8,272,512]{2,1,0:T(8,128)(2,1)}, u32[]{:S(2)}) copy-start(bf16[8,272,512]{2,1,0:T(8,128)(2,1)} %get-tuple-element.147) | copy-start | bytes 6684676
  240.9 8.7 %collective-permute-start.31 = (bf16[4,272,512]{2,1,0:T(8,128)(2,1)}, bf16[4,272,512]{2,1,0:T(8,128)(2,1)S(1)}, u32[]{:S(2)}, u32[]{:S(2)}) collective-permute-start(bf16[4,272,512]{2,1,0:T(8,128)(2,1)} %get-tuple-element.163), channel_id=1, source_target_pairs={{0,1},{1,0},{2,3},{3,2},{4,5},{5,4},{6,7},{7,6},{8,9},{9,8},{10,11... | collective-permute-start | bytes 3342344 | tf_op jit(solution)/shard_map/ppermute | solution.py:636
  246.2 29.8 %collective-permute-start.32 = (bf16[2,272,512]{2,1,0:T(8,128)(2,1)}, bf16[2,272,512]{2,1,0:T(8,128)(2,1)}, u32[]{:S(2)}, u32[]{:S(2)}) collective-permute-start(bf16[2,272,512]{2,1,0:T(8,128)(2,1)} %fusion.1), channel_id=1, source_target_pairs={{0,4},{1,5},{2,6},{3,7},{4,0},{5,1},{6,2},{7,3},{8,12},{9,13},{10,... | collective-permute-start | bytes 1671176 | tf_op jit(solution)/shard_map/ppermute | solution.py:636
  250.8 25.2 %collective-permute-start.33 = (bf16[1,2,272,512]{3,2,1,0:T(8,128)(2,1)}, bf16[1,2,272,512]{3,2,1,0:T(8,128)(2,1)}, u32[]{:S(2)}, u32[]{:S(2)}) collective-permute-start(bf16[1,2,272,512]{3,2,1,0:T(8,128)(2,1)} %fusion.2), channel_id=1, source_target_pairs={{0,4},{1,5},{2,6},{3,7},{4,0},{5,1},{6,2},{7,3},{8,12},{9,13},{10,... | collective-permute-start | bytes 1671176 | tf_op jit(solution)/shard_map/ppermute | solution.py:636
  276.0 5.9 %collective-permute-start.35 = (bf16[4,272,512]{2,1,0:T(8,128)(2,1)}, bf16[4,272,512]{2,1,0:T(8,128)(2,1)S(1)}, u32[]{:S(2)}, u32[]{:S(2)}) collective-permute-start(bf16[4,272,512]{2,1,0:T(8,128)(2,1)} %get-tuple-element.181), channel_id=1, source_target_pairs={{0,1},{1,0},{2,3},{3,2},{4,5},{5,4},{6,7},{7,6},{8,9},{9,8},{10,11... | collective-permute-start | bytes 3342344 | tf_op jit(solution)/shard_map/ppermute | solution.py:636
  279.7 27.0 %collective-permute-start.34 = (bf16[1,272,512]{2,1,0:T(8,128)(2,1)S(1)}, bf16[1,272,512]{2,1,0:T(8,128)(2,1)S(1)}, u32[]{:S(2)}, u32[]{:S(2)}) collective-permute-start(bf16[1,272,512]{2,1,0:T(8,128)(2,1)S(1)} %fusion.5), channel_id=1, source_target_pairs={{0,2},{1,3},{2,0},{3,1},{4,6},{5,7},{6,4},{7,5},{8,10},{9,11},{10,... | collective-permute-start | bytes 835592 | tf_op jit(solution)/shard_map/ppermute | solution.py:636
  282.1 24.5 %collective-permute-start.36 = (bf16[1,2,272,512]{3,2,1,0:T(8,128)(2,1)S(1)}, bf16[1,2,272,512]{3,2,1,0:T(8,128)(2,1)S(1)}, u32[]{:S(2)}, u32[]{:S(2)}) collective-permute-start(bf16[1,2,272,512]{3,2,1,0:T(8,128)(2,1)S(1)} %fusion.3), channel_id=1, source_target_pairs={{0,2},{1,3},{2,0},{3,1},{4,6},{5,7},{6,4},{7,5},{8,10},{9,11},{10,... | collective-permute-start | bytes 1671176 | tf_op jit(solution)/shard_map/ppermute | solution.py:636
  306.6 26.6 %copy-start.21 = (bf16[1,272,512]{2,1,0:T(8,128)(2,1)}, bf16[1,272,512]{2,1,0:T(8,128)(2,1)S(1)}, u32[]{:S(2)}) copy-start(bf16[1,272,512]{2,1,0:T(8,128)(2,1)S(1)} %collective-permute-done.34) | copy-start | bytes 835588
  306.6 26.6 %copy-start.18 = (bf16[1,2,272,512]{3,2,1,0:T(8,128)(2,1)}, bf16[1,2,272,512]{3,2,1,0:T(8,128)(2,1)S(1)}, u32[]{:S(2)}) copy-start(bf16[1,2,272,512]{3,2,1,0:T(8,128)(2,1)S(1)} %collective-permute-done.36) | copy-start | bytes 1671172
  307.4 33.3 %collective-permute-start.38 = (bf16[8,208,512]{2,1,0:T(8,128)(2,1)}, bf16[8,208,512]{2,1,0:T(8,128)(2,1)}, u32[]{:S(2)}, u32[]{:S(2)}) collective-permute-start(bf16[8,208,512]{2,1,0:T(8,128)(2,1)} %get-tuple-element.211), channel_id=1, source_target_pairs={{0,1},{1,0},{2,3},{3,2},{4,5},{5,4},{6,7},{7,6},{8,9},{9,8},{10,11... | collective-permute-start | bytes 5111816 | tf_op jit(solution)/shard_map/ppermute | solution.py:636
  307.4 26.4 %copy-start = (bf16[2,272,512]{2,1,0:T(8,128)(2,1)S(1)}, bf16[2,272,512]{2,1,0:T(8,128)(2,1)}, u32[]{:S(2)}) copy-start(bf16[2,272,512]{2,1,0:T(8,128)(2,1)} %dynamic-slice_bitcast_fusion.2) | copy-start | bytes 1671172
  307.5 26.4 %copy-start.1 = (bf16[2,272,512]{2,1,0:T(8,128)(2,1)S(1)}, bf16[2,272,512]{2,1,0:T(8,128)(2,1)}, u32[]{:S(2)}) copy-start(bf16[2,272,512]{2,1,0:T(8,128)(2,1)} %dynamic-slice_bitcast_fusion.1) | copy-start | bytes 1671172
  307.5 26.4 %copy-start.3 = (bf16[1,272,512]{2,1,0:T(8,128)(2,1)S(1)}, bf16[1,272,512]{2,1,0:T(8,128)(2,1)}, u32[]{:S(2)}) copy-start(bf16[1,272,512]{2,1,0:T(8,128)(2,1)} %dynamic-slice_bitcast_fusion.11) | copy-start | bytes 835588
  333.3 9.9 %collective-permute-start.37 = (bf16[8,208,512]{2,1,0:T(8,128)(2,1)}, bf16[8,208,512]{2,1,0:T(8,128)(2,1)}, u32[]{:S(2)}, u32[]{:S(2)}) collective-permute-start(bf16[8,208,512]{2,1,0:T(8,128)(2,1)} %get-tuple-element.210), channel_id=1, source_target_pairs={{0,1},{1,0},{2,3},{3,2},{4,5},{5,4},{6,7},{7,6},{8,9},{9,8},{10,11... | collective-permute-start | bytes 5111816 | tf_op jit(solution)/shard_map/ppermute | solution.py:636
  339.0 27.2 %collective-permute-start.41 = (bf16[1,272,512]{2,1,0:T(8,128)(2,1)S(1)}, bf16[1,272,512]{2,1,0:T(8,128)(2,1)S(1)}, u32[]{:S(2)}, u32[]{:S(2)}) collective-permute-start(bf16[1,272,512]{2,1,0:T(8,128)(2,1)S(1)} %fusion.4), channel_id=1, source_target_pairs={{0,4},{1,5},{2,6},{3,7},{4,0},{5,1},{6,2},{7,3},{8,12},{9,13},{10,... | collective-permute-start | bytes 835592 | tf_op jit(solution)/shard_map/ppermute | solution.py:636
  346.1 20.1 %collective-permute-start.42 = (bf16[2,2,96,512]{3,2,0,1:T(8,128)(2,1)S(1)}, bf16[2,2,96,512]{3,2,0,1:T(8,128)(2,1)S(1)}, u32[]{:S(2)}, u32[]{:S(2)}) collective-permute-start(bf16[2,2,96,512]{3,2,0,1:T(8,128)(2,1)S(1)} %fusion.16), channel_id=1, source_target_pairs={{0,2},{1,3},{2,0},{3,1},{4,6},{5,7},{6,4},{7,5},{8,10},{9,11},{10,... | collective-permute-start | bytes 1179656 | tf_op jit(solution)/shard_map/ppermute | solution.py:636
  346.6 19.6 %collective-permute-start.43 = (bf16[2,2,112,512]{3,2,0,1:T(8,128)(2,1)S(1)}, bf16[2,2,112,512]{3,2,0,1:T(8,128)(2,1)S(1)}, u32[]{:S(2)}, u32[]{:S(2)}) collective-permute-start(bf16[2,2,112,512]{3,2,0,1:T(8,128)(2,1)S(1)} %fusion.9), channel_id=1, source_target_pairs={{0,4},{1,5},{2,6},{3,7},{4,0},{5,1},{6,2},{7,3},{8,12},{9,13},{10,... | collective-permute-start | bytes 1376264 | tf_op jit(solution)/shard_map/ppermute | solution.py:636
  347.5 18.0 %collective-permute-start.39 = (bf16[2,2,96,512]{3,2,0,1:T(8,128)(2,1)S(1)}, bf16[2,2,96,512]{3,2,0,1:T(8,128)(2,1)S(1)}, u32[]{:S(2)}, u32[]{:S(2)}) collective-permute-start(bf16[2,2,96,512]{3,2,0,1:T(8,128)(2,1)S(1)} %fusion.15), channel_id=1, source_target_pairs={{0,2},{1,3},{2,0},{3,1},{4,6},{5,7},{6,4},{7,5},{8,10},{9,11},{10,... | collective-permute-start | bytes 1179656 | tf_op jit(solution)/shard_map/ppermute | solution.py:636
  349.3 20.4 %collective-permute-start.40 = (bf16[2,2,112,512]{3,2,0,1:T(8,128)(2,1)S(1)}, bf16[2,2,112,512]{3,2,0,1:T(8,128)(2,1)S(1)}, u32[]{:S(2)}, u32[]{:S(2)}) collective-permute-start(bf16[2,2,112,512]{3,2,0,1:T(8,128)(2,1)S(1)} %fusion.8), channel_id=1, source_target_pairs={{0,4},{1,5},{2,6},{3,7},{4,0},{5,1},{6,2},{7,3},{8,12},{9,13},{10,... | collective-permute-start | bytes 1376264 | tf_op jit(solution)/shard_map/ppermute | solution.py:636
  365.6 10.1 %collective-permute-start.44 = (bf16[2,96,512]{2,1,0:T(8,128)(2,1)S(1)}, bf16[2,96,512]{2,1,0:T(8,128)(2,1)S(1)}, u32[]{:S(2)}, u32[]{:S(2)}) collective-permute-start(bf16[2,96,512]{2,1,0:T(8,128)(2,1)S(1)} %fusion.18), channel_id=1, source_target_pairs={{0,4},{1,5},{2,6},{3,7},{4,0},{5,1},{6,2},{7,3},{8,12},{9,13},{10,... | collective-permute-start | bytes 589832 | tf_op jit(solution)/shard_map/ppermute | solution.py:636
  366.3 12.0 %collective-permute-start.47 = (bf16[2,112,512]{2,1,0:T(8,128)(2,1)S(1)}, bf16[2,112,512]{2,1,0:T(8,128)(2,1)S(1)}, u32[]{:S(2)}, u32[]{:S(2)}) collective-permute-start(bf16[2,112,512]{2,1,0:T(8,128)(2,1)S(1)} %fusion.10), channel_id=1, source_target_pairs={{0,2},{1,3},{2,0},{3,1},{4,6},{5,7},{6,4},{7,5},{8,10},{9,11},{10,... | collective-permute-start | bytes 688136 | tf_op jit(solution)/shard_map/ppermute | solution.py:636
  367.0 9.9 %collective-permute-start.46 = (bf16[2,96,512]{2,1,0:T(8,128)(2,1)S(1)}, bf16[2,96,512]{2,1,0:T(8,128)(2,1)S(1)}, u32[]{:S(2)}, u32[]{:S(2)}) collective-permute-start(bf16[2,96,512]{2,1,0:T(8,128)(2,1)S(1)} %fusion.17), channel_id=1, source_target_pairs={{0,4},{1,5},{2,6},{3,7},{4,0},{5,1},{6,2},{7,3},{8,12},{9,13},{10,... | collective-permute-start | bytes 589832 | tf_op jit(solution)/shard_map/ppermute | solution.py:636
  369.8 8.5 %collective-permute-start.45 = (bf16[2,112,512]{2,1,0:T(8,128)(2,1)S(1)}, bf16[2,112,512]{2,1,0:T(8,128)(2,1)S(1)}, u32[]{:S(2)}, u32[]{:S(2)}) collective-permute-start(bf16[2,112,512]{2,1,0:T(8,128)(2,1)S(1)} %fusion.11), channel_id=1, source_target_pairs={{0,2},{1,3},{2,0},{3,1},{4,6},{5,7},{6,4},{7,5},{8,10},{9,11},{10,... | collective-permute-start | bytes 688136 | tf_op jit(solution)/shard_map/ppermute | solution.py:636
  373.7 9.1 %collective-permute-start.53 = (bf16[272,512]{1,0:T(8,128)(2,1)S(1)}, bf16[272,512]{1,0:T(8,128)(2,1)S(1)}, u32[]{:S(2)}, u32[]{:S(2)}) collective-permute-start(bf16[272,512]{1,0:T(8,128)(2,1)S(1)} %get-tuple-element.218), channel_id=1, source_target_pairs={{0,24},{1,25},{2,26},{3,27},{4,28},{5,29},{6,30},{7,31},{8,0},{9,1... | collective-permute-start | bytes 835592 | tf_op jit(solution)/shard_map/ppermute | solution.py:790
  375.7 35.0 %collective-permute-start.52 = (bf16[272,512]{1,0:T(8,128)(2,1)S(1)}, bf16[272,512]{1,0:T(8,128)(2,1)S(1)}, u32[]{:S(2)}, u32[]{:S(2)}) collective-permute-start(bf16[272,512]{1,0:T(8,128)(2,1)S(1)} %get-tuple-element.219), channel_id=1, source_target_pairs={{0,16},{1,17},{2,18},{3,19},{4,20},{5,21},{6,22},{7,23},{8,24},{9,... | collective-permute-start | bytes 835592 | tf_op jit(solution)/shard_map/ppermute | solution.py:790
  376.9 33.7 %collective-permute-start.51 = (bf16[272,512]{1,0:T(8,128)(2,1)S(1)}, bf16[272,512]{1,0:T(8,128)(2,1)S(1)}, u32[]{:S(2)}, u32[]{:S(2)}) collective-permute-start(bf16[272,512]{1,0:T(8,128)(2,1)S(1)} %get-tuple-element.217), channel_id=1, source_target_pairs={{0,8},{1,9},{2,10},{3,11},{4,12},{5,13},{6,14},{7,15},{8,16},{9,17... | collective-permute-start | bytes 835592 | tf_op jit(solution)/shard_map/ppermute | solution.py:790
  378.9 32.1 %collective-permute-start.50 = (bf16[208,512]{1,0:T(8,128)(2,1)S(1)}, bf16[208,512]{1,0:T(8,128)(2,1)S(1)}, u32[]{:S(2)}, u32[]{:S(2)}) collective-permute-start(bf16[208,512]{1,0:T(8,128)(2,1)S(1)} %get-tuple-element.221), channel_id=1, source_target_pairs={{0,24},{1,25},{2,26},{3,27},{4,28},{5,29},{6,30},{7,31},{8,0},{9,1... | collective-permute-start | bytes 638984 | tf_op jit(solution)/shard_map/ppermute | solution.py:790
  381.4 34.6 %collective-permute-start.49 = (bf16[208,512]{1,0:T(8,128)(2,1)S(1)}, bf16[208,512]{1,0:T(8,128)(2,1)S(1)}, u32[]{:S(2)}, u32[]{:S(2)}) collective-permute-start(bf16[208,512]{1,0:T(8,128)(2,1)S(1)} %get-tuple-element.222), channel_id=1, source_target_pairs={{0,16},{1,17},{2,18},{3,19},{4,20},{5,21},{6,22},{7,23},{8,24},{9,... | collective-permute-start | bytes 638984 | tf_op jit(solution)/shard_map/ppermute | solution.py:790
  382.9 33.1 %collective-permute-start.48 = (bf16[208,512]{1,0:T(8,128)(2,1)S(1)}, bf16[208,512]{1,0:T(8,128)(2,1)S(1)}, u32[]{:S(2)}, u32[]{:S(2)}) collective-permute-start(bf16[208,512]{1,0:T(8,128)(2,1)S(1)} %get-tuple-element.220), channel_id=1, source_target_pairs={{0,8},{1,9},{2,10},{3,11},{4,12},{5,13},{6,14},{7,15},{8,16},{9,17... | collective-permute-start | bytes 638984 | tf_op jit(solution)/shard_map/ppermute | solution.py:790
  (29 other events, 242.7 us)

commit v3 on v2

--- a/solution.py
+++ b/solution.py
@@ -133,6 +133,8 @@
 
         def emit(*done, tile=None):
             for ref in done:
+                if id(ref) not in place:
+                    continue
                 part = (lambda r: r) if tile is None else (lambda r: r.at[rows_of(tile)])
                 moves.send(part(ref), part(place[id(ref)]))
 
@@ -302,20 +304,6 @@
         v_ref[rows, :] = total
         low_ref[rows, :] = normed(total, gain, bias).astype(BF)
         emit(low_ref, v_ref, h_ref, gp_ref, tile=i)
-
-
-def ffn_fwd(at, base, a, res, w, vecs):
-    t = a.shape[0]
-    return call(
-        functools.partial(ffn_fwd_body, at),
-        (),
-        (a, res, part_of(w, base, 2 * FF), vecs),
-        [((t, FF), BF), ((t, FF), BF), ((t, D), F32), ((t, D), BF), ((4, D, D), BF)],
-        [],
-        [],
-        12,
-        tiled=2,
-    )
 
 
 def ffn_bwd_body(at, before, plan, base, seal, count, moves, emit, words, ins, raw_in, outs, raw, own):
@@ -477,18 +465,39 @@
         emit(out_ref, low_ref, pre_ref, tile=i)
 
 
-def attn_fwd(kind, at, base, lq, lk, xq, xk, w, vecs):
-    t = xq.shape[0]
+def forward_body(kinds, moves, emit, words, ins, raw_in, outs, raw, own):
+    *inputs, vec_ref = ins
+    segk_ref, *mids = own
+    at = 0
+    x_ref = res_ref = inputs.pop(0)
+    for i, kind in enumerate(kinds):
+        lengths = (words[0], words[-1]) if kind == "cross" else (words[0], words[0])
+        sources = (x_ref, inputs.pop(0)) if kind == "cross" else (x_ref,)
+        low_outs = outs[7 * i : 7 * i + 7]
+        attn_fwd_body(
+            kind, at, moves, emit, lengths, (*sources, inputs.pop(0), vec_ref), raw_in,
+            (*low_outs[:5], mids[i], *low_outs[5:]), raw, (segk_ref,)
+        )
+        x_ref = mids[i]
+        at += 2
+    ffn_fwd_body(at, moves, emit, words, (x_ref, res_ref, inputs.pop(0), vec_ref), raw_in, outs[7 * len(kinds) :], raw, ())
+
+
+def forward(kinds, lengths, x, other, w, vecs):
+    t = x.shape[0]
     low, full = ((t, D), BF), ((t, D), F32)
+    ins = [x]
+    for i, kind in enumerate(kinds):
+        ins += ([other] if kind == "cross" else []) + [part_of(w, i * FF, FF)]
     return call(
-        functools.partial(attn_fwd_body, kind, at),
-        (lq, lk),
-        ((xq, xk) if kind == "cross" else (xq,)) + (part_of(w, base, 4 * D), vecs),
-        [low, low, low, low, full, full, low, ((8, t), F32)],
+        functools.partial(forward_body, kinds),
+        lengths,
+        (*ins, part_of(w, len(kinds) * FF, 2 * FF), vecs),
+        [low, low, low, low, full, low, ((8, t), F32)] * len(kinds)
+        + [((t, FF), BF), ((t, FF), BF), full, low, ((4, D, D), BF)],
         [],
-        [pltpu.VMEM((8, t), jnp.int32)],
-        12,
-        tiled=2 if kind == "cross" else 1,
+        [pltpu.VMEM((8, t), jnp.int32)] + [pltpu.VMEM(*full)] * len(kinds),
+        30,
     )
 
 
@@ -763,19 +772,16 @@
 
 
 def first_ways(terms, aways=None):
-    half = terms[0].shape[-2] // 32 * 16
-    return (
-        halve([t[..., :half, :] for t in terms], "x", 2, aways),
-        halve([t[..., half:, :] for t in terms], "y", 1, aways),
-    )
+    half = terms[0].shape[0] // 2
+    return halve([t[:half] for t in terms], "x", 2, aways), halve([t[half:] for t in terms], "y", 1, aways)
 
 
 def second_ways(ways):
     one, two = halve(ways[0], "y", 1), halve(ways[1], "x", 1)
-    return [jnp.concatenate([a, b], axis=1) for a, b in zip(one, two)]
-
-
-def send_line(planes, base):
+    return [jnp.concatenate([a, b]) for a, b in zip(one, two)]
+
+
+def send_line(planes, base, aways=None):
     count = planes[0].shape[0]
     z = place_of("z")
     sums = total_of(planes).astype(BF)
@@ -787,6 +793,8 @@
             if base <= goal < base + count:
                 pairs.append((device, goal * 8 + device % 8))
         away = pick(sums, jnp.clip((z + step) % 4 - base, 0, count - 1), 0)
+        if aways is not None:
+            aways.append(away)
         pieces.append(lax.ppermute(away, "fsdp", pairs))
     return pieces
 
@@ -830,18 +838,13 @@
     else:
         e_all, ev = gather_plain(e_own, 4, n)
         d_all, dv = gather_plain(d_own, 6, n)
-    q1, k1, v1, o1, pre1, ax, axl, lse1 = attn_fwd("full", 0, 0, ls, ls, src, src, e_all, ev)
-    if split:
-        low, high = after(low, axl), after(high, axl)
-        low, high = widen(low, "core"), widen(high, "core")
-        ax = hold(ax, *(p for p, _ in low[:2]), *(p for p, _ in high[:2]))
-    hx, gpx, sum2, enc, wup_e = ffn_fwd(2, FF, ax, src, e_all, ev)
+    q1, k1, v1, o1, pre1, axl, lse1, hx, gpx, sum2, enc, wup_e = forward(("full",), (ls,), src, None, e_all, ev)
     if split:
         low, high = after(low, enc), after(high, enc)
-        d_all, dv = assemble([(0, 144, low), (144, 272, high)], n, 256, 6, 1)
-    q3, k3, v3, o3, pre3, h1, h1l, lse3 = attn_fwd("causal", 0, 0, lt, lt, tgt, tgt, d_all, dv)
-    q4, k4, v4, o4, pre4, h2, h2l, lse4 = attn_fwd("cross", 2, FF, lt, ls, h1, enc, d_all, dv)
-    hy, gpy, sum5, final, wup_d = ffn_fwd(4, 2 * FF, h2, tgt, d_all, dv)
+        d_all, dv = assemble([(0, 144, widen(low, "core")), (144, 272, widen(high, "core"))], n, 256, 6, 1)
+    q3, k3, v3, o3, pre3, h1l, lse3, q4, k4, v4, o4, pre4, h2l, lse4, hy, gpy, sum5, final, wup_d = forward(
+        ("causal", "cross"), (lt, ls), tgt, enc, d_all, dv
+    )
     if split:
         d_plan = [("owned", 256, ((16, 16),)), ("owned", 256, ((8, 8),)), ("owned", 256, ((0, 8),))]
         e_plan = [("owned", 192, ((16, 16), (10, 6))), ("owned", 192, ((0, 16),))]
@@ -851,40 +854,45 @@
     g3, first3, dgb, ds5, ds4 = ffn_bwd(4, 2, d_plan[0], 2 * FF, cotangent, sum5, hy, gpy, h2l, pre4, wup_d, d_all, dv)
     if split:
         p23 = begin_plane(*g3)
-        p23 = halve(p23, "x", 2)
-        ds4 = hold(ds4, *p23[:-1])
+        aways = []
+        p23 = halve(p23, "x", 2, aways)
+        ds4 = hold(ds4, *aways)
     g2, first2, dgb, ds3, denc = attn_bwd(
         "cross", 0, d_plan[1], FF, lt, ls, ds4, q4, k4, v4, o4, lse4, h1l, enc, d_all, dv, pre3, dgb, first3
     )
     if split:
         p23[-1], ds3, *g2 = lax.optimization_barrier((p23[-1], ds3, *g2))
         p1 = begin_plane(*g2)
-        p23, p1 = halve(p23, "y", 1), halve(p1, "y", 1)
-        ds3 = hold(ds3, *p23[:-1], *p1[:-1])
+        aways = []
+        p23, p1 = halve(p23, "y", 1, aways), halve(p1, "y", 1, aways)
+        ds3 = hold(ds3, *aways)
     g1, _, tgt_grad = attn_bwd(
         "causal", 0, d_plan[2], 0, lt, lt, ds3, q3, k3, v3, o3, lse3, tgt, tgt, d_all, dv, ds5, dgb, first2
     )
     if split:
         p23[-1], p1[-1], denc, *g1 = lax.optimization_barrier((p23[-1], p1[-1], denc, *g1, tgt_grad))[:5]
         p0 = begin_plane(*g1)
-        p1, p0 = halve(p1, "x", 1), halve(p0, "x", 2)
-        denc = hold(denc, *p1[:-1], *p0[:-1])
+        aways = []
+        p1, p0 = halve(p1, "x", 1, aways), halve(p0, "x", 2, aways)
+        denc = hold(denc, *aways)
     seal = 3 * FF if split else None
     f, first, egb, ds2, ds1 = ffn_bwd(2, 0, e_plan[0], FF, denc, sum2, hx, gpx, axl, pre1, wup_e, e_all, ev, dgb, seal=seal)
     if split:
         p1[-1], p0[-1], ds1, *f = lax.optimization_barrier((p1[-1], p0[-1], ds1, *f))
         e23 = begin_plane(*f[:2])
-        p0, e23 = halve(p0, "y", 1), first_ways(e23)
-        ds1 = hold(ds1, *p0[:-1])
+        p0 = halve(p0, "y", 1)
+        aways = []
+        e23 = first_ways(e23, aways)
+        d_planes = [jnp.concatenate(t) for t in zip(p0, p1, p23)]
+        dz = send_line(d_planes, 0, aways)
+        ds1 = hold(ds1, *aways)
     a, _, src_grad = attn_bwd(
         "full", 0, e_plan[1], 0, ls, ls, ds1, q1, k1, v1, o1, lse1, src, src, e_all, ev, ds2, egb, first, f[2:]
     )
     if split:
         aways = []
         e01 = first_ways(begin_plane(*a), aways)
-        p0[-1], e23[0][-1], e23[1][-1] = lax.optimization_barrier((p0[-1], e23[0][-1], e23[1][-1], *aways))[:3]
-        d_planes = [jnp.concatenate(t) for t in zip(p0, p1, p23)]
-        dz = send_line(d_planes, 0)
+        e23[0][-1], e23[1][-1], *dz = lax.optimization_barrier((e23[0][-1], e23[1][-1], *dz, *aways))[:5]
         e_planes = [jnp.concatenate(t) for t in zip(second_ways(e01), second_ways(e23))]
         ez = send_line(e_planes, 0)
         d_sum = end_line(d_planes, dz, 0)

time: 425 us -> 407 us (0.958)
  the two profiles are of different devices: /device:TPU:0 before, /device:TPU:9 now
where the time goes in v3:
time: 407 us; the launch traced here: 400 us
  Pallas kernels  200 us (49%)
  waiting for transfers between devices  104 us (26%)
  starting transfers between devices  51.7 us (13%)
  local copies, waits for them, and re-layouts  28 us (7%)
  other arithmetic  14.9 us (4%)
    pallas_call x7, Pallas kernels, call(): pl.pallas_call(kernel, out_shape=tuple((jax.ShapeDtypeStruct(s, d) for s,...  187 us
    ppermute x48, waiting for transfers between devices, shifted(): return lax.ppermute(block, 'fsdp', pairs)  67.5 us
    ppermute x48, starting transfers between devices, shifted(): return lax.ppermute(block, 'fsdp', pairs)  44.3 us
    ppermute x6, waiting for transfers between devices, send_line(): pieces.append(lax.ppermute(away, 'fsdp', pairs))  36 us
    pallas_call x2, Pallas kernels, assemble(): pl.pallas_call(functools.partial(assemble_body, spans, labels, rows, vect...  12.9 us
    unnamed x127, local copies, waits for them, and re-layouts  12.1 us
    convert_element_type x14, other arithmetic, halve(): away = total_of([pick(t, 1 - at, axis) for t in terms]).astype(BF)  11.2 us
  transfers between devices with their start and end apart: 54, of which 24 were waited for; matrix products, arithmetic and copies ran while one was open for 6% of the time, Pallas kernels for 27%

profile of v3, /device:TPU:9, one launch (start us, length us, event | category | flops | bytes accessed | tf_op | source)
XLA Modules:
  0.0 400.4 jit_solution(3393610415946463683)
XLA Ops:
  0.6 1.1 pad_dynamic-slice_fusion.2
  1.9 1.3 collective-permute-start.11
  4.3 1.4 collective-permute-start.13
  6.7 1.3 collective-permute-start
  8.5 1.7 collective-permute-done
  10.3 3.1 collective-permute-start.2
  13.4 2.3 collective-permute-done.12
  15.8 7.9 %collective-permute-done.13 = bf16[1,144,512]{2,1,0:T(8,128)(2,1)S(1)} collective-permute-done((bf16[1,144,512]{2,1,0:T(8,128)(2,1)S(1)}, bf16[1,144,512]{2,1,0:T(8,128)(2,1)S(1)}, u32[]{:S(2)}, u32[]{:S(2)}) %collective-permute-start.13) | collective-permute-done | bytes 147488 | tf_op jit(solution)/shard_map/ppermute | solution.py:645
  23.7 1.3 collective-permute-start.18
  25.1 1.3 collective-permute-start.14
  26.5 2.8 collective-permute-done.3
  29.7 2.7 collective-permute-done.18
  32.5 1.3 collective-permute-start.19
  34.2 1.3 collective-permute-start.15
  35.5 1.5 collective-permute-done.4
  37.0 2.3 collective-permute-start.16
  39.3 7.8 %collective-permute-done.5 = bf16[1,272,512]{2,1,0:T(8,128)(2,1)S(1)} collective-permute-done((bf16[1,272,512]{2,1,0:T(8,128)(2,1)S(1)}, bf16[1,272,512]{2,1,0:T(8,128)(2,1)S(1)}, u32[]{:S(2)}, u32[]{:S(2)}) %collective-permute-start.5) | collective-permute-done | bytes 278560 | tf_op jit(solution)/shard_map/ppermute | solution.py:645
  47.1 2.9 collective-permute-start.6
  50.0 5.5 %collective-permute-done.6 = bf16[1,272,512]{2,1,0:T(8,128)(2,1)S(1)} collective-permute-done((bf16[1,272,512]{2,1,0:T(8,128)(2,1)S(1)}, bf16[1,272,512]{2,1,0:T(8,128)(2,1)S(1)}, u32[]{:S(2)}, u32[]{:S(2)}) %collective-permute-start.6) | collective-permute-done | bytes 278560 | tf_op jit(solution)/shard_map/ppermute | solution.py:645
  55.5 1.3 collective-permute-start.20
  56.9 1.7 collective-permute-done.8.refs_1_
  58.6 2.4 collective-permute-start.10
  62.7 1.3 collective-permute-start.25
  64.0 1.2 collective-permute-start.7
  67.6 5.7 %shard_map.110 = (bf16[32,192,512]{2,1,0:T(8,128)(2,1)}, f32[16,512]{1,0:T(8,128)}) custom-call(bf16[8,64,512]{2,1,0:T(8,128)(2,1)} %copy-done.43, bf16[8,64,512]{2,1,0:T(8,128)(2,1)} %copy-done.51, bf16[8,64,512]{2,1,0:T(8,128)(2,1)} %copy-done.55, bf16[8,64,512]{2,1,0:T(8,128)(2,1)} %copy-done.54, bf16[8,64,512]{2,1,0:T(8,128)(2,1)} %copy-done.42, ...), custom_call_target="tpu_custom_call" | custom-call | flops 80000000000 | bytes 1048576 | tf_op jit(solution)/shard_map/pallas_call | solution.py:710
  73.4 2.7 collective-permute-done.25
  77.8 1.2 collective-permute-start.26
  80.7 1.2 collective-permute-start.22
  81.9 28.3 %shard_map.111 = (bf16[1024,512]{1,0:T(8,128)(2,1)}, bf16[1024,512]{1,0:T(8,128)(2,1)}, bf16[1024,512]{1,0:T(8,128)(2,1)}, bf16[1024,512]{1,0:T(8,128)(2,1)}, f3...) custom-call(s32[1,16]{1,0:T(1,128)} %refs_1_.9, ...), custom_call_target="tpu_custom_call" | custom-call | flops 299999985664 | bytes 1048576 | tf_op jit(solution)/shard_map/pallas_call | solution.py:148
  110.3 1.6 collective-permute-start.23
  112.5 5.3 %collective-permute-done.27.refs_6_ = bf16[8,128,512]{2,1,0:T(8,128)(2,1)S(1)} collective-permute-done((bf16[8,128,512]{2,1,0:T(8,128)(2,1)}, bf16[8,128,512]{2,1,0:T(8,128)(2,1)S(1)}, u32[]{:S(2)}, u32[]{:S(2)}) %collective-permute-start.27) | collective-permute-done | bytes 1048608 | tf_op jit(solution)/shard_map/ppermute | solution.py:645
  117.8 1.5 collective-permute-done.28.refs_7_
  121.6 7.2 %shard_map.112 = (bf16[32,272,512]{2,1,0:T(8,128)(2,1)}, f32[16,512]{1,0:T(8,128)}) custom-call(bf16[8,144,512]{2,1,0:T(8,128)(2,1)} %constant_dynamic-update-slice_fusion.17.refs_0_, bf16[8,144,512]{2,1,0:T(8,128)(2,1)} %collective-permute-done.22.refs_1_, bf16[8,144,512]{2,1,0:T(8,128)(2,1)} %copy-done.44, bf16[8,144,512]{2,1,0:T(8,128)(2,1)} %copy-done.45, ...), custom_call_target="tpu_custom_call" | custom-call | flops 80000000000 | bytes 1048576 | tf_op jit(solution)/shard_map/pallas_call | solution.py:710
  128.8 37.4 %shard_map.113 = (bf16[1024,512]{1,0:T(8,128)(2,1)}, bf16[1024,512]{1,0:T(8,128)(2,1)}, bf16[1024,512]{1,0:T(8,128)(2,1)}, bf16[1024,512]{1,0:T(8,128)(2,1)}, f3...) custom-call(s32[1,16]{1,0:T(1,128)} %refs_1_.8, ...), custom_call_target="tpu_custom_call" | custom-call | flops 299999985664 | bytes 1048576 | tf_op jit(solution)/shard_map/pallas_call | solution.py:148
  166.3 21.6 %shard_map.114 = (bf16[8,272,512]{2,1,0:T(8,128)(2,1)}, bf16[8,272,512]{2,1,0:T(8,128)(2,1)}, bf16[16,512]{1,0:T(8,128)(2,1)}, f32[16,512]{1,0:T(8,128)}, f32[1024,512]{1,0:T(8,128)}, /*index=5*/f32[1024,512]{1,0:T(8,128)}) custom-call(bf16[1024,512]{1,0:T(8,128)(2,1)} %refs_0_.8, f32[1024,512]{1,0:T(8,128)} %get-tuple-element.119.refs_1_, ...), custom_call_target="tpu_custom_call" | custom-call | flops 130000003072 | bytes 1048576 | tf_op jit(solution)/shard_map/pallas_call | solution.py:148
  188.3 4.2 %collective-permute-done.29 = bf16[8,272,512]{2,1,0:T(8,128)(2,1)S(1)} collective-permute-done((bf16[8,272,512]{2,1,0:T(8,128)(2,1)}, bf16[8,272,512]{2,1,0:T(8,128)(2,1)S(1)}, u32[]{:S(2)}, u32[]{:S(2)}) %collective-permute-start.29) | collective-permute-done | bytes 2228256 | tf_op jit(solution)/shard_map/ppermute | solution.py:645
  192.5 3.4 fusion
  195.9 1.4 collective-permute-start.30
  197.3 27.9 %shard_map.115 = (bf16[4,272,512]{2,1,0:T(8,128)(2,1)}, bf16[4,272,512]{2,1,0:T(8,128)(2,1)}, bf16[16,512]{1,0:T(8,128)(2,1)}, f32[16,512]{1,0:T(8,128)}, f32[1024,512]{1,0:T(8,128)}, /*index=5*/f32[1024,512]{1,0:T(8,128)}) custom-call(s32[1,16]{1,0:T(1,128)} %refs_1_.8, s32[1,16]{1,0:T(1,128)} %refs_1_.9, f32[1024,512]{1,0:T(8,128)} %get-tuple-element.128.refs_2_, ...), custom_call_target="tpu_custom_call" | custom-call | flops 260000006144 | bytes 1048576 | tf_op jit(solution)/shard_map/pallas_call | solution.py:148
  225.7 2.5 fusion.1
  228.9 1.1 fusion.2
  230.8 24.7 %shard_map.116 = (bf16[4,272,512]{2,1,0:T(8,128)(2,1)}, bf16[4,272,512]{2,1,0:T(8,128)(2,1)}, bf16[16,512]{1,0:T(8,128)(2,1)}, f32[1024,512]{1,0:T(8,128)}) custom-call(s32[1,16]{1,0:T(1,128)} %refs_1_.8, s32[1,16]{1,0:T(1,128)} %refs_1_.8, f32[1024,512]{1,0:T(8,128)} %get-tuple-element.146.refs_2_, bf16[1024,512]{1,0:T(8,128)(2,1)} %get-tuple-element.147.refs_3_, ...), custom_call_target="tpu_custom_call" | custom-call | flops 260000006144 | bytes 1048576 | tf_op jit(solution)/shard_map/pallas_call | solution.py:148
  256.3 1.2 dynamic-slice_bitcast_fusion.2
  257.5 1.3 dynamic-slice_bitcast_fusion.1
  258.9 1.4 dynamic-slice_bitcast_fusion
  260.6 1.4 fusion.5
  262.5 1.2 collective-permute-start.36
  263.7 21.5 %shard_map.117 = (bf16[8,208,512]{2,1,0:T(8,128)(2,1)}, bf16[8,208,512]{2,1,0:T(8,128)(2,1)}, bf16[3,208,512]{2,1,0:T(8,128)(2,1)}, bf16[3,208,512]{2,1,0:T(8,12...) custom-call(f32[1024,512]{1,0:T(8,128)} %get-tuple-element.162.refs_0_, ...), custom_call_target="tpu_custom_call" | custom-call | flops 130000003072 | bytes 1048576 | tf_op jit(solution)/shard_map/pallas_call | solution.py:148
  288.9 6.7 %collective-permute-done.38 = bf16[1,272,512]{2,1,0:T(8,128)(2,1)S(1)} collective-permute-done((bf16[1,272,512]{2,1,0:T(8,128)(2,1)S(1)}, bf16[1,272,512]{2,1,0:T(8,128)(2,1)S(1)}, u32[]{:S(2)}, u32[]{:S(2)}) %collective-permute-start.38) | collective-permute-done | bytes 278560 | tf_op jit(solution)/shard_map/ppermute | solution.py:645
  300.9 25.8 %shard_map.118 = (bf16[8,208,512]{2,1,0:T(8,128)(2,1)}, bf16[8,208,512]{2,1,0:T(8,128)(2,1)}, bf16[16,512]{1,0:T(8,128)(2,1)}, f32[1024,512]{1,0:T(8,128)}) custom-call(s32[1,16]{1,0:T(1,128)} %refs_1_.9, s32[1,16]{1,0:T(1,128)} %refs_1_.9, f32[1024,512]{1,0:T(8,128)} %get-tuple-element.180.refs_2_, bf16[1024,512]{1,0:T(8,128)(2,1)} %get-tuple-element.181.refs_3_, ...), custom_call_target="tpu_custom_call" | custom-call | flops 260000006144 | bytes 1048576 | tf_op jit(solution)/shard_map/pallas_call | solution.py:148
  330.3 1.2 collective-permute-start.45
  331.6 1.5 collective-permute-start.46
  335.5 1.5 fusion.19
  337.2 1.3 collective-permute-done.44
  339.2 15.2 %collective-permute-done.45 = bf16[272,512]{1,0:T(8,128)(2,1)S(1)} collective-permute-done((bf16[272,512]{1,0:T(8,128)(2,1)S(1)}, bf16[272,512]{1,0:T(8,128)(2,1)S(1)}, u32[]{:S(2)}, u32[]{:S(2)}) %collective-permute-start.45) | collective-permute-done | bytes 278560 | tf_op jit(solution)/shard_map/ppermute | solution.py:798
  354.8 1.8 collective-permute-done.46
  356.6 1.2 fusion.7
  360.3 4.9 %collective-permute-done.40 = bf16[1,2,208,512]{3,2,1,0:T(8,128)(2,1)S(1)} collective-permute-done((bf16[1,2,208,512]{3,2,1,0:T(8,128)(2,1)S(1)}, bf16[1,2,208,512]{3,2,1,0:T(8,128)(2,1)S(1)}, u32[]{:S(2)}, u32[]{:S(2)}) %collective-permute-start.40) | collective-permute-done | bytes 426016 | tf_op jit(solution)/shard_map/ppermute | solution.py:645
  366.1 4.3 %collective-permute-done.47 = bf16[1,208,512]{2,1,0:T(8,128)(2,1)S(1)} collective-permute-done((bf16[1,208,512]{2,1,0:T(8,128)(2,1)S(1)}, bf16[1,208,512]{2,1,0:T(8,128)(2,1)S(1)}, u32[]{:S(2)}, u32[]{:S(2)}) %collective-permute-start.47) | collective-permute-done | bytes 213024 | tf_op jit(solution)/shard_map/ppermute | solution.py:645
  370.4 4.0 collective-permute-done.48
  375.2 3.2 collective-permute-start.52
  378.3 1.4 collective-permute-start.53
  380.4 12.2 %collective-permute-done.52 = bf16[208,512]{1,0:T(8,128)(2,1)S(1)} collective-permute-done((bf16[208,512]{1,0:T(8,128)(2,1)S(1)}, bf16[208,512]{1,0:T(8,128)(2,1)S(1)}, u32[]{:S(2)}, u32[]{:S(2)}) %collective-permute-start.52) | collective-permute-done | bytes 213024 | tf_op jit(solution)/shard_map/ppermute | solution.py:798
  392.6 5.1 %collective-permute-done.53 = bf16[208,512]{1,0:T(8,128)(2,1)S(1)} collective-permute-done((bf16[208,512]{1,0:T(8,128)(2,1)S(1)}, bf16[208,512]{1,0:T(8,128)(2,1)S(1)}, u32[]{:S(2)}, u32[]{:S(2)}) %collective-permute-start.53) | collective-permute-done | bytes 213024 | tf_op jit(solution)/shard_map/ppermute | solution.py:798
  (265 shorter events, 41.4 us)
Async XLA Ops:
  1.9 11.5 %collective-permute-start.11 = (bf16[1,144,512]{2,1,0:T(8,128)(2,1)S(1)}, bf16[1,144,512]{2,1,0:T(8,128)(2,1)S(1)}, u32[]{:S(2)}, u32[]{:S(2)}) collective-permute-start(bf16[1,144,512]{2,1,0:T(8,128)(2,1)S(1)} %broadcast_in_dim.7), channel_id=1, source_target_pairs={{0,8},{1,9},{2,10},{3,11},{4,12},{5,13},{6,14},{7,15},{8,16},{9,17... | collective-permute-start | bytes 442376 | tf_op jit(solution)/shard_map/ppermute | solution.py:645
  3.2 12.5 %collective-permute-start.12 = (bf16[1,144,512]{2,1,0:T(8,128)(2,1)S(1)}, bf16[1,144,512]{2,1,0:T(8,128)(2,1)S(1)}, u32[]{:S(2)}, u32[]{:S(2)}) collective-permute-start(bf16[1,144,512]{2,1,0:T(8,128)(2,1)S(1)} %broadcast_in_dim.7), channel_id=1, source_target_pairs={{0,16},{1,17},{2,18},{3,19},{4,20},{5,21},{6,22},{7,23},{8,24},{9,... | collective-permute-start | bytes 442376 | tf_op jit(solution)/shard_map/ppermute | solution.py:645
  4.3 19.3 %collective-permute-start.13 = (bf16[1,144,512]{2,1,0:T(8,128)(2,1)S(1)}, bf16[1,144,512]{2,1,0:T(8,128)(2,1)S(1)}, u32[]{:S(2)}, u32[]{:S(2)}) collective-permute-start(bf16[1,144,512]{2,1,0:T(8,128)(2,1)S(1)} %broadcast_in_dim.7), channel_id=1, source_target_pairs={{0,24},{1,25},{2,26},{3,27},{4,28},{5,29},{6,30},{7,31},{8,0},{9,1... | collective-permute-start | bytes 442376 | tf_op jit(solution)/shard_map/ppermute | solution.py:645
  6.7 3.5 collective-permute-start
  10.2 16.2 %collective-permute-start.1 = (bf16[2,64,512]{2,1,0:T(8,128)(2,1)S(1)}, bf16[2,64,512]{2,1,0:T(8,128)(2,1)S(1)}, u32[]{:S(2)}, u32[]{:S(2)}) collective-permute-start(bf16[2,64,512]{2,1,0:T(8,128)(2,1)S(1)} %get-tuple-element.230), channel_id=1, source_target_pairs={{0,8},{1,9},{2,10},{3,11},{4,12},{5,13},{6,14},{7,15},{8,16},{9,17... | collective-permute-start | bytes 393224 | tf_op jit(solution)/shard_map/ppermute | solution.py:645
  10.3 16.2 %collective-permute-start.2 = (bf16[2,64,512]{2,1,0:T(8,128)(2,1)S(1)}, bf16[2,64,512]{2,1,0:T(8,128)(2,1)S(1)}, u32[]{:S(2)}, u32[]{:S(2)}) collective-permute-start(bf16[2,64,512]{2,1,0:T(8,128)(2,1)S(1)} %get-tuple-element.230), channel_id=1, source_target_pairs={{0,16},{1,17},{2,18},{3,19},{4,20},{5,21},{6,22},{7,23},{8,24},{9,... | collective-permute-start | bytes 393224 | tf_op jit(solution)/shard_map/ppermute | solution.py:645
  13.4 15.8 %collective-permute-start.3 = (bf16[2,64,512]{2,1,0:T(8,128)(2,1)S(1)}, bf16[2,64,512]{2,1,0:T(8,128)(2,1)S(1)}, u32[]{:S(2)}, u32[]{:S(2)}) collective-permute-start(bf16[2,64,512]{2,1,0:T(8,128)(2,1)S(1)} %get-tuple-element.230), channel_id=1, source_target_pairs={{0,24},{1,25},{2,26},{3,27},{4,28},{5,29},{6,30},{7,31},{8,0},{9,1... | collective-permute-start | bytes 393224 | tf_op jit(solution)/shard_map/ppermute | solution.py:645
  23.7 8.7 %collective-permute-start.18 = (bf16[4,80,512]{2,1,0:T(8,128)(2,1)S(1)}, bf16[4,80,512]{2,1,0:T(8,128)(2,1)S(1)}, u32[]{:S(2)}, u32[]{:S(2)}) collective-permute-start(bf16[4,80,512]{2,1,0:T(8,128)(2,1)S(1)} %pad_maximum_fusion.8), channel_id=1, source_target_pairs={{0,4},{1,5},{2,6},{3,7},{4,0},{5,1},{6,2},{7,3},{8,12},{9,13},{10,... | collective-permute-start | bytes 983048 | tf_op jit(solution)/shard_map/ppermute | solution.py:645
  25.1 9.0 %collective-permute-start.14 = (bf16[4,64,512]{2,1,0:T(8,128)(2,1)S(1)}, bf16[4,64,512]{2,1,0:T(8,128)(2,1)S(1)}, u32[]{:S(2)}, u32[]{:S(2)}) collective-permute-start(bf16[4,64,512]{2,1,0:T(8,128)(2,1)S(1)} %pad_maximum_fusion.9), channel_id=1, source_target_pairs={{0,2},{1,3},{2,0},{3,1},{4,6},{5,7},{6,4},{7,5},{8,10},{9,11},{10,... | collective-permute-start | bytes 786440 | tf_op jit(solution)/shard_map/ppermute | solution.py:645
  29.3 7.7 %collective-permute-start.4 = (bf16[1,272,512]{2,1,0:T(8,128)(2,1)S(1)}, bf16[1,272,512]{2,1,0:T(8,128)(2,1)S(1)}, u32[]{:S(2)}, u32[]{:S(2)}) collective-permute-start(bf16[1,272,512]{2,1,0:T(8,128)(2,1)S(1)} %broadcast_in_dim_reshape.3), channel_id=1, source_target_pairs={{0,8},{1,9},{2,10},{3,11},{4,12},{5,13},{6,14},{7,15},{8,16},{9,17... | collective-permute-start | bytes 835592 | tf_op jit(solution)/shard_map/ppermute | solution.py:645
  29.3 17.8 %collective-permute-start.5 = (bf16[1,272,512]{2,1,0:T(8,128)(2,1)S(1)}, bf16[1,272,512]{2,1,0:T(8,128)(2,1)S(1)}, u32[]{:S(2)}, u32[]{:S(2)}) collective-permute-start(bf16[1,272,512]{2,1,0:T(8,128)(2,1)S(1)} %broadcast_in_dim_reshape.3), channel_id=1, source_target_pairs={{0,16},{1,17},{2,18},{3,19},{4,20},{5,21},{6,22},{7,23},{8,24},{9,... | collective-permute-start | bytes 835592 | tf_op jit(solution)/shard_map/ppermute | solution.py:645
  32.5 29.9 %copy-start.41 = (bf16[8,80,512]{2,1,0:T(8,128)(2,1)}, bf16[8,80,512]{2,1,0:T(8,128)(2,1)S(1)}, u32[]{:S(2)}) copy-start(bf16[8,80,512]{2,1,0:T(8,128)(2,1)S(1)} %constant_dynamic-update-slice_fusion.12.refs_8_) | copy-start | bytes 1966084
  32.5 24.3 %collective-permute-start.19 = (bf16[8,80,512]{2,1,0:T(8,128)(2,1)S(1)}, bf16[8,80,512]{2,1,0:T(8,128)(2,1)S(1)}, u32[]{:S(2)}, u32[]{:S(2)}) collective-permute-start(bf16[8,80,512]{2,1,0:T(8,128)(2,1)S(1)} %constant_dynamic-update-slice_fusion.12.refs_8_), channel_id=1, source_target_pairs={{0,2},{1,3},{2,0},{3,1},{4,6},{5,7},{6,4},{7,5},{8,10},{9,11},{10,... | collective-permute-start | bytes 1966088 | tf_op jit(solution)/shard_map/ppermute | solution.py:645
  33.8 28.6 %copy-start.43 = (bf16[8,64,512]{2,1,0:T(8,128)(2,1)}, bf16[8,64,512]{2,1,0:T(8,128)(2,1)S(1)}, u32[]{:S(2)}) copy-start(bf16[8,64,512]{2,1,0:T(8,128)(2,1)S(1)} %constant_dynamic-update-slice_fusion.2.refs_0_) | copy-start | bytes 1572868
  33.8 24.7 %collective-permute-start.8 = (bf16[8,64,512]{2,1,0:T(8,128)(2,1)S(1)}, bf16[8,64,512]{2,1,0:T(8,128)(2,1)S(1)}, u32[]{:S(2)}, u32[]{:S(2)}) collective-permute-start(bf16[8,64,512]{2,1,0:T(8,128)(2,1)S(1)} %constant_dynamic-update-slice_fusion.2.refs_0_), channel_id=1, source_target_pairs={{0,2},{1,3},{2,0},{3,1},{4,6},{5,7},{6,4},{7,5},{8,10},{9,11},{10,... | collective-permute-start | bytes 1572872 | tf_op jit(solution)/shard_map/ppermute | solution.py:645
  34.2 28.3 %copy-start.42 = (bf16[8,64,512]{2,1,0:T(8,128)(2,1)}, bf16[8,64,512]{2,1,0:T(8,128)(2,1)S(1)}, u32[]{:S(2)}) copy-start(bf16[8,64,512]{2,1,0:T(8,128)(2,1)S(1)} %constant_dynamic-update-slice_fusion.7.refs_4_) | copy-start | bytes 1572868
  34.2 26.8 %collective-permute-start.15 = (bf16[8,64,512]{2,1,0:T(8,128)(2,1)S(1)}, bf16[8,64,512]{2,1,0:T(8,128)(2,1)S(1)}, u32[]{:S(2)}, u32[]{:S(2)}) collective-permute-start(bf16[8,64,512]{2,1,0:T(8,128)(2,1)S(1)} %constant_dynamic-update-slice_fusion.7.refs_4_), channel_id=1, source_target_pairs={{0,4},{1,5},{2,6},{3,7},{4,0},{5,1},{6,2},{7,3},{8,12},{9,13},{10,... | collective-permute-start | bytes 1572872 | tf_op jit(solution)/shard_map/ppermute | solution.py:645
  37.0 24.0 %collective-permute-start.16 = (bf16[8,64,512]{2,1,0:T(8,128)(2,1)S(1)}, bf16[8,64,512]{2,1,0:T(8,128)(2,1)S(1)}, u32[]{:S(2)}, u32[]{:S(2)}) collective-permute-start(bf16[8,64,512]{2,1,0:T(8,128)(2,1)S(1)} %constant_dynamic-update-slice_fusion.7.refs_4_), channel_id=1, source_target_pairs={{0,1},{1,0},{2,3},{3,2},{4,5},{5,4},{6,7},{7,6},{8,9},{9,8},{10,11... | collective-permute-start | bytes 1572872 | tf_op jit(solution)/shard_map/ppermute | solution.py:645
  47.1 8.4 %collective-permute-start.6 = (bf16[1,272,512]{2,1,0:T(8,128)(2,1)S(1)}, bf16[1,272,512]{2,1,0:T(8,128)(2,1)S(1)}, u32[]{:S(2)}, u32[]{:S(2)}) collective-permute-start(bf16[1,272,512]{2,1,0:T(8,128)(2,1)S(1)} %broadcast_in_dim_reshape.3), channel_id=1, source_target_pairs={{0,24},{1,25},{2,26},{3,27},{4,28},{5,29},{6,30},{7,31},{8,0},{9,1... | collective-permute-start | bytes 835592 | tf_op jit(solution)/shard_map/ppermute | solution.py:645
  55.5 7.2 %collective-permute-start.20 = (bf16[8,80,512]{2,1,0:T(8,128)(2,1)S(1)}, bf16[8,80,512]{2,1,0:T(8,128)(2,1)S(1)}, u32[]{:S(2)}, u32[]{:S(2)}) collective-permute-start(bf16[8,80,512]{2,1,0:T(8,128)(2,1)S(1)} %constant_dynamic-update-slice_fusion.12.refs_8_), channel_id=1, source_target_pairs={{0,1},{1,0},{2,3},{3,2},{4,5},{5,4},{6,7},{7,6},{8,9},{9,8},{10,11... | collective-permute-start | bytes 1966088 | tf_op jit(solution)/shard_map/ppermute | solution.py:645
  56.8 10.0 %collective-permute-start.21 = (bf16[8,80,512]{2,1,0:T(8,128)(2,1)S(1)}, bf16[8,80,512]{2,1,0:T(8,128)(2,1)S(1)}, u32[]{:S(2)}, u32[]{:S(2)}) collective-permute-start(bf16[8,80,512]{2,1,0:T(8,128)(2,1)S(1)} %collective-permute-done.19.refs_9_), channel_id=1, source_target_pairs={{0,1},{1,0},{2,3},{3,2},{4,5},{5,4},{6,7},{7,6},{8,9},{9,8},{10,11... | collective-permute-start | bytes 1966088 | tf_op jit(solution)/shard_map/ppermute | solution.py:645
  58.6 5.4 %collective-permute-start.10 = (bf16[8,64,512]{2,1,0:T(8,128)(2,1)S(1)}, bf16[8,64,512]{2,1,0:T(8,128)(2,1)S(1)}, u32[]{:S(2)}, u32[]{:S(2)}) collective-permute-start(bf16[8,64,512]{2,1,0:T(8,128)(2,1)S(1)} %collective-permute-done.8.refs_1_), channel_id=1, source_target_pairs={{0,1},{1,0},{2,3},{3,2},{4,5},{5,4},{6,7},{7,6},{8,9},{9,8},{10,11... | collective-permute-start | bytes 1572872 | tf_op jit(solution)/shard_map/ppermute | solution.py:645
  61.0 4.2 %collective-permute-start.9 = (bf16[8,64,512]{2,1,0:T(8,128)(2,1)S(1)}, bf16[8,64,512]{2,1,0:T(8,128)(2,1)S(1)}, u32[]{:S(2)}, u32[]{:S(2)}) collective-permute-start(bf16[8,64,512]{2,1,0:T(8,128)(2,1)S(1)} %constant_dynamic-update-slice_fusion.2.refs_0_), channel_id=1, source_target_pairs={{0,1},{1,0},{2,3},{3,2},{4,5},{5,4},{6,7},{7,6},{8,9},{9,8},{10,11... | collective-permute-start | bytes 1572872 | tf_op jit(solution)/shard_map/ppermute | solution.py:645
  61.9 3.3 collective-permute-start.17
  62.7 13.4 %collective-permute-start.25 = (bf16[4,128,512]{2,1,0:T(8,128)(2,1)S(1)}, bf16[4,128,512]{2,1,0:T(8,128)(2,1)S(1)}, u32[]{:S(2)}, u32[]{:S(2)}) collective-permute-start(bf16[4,128,512]{2,1,0:T(8,128)(2,1)S(1)} %pad_maximum_fusion.7), channel_id=1, source_target_pairs={{0,4},{1,5},{2,6},{3,7},{4,0},{5,1},{6,2},{7,3},{8,12},{9,13},{10,... | collective-permute-start | bytes 1572872 | tf_op jit(solution)/shard_map/ppermute | solution.py:645
  64.0 15.0 %collective-permute-start.7 = (bf16[4,144,512]{2,1,0:T(8,128)(2,1)S(1)}, bf16[4,144,512]{2,1,0:T(8,128)(2,1)S(1)}, u32[]{:S(2)}, u32[]{:S(2)}) collective-permute-start(bf16[4,144,512]{2,1,0:T(8,128)(2,1)S(1)} %pad_maximum_fusion.6), channel_id=1, source_target_pairs={{0,2},{1,3},{2,0},{3,1},{4,6},{5,7},{6,4},{7,5},{8,10},{9,11},{10,... | collective-permute-start | bytes 1769480 | tf_op jit(solution)/shard_map/ppermute | solution.py:645
  77.8 34.2 %collective-permute-start.26 = (bf16[8,128,512]{2,1,0:T(8,128)(2,1)}, bf16[8,128,512]{2,1,0:T(8,128)(2,1)}, u32[]{:S(2)}, u32[]{:S(2)}) collective-permute-start(bf16[8,128,512]{2,1,0:T(8,128)(2,1)} %constant_dynamic-update-slice_fusion.19.refs_4_), channel_id=1, source_target_pairs={{0,2},{1,3},{2,0},{3,1},{4,6},{5,7},{6,4},{7,5},{8,10},{9,11},{10,... | collective-permute-start | bytes 3145736 | tf_op jit(solution)/shard_map/ppermute | solution.py:645
  80.7 29.6 %collective-permute-start.22 = (bf16[8,144,512]{2,1,0:T(8,128)(2,1)}, bf16[8,144,512]{2,1,0:T(8,128)(2,1)}, u32[]{:S(2)}, u32[]{:S(2)}) collective-permute-start(bf16[8,144,512]{2,1,0:T(8,128)(2,1)} %constant_dynamic-update-slice_fusion.17.refs_0_), channel_id=1, source_target_pairs={{0,4},{1,5},{2,6},{3,7},{4,0},{5,1},{6,2},{7,3},{8,12},{9,13},{10,... | collective-permute-start | bytes 3538952 | tf_op jit(solution)/shard_map/ppermute | solution.py:645
  110.3 9.0 %collective-permute-start.23 = (bf16[8,144,512]{2,1,0:T(8,128)(2,1)}, bf16[8,144,512]{2,1,0:T(8,128)(2,1)S(1)}, u32[]{:S(2)}, u32[]{:S(2)}) collective-permute-start(bf16[8,144,512]{2,1,0:T(8,128)(2,1)} %constant_dynamic-update-slice_fusion.17.refs_0_), channel_id=1, source_target_pairs={{0,1},{1,0},{2,3},{3,2},{4,5},{5,4},{6,7},{7,6},{8,9},{9,8},{10,11... | collective-permute-start | bytes 3538952 | tf_op jit(solution)/shard_map/ppermute | solution.py:645
  111.9 7.4 %collective-permute-start.24 = (bf16[8,144,512]{2,1,0:T(8,128)(2,1)}, bf16[8,144,512]{2,1,0:T(8,128)(2,1)S(1)}, u32[]{:S(2)}, u32[]{:S(2)}) collective-permute-start(bf16[8,144,512]{2,1,0:T(8,128)(2,1)} %collective-permute-done.22.refs_1_), channel_id=1, source_target_pairs={{0,1},{1,0},{2,3},{3,2},{4,5},{5,4},{6,7},{7,6},{8,9},{9,8},{10,11... | collective-permute-start | bytes 3538952 | tf_op jit(solution)/shard_map/ppermute | solution.py:645
  112.0 5.8 %collective-permute-start.27 = (bf16[8,128,512]{2,1,0:T(8,128)(2,1)}, bf16[8,128,512]{2,1,0:T(8,128)(2,1)S(1)}, u32[]{:S(2)}, u32[]{:S(2)}) collective-permute-start(bf16[8,128,512]{2,1,0:T(8,128)(2,1)} %constant_dynamic-update-slice_fusion.19.refs_4_), channel_id=1, source_target_pairs={{0,1},{1,0},{2,3},{3,2},{4,5},{5,4},{6,7},{7,6},{8,9},{9,8},{10,11... | collective-permute-start | bytes 3145736 | tf_op jit(solution)/shard_map/ppermute | solution.py:645
  112.4 6.9 %collective-permute-start.28 = (bf16[8,128,512]{2,1,0:T(8,128)(2,1)}, bf16[8,128,512]{2,1,0:T(8,128)(2,1)S(1)}, u32[]{:S(2)}, u32[]{:S(2)}) collective-permute-start(bf16[8,128,512]{2,1,0:T(8,128)(2,1)} %collective-permute-done.26.refs_5_), channel_id=1, source_target_pairs={{0,1},{1,0},{2,3},{3,2},{4,5},{5,4},{6,7},{7,6},{8,9},{9,8},{10,11... | collective-permute-start | bytes 3145736 | tf_op jit(solution)/shard_map/ppermute | solution.py:645
  187.9 4.6 %collective-permute-start.29 = (bf16[8,272,512]{2,1,0:T(8,128)(2,1)}, bf16[8,272,512]{2,1,0:T(8,128)(2,1)S(1)}, u32[]{:S(2)}, u32[]{:S(2)}) collective-permute-start(bf16[8,272,512]{2,1,0:T(8,128)(2,1)} %get-tuple-element.126), channel_id=1, source_target_pairs={{0,1},{1,0},{2,3},{3,2},{4,5},{5,4},{6,7},{7,6},{8,9},{9,8},{10,11... | collective-permute-start | bytes 6684680 | tf_op jit(solution)/shard_map/ppermute | solution.py:645
  195.9 29.3 %collective-permute-start.30 = (bf16[2,2,272,512]{3,2,0,1:T(8,128)(2,1)}, bf16[2,2,272,512]{3,2,0,1:T(8,128)(2,1)}, u32[]{:S(2)}, u32[]{:S(2)}) collective-permute-start(bf16[2,2,272,512]{3,2,0,1:T(8,128)(2,1)} %fusion), channel_id=1, source_target_pairs={{0,2},{1,3},{2,0},{3,1},{4,6},{5,7},{6,4},{7,5},{8,10},{9,11},{10,... | collective-permute-start | bytes 3342344 | tf_op jit(solution)/shard_map/ppermute | solution.py:645
  225.2 3.7 collective-permute-start.31
  228.2 27.4 %collective-permute-start.32 = (bf16[2,272,512]{2,1,0:T(8,128)(2,1)}, bf16[2,272,512]{2,1,0:T(8,128)(2,1)}, u32[]{:S(2)}, u32[]{:S(2)}) collective-permute-start(bf16[2,272,512]{2,1,0:T(8,128)(2,1)} %fusion.1), channel_id=1, source_target_pairs={{0,4},{1,5},{2,6},{3,7},{4,0},{5,1},{6,2},{7,3},{8,12},{9,13},{10,... | collective-permute-start | bytes 1671176 | tf_op jit(solution)/shard_map/ppermute | solution.py:645
  230.1 25.6 %collective-permute-start.33 = (bf16[1,2,272,512]{3,2,1,0:T(8,128)(2,1)}, bf16[1,2,272,512]{3,2,1,0:T(8,128)(2,1)}, u32[]{:S(2)}, u32[]{:S(2)}) collective-permute-start(bf16[1,2,272,512]{3,2,1,0:T(8,128)(2,1)} %fusion.2), channel_id=1, source_target_pairs={{0,4},{1,5},{2,6},{3,7},{4,0},{5,1},{6,2},{7,3},{8,12},{9,13},{10,... | collective-permute-start | bytes 1671176 | tf_op jit(solution)/shard_map/ppermute | solution.py:645
  255.6 6.8 %collective-permute-start.35 = (bf16[4,272,512]{2,1,0:T(8,128)(2,1)}, bf16[4,272,512]{2,1,0:T(8,128)(2,1)S(1)}, u32[]{:S(2)}, u32[]{:S(2)}) collective-permute-start(bf16[4,272,512]{2,1,0:T(8,128)(2,1)} %get-tuple-element.160), channel_id=1, source_target_pairs={{0,1},{1,0},{2,3},{3,2},{4,5},{5,4},{6,7},{7,6},{8,9},{9,8},{10,11... | collective-permute-start | bytes 3342344 | tf_op jit(solution)/shard_map/ppermute | solution.py:645
  257.5 39.3 %copy-start = (bf16[2,272,512]{2,1,0:T(8,128)(2,1)}, bf16[2,272,512]{2,1,0:T(8,128)(2,1)S(1)}, u32[]{:S(2)}) copy-start(bf16[2,272,512]{2,1,0:T(8,128)(2,1)S(1)} %dynamic-slice_bitcast_fusion.2) | copy-start | bytes 1671172
  258.8 38.0 %copy-start.2 = (bf16[2,272,512]{2,1,0:T(8,128)(2,1)}, bf16[2,272,512]{2,1,0:T(8,128)(2,1)S(1)}, u32[]{:S(2)}) copy-start(bf16[2,272,512]{2,1,0:T(8,128)(2,1)S(1)} %dynamic-slice_bitcast_fusion.1) | copy-start | bytes 1671172
  258.9 37.9 %copy-start.15 = (bf16[1,272,512]{2,1,0:T(8,128)(2,1)}, bf16[1,272,512]{2,1,0:T(8,128)(2,1)S(1)}, u32[]{:S(2)}) copy-start(bf16[1,272,512]{2,1,0:T(8,128)(2,1)S(1)} %dynamic-slice_bitcast_fusion.10) | copy-start | bytes 835588
  260.5 36.3 %copy-start.4 = (bf16[2,272,512]{2,1,0:T(8,128)(2,1)}, bf16[2,272,512]{2,1,0:T(8,128)(2,1)S(1)}, u32[]{:S(2)}) copy-start(bf16[2,272,512]{2,1,0:T(8,128)(2,1)S(1)} %dynamic-slice_bitcast_fusion) | copy-start | bytes 1671172
  260.6 36.3 %copy-start.17 = (bf16[1,272,512]{2,1,0:T(8,128)(2,1)}, bf16[1,272,512]{2,1,0:T(8,128)(2,1)S(1)}, u32[]{:S(2)}) copy-start(bf16[1,272,512]{2,1,0:T(8,128)(2,1)S(1)} %dynamic-slice_bitcast_fusion.8) | copy-start | bytes 835588
  262.0 23.2 %collective-permute-start.34 = (bf16[1,272,512]{2,1,0:T(8,128)(2,1)S(1)}, bf16[1,272,512]{2,1,0:T(8,128)(2,1)S(1)}, u32[]{:S(2)}, u32[]{:S(2)}) collective-permute-start(bf16[1,272,512]{2,1,0:T(8,128)(2,1)S(1)} %fusion.5), channel_id=1, source_target_pairs={{0,2},{1,3},{2,0},{3,1},{4,6},{5,7},{6,4},{7,5},{8,10},{9,11},{10,... | collective-permute-start | bytes 835592 | tf_op jit(solution)/shard_map/ppermute | solution.py:645
  262.5 22.7 %collective-permute-start.36 = (bf16[1,2,272,512]{3,2,1,0:T(8,128)(2,1)S(1)}, bf16[1,2,272,512]{3,2,1,0:T(8,128)(2,1)S(1)}, u32[]{:S(2)}, u32[]{:S(2)}) collective-permute-start(bf16[1,2,272,512]{3,2,1,0:T(8,128)(2,1)S(1)} %fusion.3), channel_id=1, source_target_pairs={{0,2},{1,3},{2,0},{3,1},{4,6},{5,7},{6,4},{7,5},{8,10},{9,11},{10,... | collective-permute-start | bytes 1671176 | tf_op jit(solution)/shard_map/ppermute | solution.py:645
  285.2 13.6 %collective-permute-start.37 = (bf16[8,208,512]{2,1,0:T(8,128)(2,1)}, bf16[8,208,512]{2,1,0:T(8,128)(2,1)S(1)}, u32[]{:S(2)}, u32[]{:S(2)}) collective-permute-start(bf16[8,208,512]{2,1,0:T(8,128)(2,1)} %get-tuple-element.176), channel_id=1, source_target_pairs={{0,1},{1,0},{2,3},{3,2},{4,5},{5,4},{6,7},{7,6},{8,9},{9,8},{10,11... | collective-permute-start | bytes 5111816 | tf_op jit(solution)/shard_map/ppermute | solution.py:645
  287.3 8.3 %collective-permute-start.38 = (bf16[1,272,512]{2,1,0:T(8,128)(2,1)S(1)}, bf16[1,272,512]{2,1,0:T(8,128)(2,1)S(1)}, u32[]{:S(2)}, u32[]{:S(2)}) collective-permute-start(bf16[1,272,512]{2,1,0:T(8,128)(2,1)S(1)} %fusion.4), channel_id=1, source_target_pairs={{0,4},{1,5},{2,6},{3,7},{4,0},{5,1},{6,2},{7,3},{8,12},{9,13},{10,... | collective-permute-start | bytes 835592 | tf_op jit(solution)/shard_map/ppermute | solution.py:645
  300.9 26.7 %copy-start.1 = (bf16[2,272,512]{2,1,0:T(8,128)(2,1)S(1)}, bf16[2,272,512]{2,1,0:T(8,128)(2,1)}, u32[]{:S(2)}) copy-start(bf16[2,272,512]{2,1,0:T(8,128)(2,1)} %copy-done) | copy-start | bytes 1671172
  300.9 26.7 %copy-start.3 = (bf16[2,272,512]{2,1,0:T(8,128)(2,1)S(1)}, bf16[2,272,512]{2,1,0:T(8,128)(2,1)}, u32[]{:S(2)}) copy-start(bf16[2,272,512]{2,1,0:T(8,128)(2,1)} %copy-done.2) | copy-start | bytes 1671172
  326.7 6.8 %collective-permute-start.39 = (bf16[8,208,512]{2,1,0:T(8,128)(2,1)}, bf16[8,208,512]{2,1,0:T(8,128)(2,1)}, u32[]{:S(2)}, u32[]{:S(2)}) collective-permute-start(bf16[8,208,512]{2,1,0:T(8,128)(2,1)} %get-tuple-element.193), channel_id=1, source_target_pairs={{0,1},{1,0},{2,3},{3,2},{4,5},{5,4},{6,7},{7,6},{8,9},{9,8},{10,11... | collective-permute-start | bytes 5111816 | tf_op jit(solution)/shard_map/ppermute | solution.py:645
  330.3 8.3 %collective-permute-start.44 = (bf16[272,512]{1,0:T(8,128)(2,1)S(1)}, bf16[272,512]{1,0:T(8,128)(2,1)S(1)}, u32[]{:S(2)}, u32[]{:S(2)}) collective-permute-start(bf16[272,512]{1,0:T(8,128)(2,1)S(1)} %copy-done.39), channel_id=1, source_target_pairs={{0,8},{1,9},{2,10},{3,11},{4,12},{5,13},{6,14},{7,15},{8,16},{9,17... | collective-permute-start | bytes 835592 | tf_op jit(solution)/shard_map/ppermute | solution.py:798
  330.3 24.1 %collective-permute-start.45 = (bf16[272,512]{1,0:T(8,128)(2,1)S(1)}, bf16[272,512]{1,0:T(8,128)(2,1)S(1)}, u32[]{:S(2)}, u32[]{:S(2)}) collective-permute-start(bf16[272,512]{1,0:T(8,128)(2,1)S(1)} %copy-done.38), channel_id=1, source_target_pairs={{0,16},{1,17},{2,18},{3,19},{4,20},{5,21},{6,22},{7,23},{8,24},{9,... | collective-permute-start | bytes 835592 | tf_op jit(solution)/shard_map/ppermute | solution.py:798
  331.6 25.0 %collective-permute-start.46 = (bf16[272,512]{1,0:T(8,128)(2,1)S(1)}, bf16[272,512]{1,0:T(8,128)(2,1)S(1)}, u32[]{:S(2)}, u32[]{:S(2)}) collective-permute-start(bf16[272,512]{1,0:T(8,128)(2,1)S(1)} %copy-done.37), channel_id=1, source_target_pairs={{0,24},{1,25},{2,26},{3,27},{4,28},{5,29},{6,30},{7,31},{8,0},{9,1... | collective-permute-start | bytes 835592 | tf_op jit(solution)/shard_map/ppermute | solution.py:798
  333.1 23.4 %collective-permute-start.43 = (bf16[1,2,208,512]{3,2,1,0:T(8,128)(2,1)S(1)}, bf16[1,2,208,512]{3,2,1,0:T(8,128)(2,1)S(1)}, u32[]{:S(2)}, u32[]{:S(2)}) collective-permute-start(bf16[1,2,208,512]{3,2,1,0:T(8,128)(2,1)S(1)} %copy-done.36), channel_id=1, source_target_pairs={{0,4},{1,5},{2,6},{3,7},{4,0},{5,1},{6,2},{7,3},{8,12},{9,13},{10,... | collective-permute-start | bytes 1277960 | tf_op jit(solution)/shard_map/ppermute | solution.py:645
  334.4 22.2 %collective-permute-start.42 = (bf16[1,2,208,512]{3,2,1,0:T(8,128)(2,1)S(1)}, bf16[1,2,208,512]{3,2,1,0:T(8,128)(2,1)S(1)}, u32[]{:S(2)}, u32[]{:S(2)}) collective-permute-start(bf16[1,2,208,512]{3,2,1,0:T(8,128)(2,1)S(1)} %copy-done.35), channel_id=1, source_target_pairs={{0,2},{1,3},{2,0},{3,1},{4,6},{5,7},{6,4},{7,5},{8,10},{9,11},{10,... | collective-permute-start | bytes 1277960 | tf_op jit(solution)/shard_map/ppermute | solution.py:645
  338.5 20.8 %collective-permute-start.41 = (bf16[1,2,208,512]{3,2,1,0:T(8,128)(2,1)S(1)}, bf16[1,2,208,512]{3,2,1,0:T(8,128)(2,1)S(1)}, u32[]{:S(2)}, u32[]{:S(2)}) collective-permute-start(bf16[1,2,208,512]{3,2,1,0:T(8,128)(2,1)S(1)} %fusion.11), channel_id=1, source_target_pairs={{0,4},{1,5},{2,6},{3,7},{4,0},{5,1},{6,2},{7,3},{8,12},{9,13},{10,... | collective-permute-start | bytes 1277960 | tf_op jit(solution)/shard_map/ppermute | solution.py:645
  354.5 10.7 %collective-permute-start.40 = (bf16[1,2,208,512]{3,2,1,0:T(8,128)(2,1)S(1)}, bf16[1,2,208,512]{3,2,1,0:T(8,128)(2,1)S(1)}, u32[]{:S(2)}, u32[]{:S(2)}) collective-permute-start(bf16[1,2,208,512]{3,2,1,0:T(8,128)(2,1)S(1)} %fusion.10), channel_id=1, source_target_pairs={{0,2},{1,3},{2,0},{3,1},{4,6},{5,7},{6,4},{7,5},{8,10},{9,11},{10,... | collective-permute-start | bytes 1277960 | tf_op jit(solution)/shard_map/ppermute | solution.py:645
  357.9 16.5 %collective-permute-start.50 = (bf16[1,208,512]{2,1,0:T(8,128)(2,1)S(1)}, bf16[1,208,512]{2,1,0:T(8,128)(2,1)S(1)}, u32[]{:S(2)}, u32[]{:S(2)}) collective-permute-start(bf16[1,208,512]{2,1,0:T(8,128)(2,1)S(1)} %fusion.12), channel_id=1, source_target_pairs={{0,2},{1,3},{2,0},{3,1},{4,6},{5,7},{6,4},{7,5},{8,10},{9,11},{10,... | collective-permute-start | bytes 638984 | tf_op jit(solution)/shard_map/ppermute | solution.py:645
  358.8 15.6 %collective-permute-start.49 = (bf16[1,208,512]{2,1,0:T(8,128)(2,1)S(1)}, bf16[1,208,512]{2,1,0:T(8,128)(2,1)S(1)}, u32[]{:S(2)}, u32[]{:S(2)}) collective-permute-start(bf16[1,208,512]{2,1,0:T(8,128)(2,1)S(1)} %fusion.13), channel_id=1, source_target_pairs={{0,4},{1,5},{2,6},{3,7},{4,0},{5,1},{6,2},{7,3},{8,12},{9,13},{10,... | collective-permute-start | bytes 638984 | tf_op jit(solution)/shard_map/ppermute | solution.py:645
  359.5 14.9 %collective-permute-start.48 = (bf16[1,208,512]{2,1,0:T(8,128)(2,1)S(1)}, bf16[1,208,512]{2,1,0:T(8,128)(2,1)S(1)}, u32[]{:S(2)}, u32[]{:S(2)}) collective-permute-start(bf16[1,208,512]{2,1,0:T(8,128)(2,1)S(1)} %fusion.14), channel_id=1, source_target_pairs={{0,2},{1,3},{2,0},{3,1},{4,6},{5,7},{6,4},{7,5},{8,10},{9,11},{10,... | collective-permute-start | bytes 638984 | tf_op jit(solution)/shard_map/ppermute | solution.py:645
  365.3 5.1 %collective-permute-start.47 = (bf16[1,208,512]{2,1,0:T(8,128)(2,1)S(1)}, bf16[1,208,512]{2,1,0:T(8,128)(2,1)S(1)}, u32[]{:S(2)}, u32[]{:S(2)}) collective-permute-start(bf16[1,208,512]{2,1,0:T(8,128)(2,1)S(1)} %fusion.15), channel_id=1, source_target_pairs={{0,4},{1,5},{2,6},{3,7},{4,0},{5,1},{6,2},{7,3},{8,12},{9,13},{10,... | collective-permute-start | bytes 638984 | tf_op jit(solution)/shard_map/ppermute | solution.py:645
  375.1 5.3 %collective-permute-start.51 = (bf16[208,512]{1,0:T(8,128)(2,1)S(1)}, bf16[208,512]{1,0:T(8,128)(2,1)S(1)}, u32[]{:S(2)}, u32[]{:S(2)}) collective-permute-start(bf16[208,512]{1,0:T(8,128)(2,1)S(1)} %get-tuple-element.210), channel_id=1, source_target_pairs={{0,8},{1,9},{2,10},{3,11},{4,12},{5,13},{6,14},{7,15},{8,16},{9,17... | collective-permute-start | bytes 638984 | tf_op jit(solution)/shard_map/ppermute | solution.py:798
  375.2 17.4 %collective-permute-start.52 = (bf16[208,512]{1,0:T(8,128)(2,1)S(1)}, bf16[208,512]{1,0:T(8,128)(2,1)S(1)}, u32[]{:S(2)}, u32[]{:S(2)}) collective-permute-start(bf16[208,512]{1,0:T(8,128)(2,1)S(1)} %get-tuple-element.212), channel_id=1, source_target_pairs={{0,16},{1,17},{2,18},{3,19},{4,20},{5,21},{6,22},{7,23},{8,24},{9,... | collective-permute-start | bytes 638984 | tf_op jit(solution)/shard_map/ppermute | solution.py:798
  378.3 19.3 %collective-permute-start.53 = (bf16[208,512]{1,0:T(8,128)(2,1)S(1)}, bf16[208,512]{1,0:T(8,128)(2,1)S(1)}, u32[]{:S(2)}, u32[]{:S(2)}) collective-permute-start(bf16[208,512]{1,0:T(8,128)(2,1)S(1)} %get-tuple-element.211), channel_id=1, source_target_pairs={{0,24},{1,25},{2,26},{3,27},{4,28},{5,29},{6,30},{7,31},{8,0},{9,1... | collective-permute-start | bytes 638984 | tf_op jit(solution)/shard_map/ppermute | solution.py:798
  (47 other events, 278.6 us)

commit v4 on v3

--- a/solution.py
+++ b/solution.py
@@ -501,6 +501,14 @@
     )
 
 
+BACK_WIDTH = {"full": 384, "causal": 256, "cross": 272}
+
+
+def four_heads(block):
+    owner = lax.broadcasted_iota(jnp.int32, block.shape, 1) // 64
+    return jnp.concatenate([jnp.where(owner == h, block, 0.0) for h in range(4)], axis=0).astype(BF)
+
+
 def attn_bwd_body(kind, before, plan, base, seal, count, moves, emit, words, ins, raw_in, outs, raw, own):
     cross = kind == "cross"
     lq_ref, lk_ref = words
@@ -517,7 +525,7 @@
         pairs = source.shape[0]
         moves.fetch(source, target.at[pl.ds(target.shape[0] - pairs, pairs)])
     tokens = q_ref.shape[0]
-    blocks, width = tokens // TILE, WIDTH[kind]
+    blocks, width = tokens // TILE, BACK_WIDTH[kind]
     ends_q, ends_k = ends_of(lq_ref), ends_of(lk_ref)
     segq_ref[...] = seg_iota(ends_q, (8, tokens), 1)
     segk_ref[...] = seg_iota(ends_k, (tokens, TILE), 0)
@@ -571,7 +579,55 @@
         dq_ref[rows, :] = jnp.concatenate(dqs, axis=1).astype(BF)
         return 0
 
-    lax.fori_loop(0, blocks, step, 0)
+    def fine_step(tile, _):
+        rows = row_tile(tile, TILE)
+        segs = segq_ref[:, rows]
+        lses = jnp.where(segs == SENTS, -LOWEST, lse_ref[:, rows])
+        inners = inner_ref[:8, rows]
+        turned = [pltpu.roll(a, TILE // 2, 1) for a in (segs, lses, inners)]
+        low = lax.broadcasted_iota(jnp.int32, (1, TILE), 1) < TILE // 2
+        for half in range(2):
+            at = tile * TILE + half * (TILE // 2)
+            if kind == "cross":
+                start = start_of(at, ends_q, ends_k) // 16 * 16
+            else:
+                start = at - TILE
+            start = pl.multiple_of(jnp.clip(start, 0, tokens - width), 16)
+            win, mine = pl.ds(start, width), pl.ds(pl.multiple_of(at, TILE // 2), TILE // 2)
+
+            def pair(which, a, b):
+                plain, other = (segs, lses, inners)[which], turned[which]
+                one, two = (plain, other) if half == 0 else (other, plain)
+                return jnp.where(low, one[a : a + 1], two[b : b + 1])
+
+            ok = segk_ref[win, :] == pair(0, 0, 0)
+            if kind == "causal":
+                places = lax.broadcasted_iota(jnp.int32, (width, TILE), 1) % (TILE // 2)
+                ok = ok & (places - lax.broadcasted_iota(jnp.int32, (width, TILE), 0) >= start - at)
+            mask = jnp.where(ok, 0.0, LOWEST)
+            mask = jnp.concatenate([mask, mask], axis=1)
+            for group in range(2):
+                lanes = slice(group * 256, (group + 1) * 256)
+                q4 = four_heads(q_ref[mine, lanes].astype(F32) * 0.125)
+                g4 = four_heads(g_ref[mine, lanes].astype(F32))
+                lse, inner = (
+                    jnp.concatenate([pair(which, 4 * group + h, 4 * group + h + 1) for h in (0, 2)], axis=1)
+                    for which in (1, 2)
+                )
+                kp, vp = k_ref[win, lanes], v_ref[win, lanes]
+                prob = jnp.exp(dot(kp, q4, NT) + mask - lse)
+                ds = (prob * (dot(vp, g4, NT) - inner)).astype(BF)
+                dk_acc[win, lanes] += dot(ds, q4)
+                dv_acc[win, lanes] += dot(prob.astype(BF), g4)
+                dq = dot(ds, kp, TN)
+                owner = lax.broadcasted_iota(jnp.int32, (TILE // 2, 256), 1) // 64
+                own = dq[:64]
+                for h in range(1, 4):
+                    own = jnp.where(owner == h, dq[64 * h : 64 * h + 64], own)
+                dq_ref[mine, lanes] = (own * 0.125).astype(BF)
+        return 0
+
+    lax.fori_loop(0, blocks, fine_step if cross else step, 0, unroll=2)
     moves.ready(vec_ref, more_ref)
 
     sums = (jnp.zeros((1, D), F32),) * 2

time: 407 us -> 403 us (level)
    pallas_call x7, Pallas kernels: 187 us -> 183 us  [call(): pl.pallas_call(kernel, out_shape=tuple((jax.ShapeDtypeStruct(s, d) for s,...]
  transfers between devices with their start and end apart: 54 -> 54, of which waited for: 24 -> 25; matrix products, arithmetic and copies ran while one was open for 6% -> 6% of each run, Pallas kernels for 27% -> 26%
where the time goes in v4:
time: 403 us; the launch traced here: 398 us
  Pallas kernels  196 us (49%)
  waiting for transfers between devices  108 us (27%)
  starting transfers between devices  48.6 us (12%)
  local copies, waits for them, and re-layouts  28.5 us (7%)
  other arithmetic  14.9 us (4%)
    pallas_call x7, Pallas kernels, call(): pl.pallas_call(kernel, out_shape=tuple((jax.ShapeDtypeStruct(s, d) for s,...  183 us
    ppermute x48, waiting for transfers between devices, shifted(): return lax.ppermute(block, 'fsdp', pairs)  70.9 us
    ppermute x48, starting transfers between devices, shifted(): return lax.ppermute(block, 'fsdp', pairs)  41.7 us
    ppermute x6, waiting for transfers between devices, send_line(): pieces.append(lax.ppermute(away, 'fsdp', pairs))  37 us
    pallas_call x2, Pallas kernels, assemble(): pl.pallas_call(functools.partial(assemble_body, spans, labels, rows, vect...  12.9 us
    unnamed x127, local copies, waits for them, and re-layouts  12.7 us
    convert_element_type x14, other arithmetic, halve(): away = total_of([pick(t, 1 - at, axis) for t in terms]).astype(BF)  11.2 us
  transfers between devices with their start and end apart: 54, of which 25 were waited for; matrix products, arithmetic and copies ran while one was open for 6% of the time, Pallas kernels for 26%

profile of v4, /device:TPU:9, one launch (start us, length us, event | category | flops | bytes accessed | tf_op | source)
XLA Modules:
  0.0 397.7 jit_solution(3850343835387669888)
XLA Ops:
  1.9 1.3 collective-permute-start.11
  4.3 1.4 collective-permute-start.13
  6.7 1.3 collective-permute-start
  8.5 1.7 collective-permute-done
  10.3 3.1 collective-permute-start.2
  13.4 2.3 collective-permute-done.12
  15.8 7.9 %collective-permute-done.13 = bf16[1,144,512]{2,1,0:T(8,128)(2,1)S(1)} collective-permute-done((bf16[1,144,512]{2,1,0:T(8,128)(2,1)S(1)}, bf16[1,144,512]{2,1,0:T(8,128)(2,1)S(1)}, u32[]{:S(2)}, u32[]{:S(2)}) %collective-permute-start.13) | collective-permute-done | bytes 147488 | tf_op jit(solution)/shard_map/ppermute | solution.py:701
  23.7 1.3 collective-permute-start.18
  25.1 1.3 collective-permute-start.14
  26.5 2.8 collective-permute-done.3
  29.7 2.7 collective-permute-done.18
  32.5 1.3 collective-permute-start.19
  34.2 1.3 collective-permute-start.15
  35.5 1.5 collective-permute-done.4
  37.0 2.3 collective-permute-start.16
  39.3 7.8 %collective-permute-done.5 = bf16[1,272,512]{2,1,0:T(8,128)(2,1)S(1)} collective-permute-done((bf16[1,272,512]{2,1,0:T(8,128)(2,1)S(1)}, bf16[1,272,512]{2,1,0:T(8,128)(2,1)S(1)}, u32[]{:S(2)}, u32[]{:S(2)}) %collective-permute-start.5) | collective-permute-done | bytes 278560 | tf_op jit(solution)/shard_map/ppermute | solution.py:701
  47.1 2.9 collective-permute-start.6
  50.0 5.5 %collective-permute-done.6 = bf16[1,272,512]{2,1,0:T(8,128)(2,1)S(1)} collective-permute-done((bf16[1,272,512]{2,1,0:T(8,128)(2,1)S(1)}, bf16[1,272,512]{2,1,0:T(8,128)(2,1)S(1)}, u32[]{:S(2)}, u32[]{:S(2)}) %collective-permute-start.6) | collective-permute-done | bytes 278560 | tf_op jit(solution)/shard_map/ppermute | solution.py:701
  55.5 1.3 collective-permute-start.20
  56.9 1.7 collective-permute-done.8.refs_1_
  58.6 2.4 collective-permute-start.10
  62.7 1.3 collective-permute-start.25
  64.0 1.2 collective-permute-start.7
  67.6 5.7 %shard_map.110 = (bf16[32,192,512]{2,1,0:T(8,128)(2,1)}, f32[16,512]{1,0:T(8,128)}) custom-call(bf16[8,64,512]{2,1,0:T(8,128)(2,1)} %copy-done.43, bf16[8,64,512]{2,1,0:T(8,128)(2,1)} %copy-done.51, bf16[8,64,512]{2,1,0:T(8,128)(2,1)} %copy-done.55, bf16[8,64,512]{2,1,0:T(8,128)(2,1)} %copy-done.54, bf16[8,64,512]{2,1,0:T(8,128)(2,1)} %copy-done.42, ...), custom_call_target="tpu_custom_call" | custom-call | flops 80000000000 | bytes 1048576 | tf_op jit(solution)/shard_map/pallas_call | solution.py:766
  73.4 2.7 collective-permute-done.25
  77.8 1.2 collective-permute-start.26
  80.7 1.2 collective-permute-start.22
  81.9 28.3 %shard_map.111 = (bf16[1024,512]{1,0:T(8,128)(2,1)}, bf16[1024,512]{1,0:T(8,128)(2,1)}, bf16[1024,512]{1,0:T(8,128)(2,1)}, bf16[1024,512]{1,0:T(8,128)(2,1)}, f3...) custom-call(s32[1,16]{1,0:T(1,128)} %refs_1_.9, ...), custom_call_target="tpu_custom_call" | custom-call | flops 299999985664 | bytes 1048576 | tf_op jit(solution)/shard_map/pallas_call | solution.py:148
  110.3 1.6 collective-permute-start.23
  112.5 5.3 %collective-permute-done.27.refs_6_ = bf16[8,128,512]{2,1,0:T(8,128)(2,1)S(1)} collective-permute-done((bf16[8,128,512]{2,1,0:T(8,128)(2,1)}, bf16[8,128,512]{2,1,0:T(8,128)(2,1)S(1)}, u32[]{:S(2)}, u32[]{:S(2)}) %collective-permute-start.27) | collective-permute-done | bytes 1048608 | tf_op jit(solution)/shard_map/ppermute | solution.py:701
  117.8 1.5 collective-permute-done.28.refs_7_
  121.6 7.2 %shard_map.112 = (bf16[32,272,512]{2,1,0:T(8,128)(2,1)}, f32[16,512]{1,0:T(8,128)}) custom-call(bf16[8,144,512]{2,1,0:T(8,128)(2,1)} %constant_dynamic-update-slice_fusion.17.refs_0_, bf16[8,144,512]{2,1,0:T(8,128)(2,1)} %collective-permute-done.22.refs_1_, bf16[8,144,512]{2,1,0:T(8,128)(2,1)} %copy-done.44, bf16[8,144,512]{2,1,0:T(8,128)(2,1)} %copy-done.45, ...), custom_call_target="tpu_custom_call" | custom-call | flops 80000000000 | bytes 1048576 | tf_op jit(solution)/shard_map/pallas_call | solution.py:766
  128.8 38.5 %shard_map.113 = (bf16[1024,512]{1,0:T(8,128)(2,1)}, bf16[1024,512]{1,0:T(8,128)(2,1)}, bf16[1024,512]{1,0:T(8,128)(2,1)}, bf16[1024,512]{1,0:T(8,128)(2,1)}, f3...) custom-call(s32[1,16]{1,0:T(1,128)} %refs_1_.8, ...), custom_call_target="tpu_custom_call" | custom-call | flops 299999985664 | bytes 1048576 | tf_op jit(solution)/shard_map/pallas_call | solution.py:148
  167.4 21.6 %shard_map.114 = (bf16[8,272,512]{2,1,0:T(8,128)(2,1)}, bf16[8,272,512]{2,1,0:T(8,128)(2,1)}, bf16[16,512]{1,0:T(8,128)(2,1)}, f32[16,512]{1,0:T(8,128)}, f32[1024,512]{1,0:T(8,128)}, /*index=5*/f32[1024,512]{1,0:T(8,128)}) custom-call(bf16[1024,512]{1,0:T(8,128)(2,1)} %refs_0_.8, f32[1024,512]{1,0:T(8,128)} %get-tuple-element.119.refs_1_, ...), custom_call_target="tpu_custom_call" | custom-call | flops 130000003072 | bytes 1048576 | tf_op jit(solution)/shard_map/pallas_call | solution.py:148
  189.4 4.2 %collective-permute-done.29 = bf16[8,272,512]{2,1,0:T(8,128)(2,1)S(1)} collective-permute-done((bf16[8,272,512]{2,1,0:T(8,128)(2,1)}, bf16[8,272,512]{2,1,0:T(8,128)(2,1)S(1)}, u32[]{:S(2)}, u32[]{:S(2)}) %collective-permute-start.29) | collective-permute-done | bytes 2228256 | tf_op jit(solution)/shard_map/ppermute | solution.py:701
  193.6 3.4 fusion
  197.3 23.7 %shard_map.115 = (bf16[4,272,512]{2,1,0:T(8,128)(2,1)}, bf16[4,272,512]{2,1,0:T(8,128)(2,1)}, bf16[16,512]{1,0:T(8,128)(2,1)}, f32[16,512]{1,0:T(8,128)}, f32[1024,512]{1,0:T(8,128)}, /*index=5*/f32[1024,512]{1,0:T(8,128)}) custom-call(s32[1,16]{1,0:T(1,128)} %refs_1_.8, s32[1,16]{1,0:T(1,128)} %refs_1_.9, f32[1024,512]{1,0:T(8,128)} %get-tuple-element.128.refs_2_, ...), custom_call_target="tpu_custom_call" | custom-call | flops 260000006144 | bytes 1048576 | tf_op jit(solution)/shard_map/pallas_call | solution.py:148
  220.9 2.2 collective-permute-done.30
  223.1 1.2 collective-permute-start.31
  224.3 2.5 fusion.1
  228.2 1.2 collective-permute-start.33
  229.4 24.0 %shard_map.116 = (bf16[4,272,512]{2,1,0:T(8,128)(2,1)}, bf16[4,272,512]{2,1,0:T(8,128)(2,1)}, bf16[16,512]{1,0:T(8,128)(2,1)}, f32[1024,512]{1,0:T(8,128)}) custom-call(s32[1,16]{1,0:T(1,128)} %refs_1_.8, s32[1,16]{1,0:T(1,128)} %refs_1_.8, f32[1024,512]{1,0:T(8,128)} %get-tuple-element.146.refs_2_, bf16[1024,512]{1,0:T(8,128)(2,1)} %get-tuple-element.147.refs_3_, ...), custom_call_target="tpu_custom_call" | custom-call | flops 260000006144 | bytes 1048576 | tf_op jit(solution)/shard_map/pallas_call | solution.py:148
  254.1 1.2 dynamic-slice_bitcast_fusion.2
  255.3 1.3 dynamic-slice_bitcast_fusion.1
  256.7 1.4 dynamic-slice_bitcast_fusion
  258.4 1.4 fusion.5
  260.3 1.3 collective-permute-start.36
  261.6 21.5 %shard_map.117 = (bf16[8,208,512]{2,1,0:T(8,128)(2,1)}, bf16[8,208,512]{2,1,0:T(8,128)(2,1)}, bf16[3,208,512]{2,1,0:T(8,128)(2,1)}, bf16[3,208,512]{2,1,0:T(8,12...) custom-call(f32[1024,512]{1,0:T(8,128)} %get-tuple-element.162.refs_0_, ...), custom_call_target="tpu_custom_call" | custom-call | flops 130000003072 | bytes 1048576 | tf_op jit(solution)/shard_map/pallas_call | solution.py:148
  285.5 1.2 copy-done.29
  286.8 6.7 %collective-permute-done.38 = bf16[1,272,512]{2,1,0:T(8,128)(2,1)S(1)} collective-permute-done((bf16[1,272,512]{2,1,0:T(8,128)(2,1)S(1)}, bf16[1,272,512]{2,1,0:T(8,128)(2,1)S(1)}, u32[]{:S(2)}, u32[]{:S(2)}) %collective-permute-start.38) | collective-permute-done | bytes 278560 | tf_op jit(solution)/shard_map/ppermute | solution.py:701
  298.8 25.2 %shard_map.118 = (bf16[8,208,512]{2,1,0:T(8,128)(2,1)}, bf16[8,208,512]{2,1,0:T(8,128)(2,1)}, bf16[16,512]{1,0:T(8,128)(2,1)}, f32[1024,512]{1,0:T(8,128)}) custom-call(s32[1,16]{1,0:T(1,128)} %refs_1_.9, s32[1,16]{1,0:T(1,128)} %refs_1_.9, f32[1024,512]{1,0:T(8,128)} %get-tuple-element.180.refs_2_, bf16[1024,512]{1,0:T(8,128)(2,1)} %get-tuple-element.181.refs_3_, ...), custom_call_target="tpu_custom_call" | custom-call | flops 260000006144 | bytes 1048576 | tf_op jit(solution)/shard_map/pallas_call | solution.py:148
  328.3 1.5 collective-permute-start.46
  332.0 1.5 fusion.19
  333.7 2.1 collective-permute-done.44
  336.0 15.7 %collective-permute-done.45 = bf16[272,512]{1,0:T(8,128)(2,1)S(1)} collective-permute-done((bf16[272,512]{1,0:T(8,128)(2,1)S(1)}, bf16[272,512]{1,0:T(8,128)(2,1)S(1)}, u32[]{:S(2)}, u32[]{:S(2)}) %collective-permute-start.45) | collective-permute-done | bytes 278560 | tf_op jit(solution)/shard_map/ppermute | solution.py:854
  351.9 1.4 collective-permute-done.46
  353.4 1.2 fusion.7
  357.0 5.5 %collective-permute-done.40 = bf16[1,2,208,512]{3,2,1,0:T(8,128)(2,1)S(1)} collective-permute-done((bf16[1,2,208,512]{3,2,1,0:T(8,128)(2,1)S(1)}, bf16[1,2,208,512]{3,2,1,0:T(8,128)(2,1)S(1)}, u32[]{:S(2)}, u32[]{:S(2)}) %collective-permute-start.40) | collective-permute-done | bytes 426016 | tf_op jit(solution)/shard_map/ppermute | solution.py:701
  362.9 4.8 %collective-permute-done.47 = bf16[1,208,512]{2,1,0:T(8,128)(2,1)S(1)} collective-permute-done((bf16[1,208,512]{2,1,0:T(8,128)(2,1)S(1)}, bf16[1,208,512]{2,1,0:T(8,128)(2,1)S(1)}, u32[]{:S(2)}, u32[]{:S(2)}) %collective-permute-start.47) | collective-permute-done | bytes 213024 | tf_op jit(solution)/shard_map/ppermute | solution.py:701
  367.7 4.0 collective-permute-done.48
  372.5 3.2 collective-permute-start.52
  375.6 1.4 collective-permute-start.53
  377.7 12.2 %collective-permute-done.52 = bf16[208,512]{1,0:T(8,128)(2,1)S(1)} collective-permute-done((bf16[208,512]{1,0:T(8,128)(2,1)S(1)}, bf16[208,512]{1,0:T(8,128)(2,1)S(1)}, u32[]{:S(2)}, u32[]{:S(2)}) %collective-permute-start.52) | collective-permute-done | bytes 213024 | tf_op jit(solution)/shard_map/ppermute | solution.py:854
  389.9 5.1 %collective-permute-done.53 = bf16[208,512]{1,0:T(8,128)(2,1)S(1)} collective-permute-done((bf16[208,512]{1,0:T(8,128)(2,1)S(1)}, bf16[208,512]{1,0:T(8,128)(2,1)S(1)}, u32[]{:S(2)}, u32[]{:S(2)}) %collective-permute-start.53) | collective-permute-done | bytes 213024 | tf_op jit(solution)/shard_map/ppermute | solution.py:854
  (265 shorter events, 39.9 us)
Async XLA Ops:
  1.9 11.5 %collective-permute-start.11 = (bf16[1,144,512]{2,1,0:T(8,128)(2,1)S(1)}, bf16[1,144,512]{2,1,0:T(8,128)(2,1)S(1)}, u32[]{:S(2)}, u32[]{:S(2)}) collective-permute-start(bf16[1,144,512]{2,1,0:T(8,128)(2,1)S(1)} %broadcast_in_dim.7), channel_id=1, source_target_pairs={{0,8},{1,9},{2,10},{3,11},{4,12},{5,13},{6,14},{7,15},{8,16},{9,17... | collective-permute-start | bytes 442376 | tf_op jit(solution)/shard_map/ppermute | solution.py:701
  3.2 12.5 %collective-permute-start.12 = (bf16[1,144,512]{2,1,0:T(8,128)(2,1)S(1)}, bf16[1,144,512]{2,1,0:T(8,128)(2,1)S(1)}, u32[]{:S(2)}, u32[]{:S(2)}) collective-permute-start(bf16[1,144,512]{2,1,0:T(8,128)(2,1)S(1)} %broadcast_in_dim.7), channel_id=1, source_target_pairs={{0,16},{1,17},{2,18},{3,19},{4,20},{5,21},{6,22},{7,23},{8,24},{9,... | collective-permute-start | bytes 442376 | tf_op jit(solution)/shard_map/ppermute | solution.py:701
  4.3 19.3 %collective-permute-start.13 = (bf16[1,144,512]{2,1,0:T(8,128)(2,1)S(1)}, bf16[1,144,512]{2,1,0:T(8,128)(2,1)S(1)}, u32[]{:S(2)}, u32[]{:S(2)}) collective-permute-start(bf16[1,144,512]{2,1,0:T(8,128)(2,1)S(1)} %broadcast_in_dim.7), channel_id=1, source_target_pairs={{0,24},{1,25},{2,26},{3,27},{4,28},{5,29},{6,30},{7,31},{8,0},{9,1... | collective-permute-start | bytes 442376 | tf_op jit(solution)/shard_map/ppermute | solution.py:701
  6.7 3.5 collective-permute-start
  10.2 16.2 %collective-permute-start.1 = (bf16[2,64,512]{2,1,0:T(8,128)(2,1)S(1)}, bf16[2,64,512]{2,1,0:T(8,128)(2,1)S(1)}, u32[]{:S(2)}, u32[]{:S(2)}) collective-permute-start(bf16[2,64,512]{2,1,0:T(8,128)(2,1)S(1)} %get-tuple-element.230), channel_id=1, source_target_pairs={{0,8},{1,9},{2,10},{3,11},{4,12},{5,13},{6,14},{7,15},{8,16},{9,17... | collective-permute-start | bytes 393224 | tf_op jit(solution)/shard_map/ppermute | solution.py:701
  10.3 16.2 %collective-permute-start.2 = (bf16[2,64,512]{2,1,0:T(8,128)(2,1)S(1)}, bf16[2,64,512]{2,1,0:T(8,128)(2,1)S(1)}, u32[]{:S(2)}, u32[]{:S(2)}) collective-permute-start(bf16[2,64,512]{2,1,0:T(8,128)(2,1)S(1)} %get-tuple-element.230), channel_id=1, source_target_pairs={{0,16},{1,17},{2,18},{3,19},{4,20},{5,21},{6,22},{7,23},{8,24},{9,... | collective-permute-start | bytes 393224 | tf_op jit(solution)/shard_map/ppermute | solution.py:701
  13.4 15.8 %collective-permute-start.3 = (bf16[2,64,512]{2,1,0:T(8,128)(2,1)S(1)}, bf16[2,64,512]{2,1,0:T(8,128)(2,1)S(1)}, u32[]{:S(2)}, u32[]{:S(2)}) collective-permute-start(bf16[2,64,512]{2,1,0:T(8,128)(2,1)S(1)} %get-tuple-element.230), channel_id=1, source_target_pairs={{0,24},{1,25},{2,26},{3,27},{4,28},{5,29},{6,30},{7,31},{8,0},{9,1... | collective-permute-start | bytes 393224 | tf_op jit(solution)/shard_map/ppermute | solution.py:701
  23.7 8.7 %collective-permute-start.18 = (bf16[4,80,512]{2,1,0:T(8,128)(2,1)S(1)}, bf16[4,80,512]{2,1,0:T(8,128)(2,1)S(1)}, u32[]{:S(2)}, u32[]{:S(2)}) collective-permute-start(bf16[4,80,512]{2,1,0:T(8,128)(2,1)S(1)} %pad_maximum_fusion.8), channel_id=1, source_target_pairs={{0,4},{1,5},{2,6},{3,7},{4,0},{5,1},{6,2},{7,3},{8,12},{9,13},{10,... | collective-permute-start | bytes 983048 | tf_op jit(solution)/shard_map/ppermute | solution.py:701
  25.1 9.0 %collective-permute-start.14 = (bf16[4,64,512]{2,1,0:T(8,128)(2,1)S(1)}, bf16[4,64,512]{2,1,0:T(8,128)(2,1)S(1)}, u32[]{:S(2)}, u32[]{:S(2)}) collective-permute-start(bf16[4,64,512]{2,1,0:T(8,128)(2,1)S(1)} %pad_maximum_fusion.9), channel_id=1, source_target_pairs={{0,2},{1,3},{2,0},{3,1},{4,6},{5,7},{6,4},{7,5},{8,10},{9,11},{10,... | collective-permute-start | bytes 786440 | tf_op jit(solution)/shard_map/ppermute | solution.py:701
  29.3 7.7 %collective-permute-start.4 = (bf16[1,272,512]{2,1,0:T(8,128)(2,1)S(1)}, bf16[1,272,512]{2,1,0:T(8,128)(2,1)S(1)}, u32[]{:S(2)}, u32[]{:S(2)}) collective-permute-start(bf16[1,272,512]{2,1,0:T(8,128)(2,1)S(1)} %broadcast_in_dim_reshape.3), channel_id=1, source_target_pairs={{0,8},{1,9},{2,10},{3,11},{4,12},{5,13},{6,14},{7,15},{8,16},{9,17... | collective-permute-start | bytes 835592 | tf_op jit(solution)/shard_map/ppermute | solution.py:701
  29.3 17.8 %collective-permute-start.5 = (bf16[1,272,512]{2,1,0:T(8,128)(2,1)S(1)}, bf16[1,272,512]{2,1,0:T(8,128)(2,1)S(1)}, u32[]{:S(2)}, u32[]{:S(2)}) collective-permute-start(bf16[1,272,512]{2,1,0:T(8,128)(2,1)S(1)} %broadcast_in_dim_reshape.3), channel_id=1, source_target_pairs={{0,16},{1,17},{2,18},{3,19},{4,20},{5,21},{6,22},{7,23},{8,24},{9,... | collective-permute-start | bytes 835592 | tf_op jit(solution)/shard_map/ppermute | solution.py:701
  32.5 29.9 %copy-start.41 = (bf16[8,80,512]{2,1,0:T(8,128)(2,1)}, bf16[8,80,512]{2,1,0:T(8,128)(2,1)S(1)}, u32[]{:S(2)}) copy-start(bf16[8,80,512]{2,1,0:T(8,128)(2,1)S(1)} %constant_dynamic-update-slice_fusion.12.refs_8_) | copy-start | bytes 1966084
  32.5 24.3 %collective-permute-start.19 = (bf16[8,80,512]{2,1,0:T(8,128)(2,1)S(1)}, bf16[8,80,512]{2,1,0:T(8,128)(2,1)S(1)}, u32[]{:S(2)}, u32[]{:S(2)}) collective-permute-start(bf16[8,80,512]{2,1,0:T(8,128)(2,1)S(1)} %constant_dynamic-update-slice_fusion.12.refs_8_), channel_id=1, source_target_pairs={{0,2},{1,3},{2,0},{3,1},{4,6},{5,7},{6,4},{7,5},{8,10},{9,11},{10,... | collective-permute-start | bytes 1966088 | tf_op jit(solution)/shard_map/ppermute | solution.py:701
  33.8 28.6 %copy-start.43 = (bf16[8,64,512]{2,1,0:T(8,128)(2,1)}, bf16[8,64,512]{2,1,0:T(8,128)(2,1)S(1)}, u32[]{:S(2)}) copy-start(bf16[8,64,512]{2,1,0:T(8,128)(2,1)S(1)} %constant_dynamic-update-slice_fusion.2.refs_0_) | copy-start | bytes 1572868
  33.8 24.7 %collective-permute-start.8 = (bf16[8,64,512]{2,1,0:T(8,128)(2,1)S(1)}, bf16[8,64,512]{2,1,0:T(8,128)(2,1)S(1)}, u32[]{:S(2)}, u32[]{:S(2)}) collective-permute-start(bf16[8,64,512]{2,1,0:T(8,128)(2,1)S(1)} %constant_dynamic-update-slice_fusion.2.refs_0_), channel_id=1, source_target_pairs={{0,2},{1,3},{2,0},{3,1},{4,6},{5,7},{6,4},{7,5},{8,10},{9,11},{10,... | collective-permute-start | bytes 1572872 | tf_op jit(solution)/shard_map/ppermute | solution.py:701
  34.2 28.3 %copy-start.42 = (bf16[8,64,512]{2,1,0:T(8,128)(2,1)}, bf16[8,64,512]{2,1,0:T(8,128)(2,1)S(1)}, u32[]{:S(2)}) copy-start(bf16[8,64,512]{2,1,0:T(8,128)(2,1)S(1)} %constant_dynamic-update-slice_fusion.7.refs_4_) | copy-start | bytes 1572868
  34.2 26.8 %collective-permute-start.15 = (bf16[8,64,512]{2,1,0:T(8,128)(2,1)S(1)}, bf16[8,64,512]{2,1,0:T(8,128)(2,1)S(1)}, u32[]{:S(2)}, u32[]{:S(2)}) collective-permute-start(bf16[8,64,512]{2,1,0:T(8,128)(2,1)S(1)} %constant_dynamic-update-slice_fusion.7.refs_4_), channel_id=1, source_target_pairs={{0,4},{1,5},{2,6},{3,7},{4,0},{5,1},{6,2},{7,3},{8,12},{9,13},{10,... | collective-permute-start | bytes 1572872 | tf_op jit(solution)/shard_map/ppermute | solution.py:701
  37.0 24.0 %collective-permute-start.16 = (bf16[8,64,512]{2,1,0:T(8,128)(2,1)S(1)}, bf16[8,64,512]{2,1,0:T(8,128)(2,1)S(1)}, u32[]{:S(2)}, u32[]{:S(2)}) collective-permute-start(bf16[8,64,512]{2,1,0:T(8,128)(2,1)S(1)} %constant_dynamic-update-slice_fusion.7.refs_4_), channel_id=1, source_target_pairs={{0,1},{1,0},{2,3},{3,2},{4,5},{5,4},{6,7},{7,6},{8,9},{9,8},{10,11... | collective-permute-start | bytes 1572872 | tf_op jit(solution)/shard_map/ppermute | solution.py:701
  47.1 8.4 %collective-permute-start.6 = (bf16[1,272,512]{2,1,0:T(8,128)(2,1)S(1)}, bf16[1,272,512]{2,1,0:T(8,128)(2,1)S(1)}, u32[]{:S(2)}, u32[]{:S(2)}) collective-permute-start(bf16[1,272,512]{2,1,0:T(8,128)(2,1)S(1)} %broadcast_in_dim_reshape.3), channel_id=1, source_target_pairs={{0,24},{1,25},{2,26},{3,27},{4,28},{5,29},{6,30},{7,31},{8,0},{9,1... | collective-permute-start | bytes 835592 | tf_op jit(solution)/shard_map/ppermute | solution.py:701
  55.5 7.2 %collective-permute-start.20 = (bf16[8,80,512]{2,1,0:T(8,128)(2,1)S(1)}, bf16[8,80,512]{2,1,0:T(8,128)(2,1)S(1)}, u32[]{:S(2)}, u32[]{:S(2)}) collective-permute-start(bf16[8,80,512]{2,1,0:T(8,128)(2,1)S(1)} %constant_dynamic-update-slice_fusion.12.refs_8_), channel_id=1, source_target_pairs={{0,1},{1,0},{2,3},{3,2},{4,5},{5,4},{6,7},{7,6},{8,9},{9,8},{10,11... | collective-permute-start | bytes 1966088 | tf_op jit(solution)/shard_map/ppermute | solution.py:701
  56.8 10.0 %collective-permute-start.21 = (bf16[8,80,512]{2,1,0:T(8,128)(2,1)S(1)}, bf16[8,80,512]{2,1,0:T(8,128)(2,1)S(1)}, u32[]{:S(2)}, u32[]{:S(2)}) collective-permute-start(bf16[8,80,512]{2,1,0:T(8,128)(2,1)S(1)} %collective-permute-done.19.refs_9_), channel_id=1, source_target_pairs={{0,1},{1,0},{2,3},{3,2},{4,5},{5,4},{6,7},{7,6},{8,9},{9,8},{10,11... | collective-permute-start | bytes 1966088 | tf_op jit(solution)/shard_map/ppermute | solution.py:701
  58.6 5.4 %collective-permute-start.10 = (bf16[8,64,512]{2,1,0:T(8,128)(2,1)S(1)}, bf16[8,64,512]{2,1,0:T(8,128)(2,1)S(1)}, u32[]{:S(2)}, u32[]{:S(2)}) collective-permute-start(bf16[8,64,512]{2,1,0:T(8,128)(2,1)S(1)} %collective-permute-done.8.refs_1_), channel_id=1, source_target_pairs={{0,1},{1,0},{2,3},{3,2},{4,5},{5,4},{6,7},{7,6},{8,9},{9,8},{10,11... | collective-permute-start | bytes 1572872 | tf_op jit(solution)/shard_map/ppermute | solution.py:701
  61.0 4.2 %collective-permute-start.9 = (bf16[8,64,512]{2,1,0:T(8,128)(2,1)S(1)}, bf16[8,64,512]{2,1,0:T(8,128)(2,1)S(1)}, u32[]{:S(2)}, u32[]{:S(2)}) collective-permute-start(bf16[8,64,512]{2,1,0:T(8,128)(2,1)S(1)} %constant_dynamic-update-slice_fusion.2.refs_0_), channel_id=1, source_target_pairs={{0,1},{1,0},{2,3},{3,2},{4,5},{5,4},{6,7},{7,6},{8,9},{9,8},{10,11... | collective-permute-start | bytes 1572872 | tf_op jit(solution)/shard_map/ppermute | solution.py:701
  61.9 3.3 collective-permute-start.17
  62.7 13.4 %collective-permute-start.25 = (bf16[4,128,512]{2,1,0:T(8,128)(2,1)S(1)}, bf16[4,128,512]{2,1,0:T(8,128)(2,1)S(1)}, u32[]{:S(2)}, u32[]{:S(2)}) collective-permute-start(bf16[4,128,512]{2,1,0:T(8,128)(2,1)S(1)} %pad_maximum_fusion.7), channel_id=1, source_target_pairs={{0,4},{1,5},{2,6},{3,7},{4,0},{5,1},{6,2},{7,3},{8,12},{9,13},{10,... | collective-permute-start | bytes 1572872 | tf_op jit(solution)/shard_map/ppermute | solution.py:701
  64.0 15.0 %collective-permute-start.7 = (bf16[4,144,512]{2,1,0:T(8,128)(2,1)S(1)}, bf16[4,144,512]{2,1,0:T(8,128)(2,1)S(1)}, u32[]{:S(2)}, u32[]{:S(2)}) collective-permute-start(bf16[4,144,512]{2,1,0:T(8,128)(2,1)S(1)} %pad_maximum_fusion.6), channel_id=1, source_target_pairs={{0,2},{1,3},{2,0},{3,1},{4,6},{5,7},{6,4},{7,5},{8,10},{9,11},{10,... | collective-permute-start | bytes 1769480 | tf_op jit(solution)/shard_map/ppermute | solution.py:701
  77.8 34.2 %collective-permute-start.26 = (bf16[8,128,512]{2,1,0:T(8,128)(2,1)}, bf16[8,128,512]{2,1,0:T(8,128)(2,1)}, u32[]{:S(2)}, u32[]{:S(2)}) collective-permute-start(bf16[8,128,512]{2,1,0:T(8,128)(2,1)} %constant_dynamic-update-slice_fusion.19.refs_4_), channel_id=1, source_target_pairs={{0,2},{1,3},{2,0},{3,1},{4,6},{5,7},{6,4},{7,5},{8,10},{9,11},{10,... | collective-permute-start | bytes 3145736 | tf_op jit(solution)/shard_map/ppermute | solution.py:701
  80.7 29.6 %collective-permute-start.22 = (bf16[8,144,512]{2,1,0:T(8,128)(2,1)}, bf16[8,144,512]{2,1,0:T(8,128)(2,1)}, u32[]{:S(2)}, u32[]{:S(2)}) collective-permute-start(bf16[8,144,512]{2,1,0:T(8,128)(2,1)} %constant_dynamic-update-slice_fusion.17.refs_0_), channel_id=1, source_target_pairs={{0,4},{1,5},{2,6},{3,7},{4,0},{5,1},{6,2},{7,3},{8,12},{9,13},{10,... | collective-permute-start | bytes 3538952 | tf_op jit(solution)/shard_map/ppermute | solution.py:701
  110.3 9.0 %collective-permute-start.23 = (bf16[8,144,512]{2,1,0:T(8,128)(2,1)}, bf16[8,144,512]{2,1,0:T(8,128)(2,1)S(1)}, u32[]{:S(2)}, u32[]{:S(2)}) collective-permute-start(bf16[8,144,512]{2,1,0:T(8,128)(2,1)} %constant_dynamic-update-slice_fusion.17.refs_0_), channel_id=1, source_target_pairs={{0,1},{1,0},{2,3},{3,2},{4,5},{5,4},{6,7},{7,6},{8,9},{9,8},{10,11... | collective-permute-start | bytes 3538952 | tf_op jit(solution)/shard_map/ppermute | solution.py:701
  111.9 7.4 %collective-permute-start.24 = (bf16[8,144,512]{2,1,0:T(8,128)(2,1)}, bf16[8,144,512]{2,1,0:T(8,128)(2,1)S(1)}, u32[]{:S(2)}, u32[]{:S(2)}) collective-permute-start(bf16[8,144,512]{2,1,0:T(8,128)(2,1)} %collective-permute-done.22.refs_1_), channel_id=1, source_target_pairs={{0,1},{1,0},{2,3},{3,2},{4,5},{5,4},{6,7},{7,6},{8,9},{9,8},{10,11... | collective-permute-start | bytes 3538952 | tf_op jit(solution)/shard_map/ppermute | solution.py:701
  112.0 5.8 %collective-permute-start.27 = (bf16[8,128,512]{2,1,0:T(8,128)(2,1)}, bf16[8,128,512]{2,1,0:T(8,128)(2,1)S(1)}, u32[]{:S(2)}, u32[]{:S(2)}) collective-permute-start(bf16[8,128,512]{2,1,0:T(8,128)(2,1)} %constant_dynamic-update-slice_fusion.19.refs_4_), channel_id=1, source_target_pairs={{0,1},{1,0},{2,3},{3,2},{4,5},{5,4},{6,7},{7,6},{8,9},{9,8},{10,11... | collective-permute-start | bytes 3145736 | tf_op jit(solution)/shard_map/ppermute | solution.py:701
  112.4 6.9 %collective-permute-start.28 = (bf16[8,128,512]{2,1,0:T(8,128)(2,1)}, bf16[8,128,512]{2,1,0:T(8,128)(2,1)S(1)}, u32[]{:S(2)}, u32[]{:S(2)}) collective-permute-start(bf16[8,128,512]{2,1,0:T(8,128)(2,1)} %collective-permute-done.26.refs_5_), channel_id=1, source_target_pairs={{0,1},{1,0},{2,3},{3,2},{4,5},{5,4},{6,7},{7,6},{8,9},{9,8},{10,11... | collective-permute-start | bytes 3145736 | tf_op jit(solution)/shard_map/ppermute | solution.py:701
  189.0 4.6 %collective-permute-start.29 = (bf16[8,272,512]{2,1,0:T(8,128)(2,1)}, bf16[8,272,512]{2,1,0:T(8,128)(2,1)S(1)}, u32[]{:S(2)}, u32[]{:S(2)}) collective-permute-start(bf16[8,272,512]{2,1,0:T(8,128)(2,1)} %get-tuple-element.126), channel_id=1, source_target_pairs={{0,1},{1,0},{2,3},{3,2},{4,5},{5,4},{6,7},{7,6},{8,9},{9,8},{10,11... | collective-permute-start | bytes 6684680 | tf_op jit(solution)/shard_map/ppermute | solution.py:701
  197.0 26.1 %collective-permute-start.30 = (bf16[2,2,272,512]{3,2,0,1:T(8,128)(2,1)}, bf16[2,2,272,512]{3,2,0,1:T(8,128)(2,1)}, u32[]{:S(2)}, u32[]{:S(2)}) collective-permute-start(bf16[2,2,272,512]{3,2,0,1:T(8,128)(2,1)} %fusion), channel_id=1, source_target_pairs={{0,2},{1,3},{2,0},{3,1},{4,6},{5,7},{6,4},{7,5},{8,10},{9,11},{10,... | collective-permute-start | bytes 3342344 | tf_op jit(solution)/shard_map/ppermute | solution.py:701
  223.1 4.0 collective-permute-start.31
  226.8 26.7 %collective-permute-start.32 = (bf16[2,272,512]{2,1,0:T(8,128)(2,1)}, bf16[2,272,512]{2,1,0:T(8,128)(2,1)}, u32[]{:S(2)}, u32[]{:S(2)}) collective-permute-start(bf16[2,272,512]{2,1,0:T(8,128)(2,1)} %fusion.1), channel_id=1, source_target_pairs={{0,4},{1,5},{2,6},{3,7},{4,0},{5,1},{6,2},{7,3},{8,12},{9,13},{10,... | collective-permute-start | bytes 1671176 | tf_op jit(solution)/shard_map/ppermute | solution.py:701
  227.1 26.4 %copy-start.32 = (bf16[4,272,512]{2,1,0:T(8,128)(2,1)}, bf16[4,272,512]{2,1,0:T(8,128)(2,1)S(1)}, u32[]{:S(2)}) copy-start(bf16[4,272,512]{2,1,0:T(8,128)(2,1)S(1)} %collective-permute-done.31) | copy-start | bytes 3342340
  228.2 25.3 %collective-permute-start.33 = (bf16[1,2,272,512]{3,2,1,0:T(8,128)(2,1)}, bf16[1,2,272,512]{3,2,1,0:T(8,128)(2,1)}, u32[]{:S(2)}, u32[]{:S(2)}) collective-permute-start(bf16[1,2,272,512]{3,2,1,0:T(8,128)(2,1)} %fusion.2), channel_id=1, source_target_pairs={{0,4},{1,5},{2,6},{3,7},{4,0},{5,1},{6,2},{7,3},{8,12},{9,13},{10,... | collective-permute-start | bytes 1671176 | tf_op jit(solution)/shard_map/ppermute | solution.py:701
  253.5 6.6 %collective-permute-start.35 = (bf16[4,272,512]{2,1,0:T(8,128)(2,1)}, bf16[4,272,512]{2,1,0:T(8,128)(2,1)S(1)}, u32[]{:S(2)}, u32[]{:S(2)}) collective-permute-start(bf16[4,272,512]{2,1,0:T(8,128)(2,1)} %get-tuple-element.160), channel_id=1, source_target_pairs={{0,1},{1,0},{2,3},{3,2},{4,5},{5,4},{6,7},{7,6},{8,9},{9,8},{10,11... | collective-permute-start | bytes 3342344 | tf_op jit(solution)/shard_map/ppermute | solution.py:701
  255.3 39.3 %copy-start = (bf16[2,272,512]{2,1,0:T(8,128)(2,1)}, bf16[2,272,512]{2,1,0:T(8,128)(2,1)S(1)}, u32[]{:S(2)}) copy-start(bf16[2,272,512]{2,1,0:T(8,128)(2,1)S(1)} %dynamic-slice_bitcast_fusion.2) | copy-start | bytes 1671172
  256.7 38.0 %copy-start.2 = (bf16[2,272,512]{2,1,0:T(8,128)(2,1)}, bf16[2,272,512]{2,1,0:T(8,128)(2,1)S(1)}, u32[]{:S(2)}) copy-start(bf16[2,272,512]{2,1,0:T(8,128)(2,1)S(1)} %dynamic-slice_bitcast_fusion.1) | copy-start | bytes 1671172
  256.7 38.0 %copy-start.15 = (bf16[1,272,512]{2,1,0:T(8,128)(2,1)}, bf16[1,272,512]{2,1,0:T(8,128)(2,1)S(1)}, u32[]{:S(2)}) copy-start(bf16[1,272,512]{2,1,0:T(8,128)(2,1)S(1)} %dynamic-slice_bitcast_fusion.10) | copy-start | bytes 835588
  258.4 36.3 %copy-start.4 = (bf16[2,272,512]{2,1,0:T(8,128)(2,1)}, bf16[2,272,512]{2,1,0:T(8,128)(2,1)S(1)}, u32[]{:S(2)}) copy-start(bf16[2,272,512]{2,1,0:T(8,128)(2,1)S(1)} %dynamic-slice_bitcast_fusion) | copy-start | bytes 1671172
  258.4 36.3 %copy-start.17 = (bf16[1,272,512]{2,1,0:T(8,128)(2,1)}, bf16[1,272,512]{2,1,0:T(8,128)(2,1)S(1)}, u32[]{:S(2)}) copy-start(bf16[1,272,512]{2,1,0:T(8,128)(2,1)S(1)} %dynamic-slice_bitcast_fusion.8) | copy-start | bytes 835588
  259.8 23.2 %collective-permute-start.34 = (bf16[1,272,512]{2,1,0:T(8,128)(2,1)S(1)}, bf16[1,272,512]{2,1,0:T(8,128)(2,1)S(1)}, u32[]{:S(2)}, u32[]{:S(2)}) collective-permute-start(bf16[1,272,512]{2,1,0:T(8,128)(2,1)S(1)} %fusion.5), channel_id=1, source_target_pairs={{0,2},{1,3},{2,0},{3,1},{4,6},{5,7},{6,4},{7,5},{8,10},{9,11},{10,... | collective-permute-start | bytes 835592 | tf_op jit(solution)/shard_map/ppermute | solution.py:701
  260.3 22.8 %collective-permute-start.36 = (bf16[1,2,272,512]{3,2,1,0:T(8,128)(2,1)S(1)}, bf16[1,2,272,512]{3,2,1,0:T(8,128)(2,1)S(1)}, u32[]{:S(2)}, u32[]{:S(2)}) collective-permute-start(bf16[1,2,272,512]{3,2,1,0:T(8,128)(2,1)S(1)} %fusion.3), channel_id=1, source_target_pairs={{0,2},{1,3},{2,0},{3,1},{4,6},{5,7},{6,4},{7,5},{8,10},{9,11},{10,... | collective-permute-start | bytes 1671176 | tf_op jit(solution)/shard_map/ppermute | solution.py:701
  283.1 13.6 %collective-permute-start.37 = (bf16[8,208,512]{2,1,0:T(8,128)(2,1)}, bf16[8,208,512]{2,1,0:T(8,128)(2,1)S(1)}, u32[]{:S(2)}, u32[]{:S(2)}) collective-permute-start(bf16[8,208,512]{2,1,0:T(8,128)(2,1)} %get-tuple-element.176), channel_id=1, source_target_pairs={{0,1},{1,0},{2,3},{3,2},{4,5},{5,4},{6,7},{7,6},{8,9},{9,8},{10,11... | collective-permute-start | bytes 5111816 | tf_op jit(solution)/shard_map/ppermute | solution.py:701
  285.2 8.3 %collective-permute-start.38 = (bf16[1,272,512]{2,1,0:T(8,128)(2,1)S(1)}, bf16[1,272,512]{2,1,0:T(8,128)(2,1)S(1)}, u32[]{:S(2)}, u32[]{:S(2)}) collective-permute-start(bf16[1,272,512]{2,1,0:T(8,128)(2,1)S(1)} %fusion.4), channel_id=1, source_target_pairs={{0,4},{1,5},{2,6},{3,7},{4,0},{5,1},{6,2},{7,3},{8,12},{9,13},{10,... | collective-permute-start | bytes 835592 | tf_op jit(solution)/shard_map/ppermute | solution.py:701
  298.8 26.1 %copy-start.3 = (bf16[2,272,512]{2,1,0:T(8,128)(2,1)S(1)}, bf16[2,272,512]{2,1,0:T(8,128)(2,1)}, u32[]{:S(2)}) copy-start(bf16[2,272,512]{2,1,0:T(8,128)(2,1)} %copy-done.2) | copy-start | bytes 1671172
  324.0 6.3 %collective-permute-start.39 = (bf16[8,208,512]{2,1,0:T(8,128)(2,1)}, bf16[8,208,512]{2,1,0:T(8,128)(2,1)}, u32[]{:S(2)}, u32[]{:S(2)}) collective-permute-start(bf16[8,208,512]{2,1,0:T(8,128)(2,1)} %get-tuple-element.193), channel_id=1, source_target_pairs={{0,1},{1,0},{2,3},{3,2},{4,5},{5,4},{6,7},{7,6},{8,9},{9,8},{10,11... | collective-permute-start | bytes 5111816 | tf_op jit(solution)/shard_map/ppermute | solution.py:701
  327.5 8.3 %collective-permute-start.44 = (bf16[272,512]{1,0:T(8,128)(2,1)S(1)}, bf16[272,512]{1,0:T(8,128)(2,1)S(1)}, u32[]{:S(2)}, u32[]{:S(2)}) collective-permute-start(bf16[272,512]{1,0:T(8,128)(2,1)S(1)} %copy-done.39), channel_id=1, source_target_pairs={{0,8},{1,9},{2,10},{3,11},{4,12},{5,13},{6,14},{7,15},{8,16},{9,17... | collective-permute-start | bytes 835592 | tf_op jit(solution)/shard_map/ppermute | solution.py:854
  327.6 24.1 %collective-permute-start.45 = (bf16[272,512]{1,0:T(8,128)(2,1)S(1)}, bf16[272,512]{1,0:T(8,128)(2,1)S(1)}, u32[]{:S(2)}, u32[]{:S(2)}) collective-permute-start(bf16[272,512]{1,0:T(8,128)(2,1)S(1)} %copy-done.38), channel_id=1, source_target_pairs={{0,16},{1,17},{2,18},{3,19},{4,20},{5,21},{6,22},{7,23},{8,24},{9,... | collective-permute-start | bytes 835592 | tf_op jit(solution)/shard_map/ppermute | solution.py:854
  328.3 25.1 %collective-permute-start.46 = (bf16[272,512]{1,0:T(8,128)(2,1)S(1)}, bf16[272,512]{1,0:T(8,128)(2,1)S(1)}, u32[]{:S(2)}, u32[]{:S(2)}) collective-permute-start(bf16[272,512]{1,0:T(8,128)(2,1)S(1)} %copy-done.37), channel_id=1, source_target_pairs={{0,24},{1,25},{2,26},{3,27},{4,28},{5,29},{6,30},{7,31},{8,0},{9,1... | collective-permute-start | bytes 835592 | tf_op jit(solution)/shard_map/ppermute | solution.py:854
  329.9 23.5 %collective-permute-start.43 = (bf16[1,2,208,512]{3,2,1,0:T(8,128)(2,1)S(1)}, bf16[1,2,208,512]{3,2,1,0:T(8,128)(2,1)S(1)}, u32[]{:S(2)}, u32[]{:S(2)}) collective-permute-start(bf16[1,2,208,512]{3,2,1,0:T(8,128)(2,1)S(1)} %copy-done.36), channel_id=1, source_target_pairs={{0,4},{1,5},{2,6},{3,7},{4,0},{5,1},{6,2},{7,3},{8,12},{9,13},{10,... | collective-permute-start | bytes 1277960 | tf_op jit(solution)/shard_map/ppermute | solution.py:701
  331.2 22.2 %collective-permute-start.42 = (bf16[1,2,208,512]{3,2,1,0:T(8,128)(2,1)S(1)}, bf16[1,2,208,512]{3,2,1,0:T(8,128)(2,1)S(1)}, u32[]{:S(2)}, u32[]{:S(2)}) collective-permute-start(bf16[1,2,208,512]{3,2,1,0:T(8,128)(2,1)S(1)} %copy-done.35), channel_id=1, source_target_pairs={{0,2},{1,3},{2,0},{3,1},{4,6},{5,7},{6,4},{7,5},{8,10},{9,11},{10,... | collective-permute-start | bytes 1277960 | tf_op jit(solution)/shard_map/ppermute | solution.py:701
  335.8 20.0 %collective-permute-start.41 = (bf16[1,2,208,512]{3,2,1,0:T(8,128)(2,1)S(1)}, bf16[1,2,208,512]{3,2,1,0:T(8,128)(2,1)S(1)}, u32[]{:S(2)}, u32[]{:S(2)}) collective-permute-start(bf16[1,2,208,512]{3,2,1,0:T(8,128)(2,1)S(1)} %fusion.11), channel_id=1, source_target_pairs={{0,4},{1,5},{2,6},{3,7},{4,0},{5,1},{6,2},{7,3},{8,12},{9,13},{10,... | collective-permute-start | bytes 1277960 | tf_op jit(solution)/shard_map/ppermute | solution.py:701
  351.8 10.7 %collective-permute-start.40 = (bf16[1,2,208,512]{3,2,1,0:T(8,128)(2,1)S(1)}, bf16[1,2,208,512]{3,2,1,0:T(8,128)(2,1)S(1)}, u32[]{:S(2)}, u32[]{:S(2)}) collective-permute-start(bf16[1,2,208,512]{3,2,1,0:T(8,128)(2,1)S(1)} %fusion.10), channel_id=1, source_target_pairs={{0,2},{1,3},{2,0},{3,1},{4,6},{5,7},{6,4},{7,5},{8,10},{9,11},{10,... | collective-permute-start | bytes 1277960 | tf_op jit(solution)/shard_map/ppermute | solution.py:701
  354.8 16.9 %collective-permute-start.50 = (bf16[1,208,512]{2,1,0:T(8,128)(2,1)S(1)}, bf16[1,208,512]{2,1,0:T(8,128)(2,1)S(1)}, u32[]{:S(2)}, u32[]{:S(2)}) collective-permute-start(bf16[1,208,512]{2,1,0:T(8,128)(2,1)S(1)} %fusion.12), channel_id=1, source_target_pairs={{0,2},{1,3},{2,0},{3,1},{4,6},{5,7},{6,4},{7,5},{8,10},{9,11},{10,... | collective-permute-start | bytes 638984 | tf_op jit(solution)/shard_map/ppermute | solution.py:701
  355.4 16.3 %collective-permute-start.49 = (bf16[1,208,512]{2,1,0:T(8,128)(2,1)S(1)}, bf16[1,208,512]{2,1,0:T(8,128)(2,1)S(1)}, u32[]{:S(2)}, u32[]{:S(2)}) collective-permute-start(bf16[1,208,512]{2,1,0:T(8,128)(2,1)S(1)} %fusion.13), channel_id=1, source_target_pairs={{0,4},{1,5},{2,6},{3,7},{4,0},{5,1},{6,2},{7,3},{8,12},{9,13},{10,... | collective-permute-start | bytes 638984 | tf_op jit(solution)/shard_map/ppermute | solution.py:701
  356.0 15.6 %collective-permute-start.48 = (bf16[1,208,512]{2,1,0:T(8,128)(2,1)S(1)}, bf16[1,208,512]{2,1,0:T(8,128)(2,1)S(1)}, u32[]{:S(2)}, u32[]{:S(2)}) collective-permute-start(bf16[1,208,512]{2,1,0:T(8,128)(2,1)S(1)} %fusion.14), channel_id=1, source_target_pairs={{0,2},{1,3},{2,0},{3,1},{4,6},{5,7},{6,4},{7,5},{8,10},{9,11},{10,... | collective-permute-start | bytes 638984 | tf_op jit(solution)/shard_map/ppermute | solution.py:701
  362.6 5.1 %collective-permute-start.47 = (bf16[1,208,512]{2,1,0:T(8,128)(2,1)S(1)}, bf16[1,208,512]{2,1,0:T(8,128)(2,1)S(1)}, u32[]{:S(2)}, u32[]{:S(2)}) collective-permute-start(bf16[1,208,512]{2,1,0:T(8,128)(2,1)S(1)} %fusion.15), channel_id=1, source_target_pairs={{0,4},{1,5},{2,6},{3,7},{4,0},{5,1},{6,2},{7,3},{8,12},{9,13},{10,... | collective-permute-start | bytes 638984 | tf_op jit(solution)/shard_map/ppermute | solution.py:701
  372.4 5.3 %collective-permute-start.51 = (bf16[208,512]{1,0:T(8,128)(2,1)S(1)}, bf16[208,512]{1,0:T(8,128)(2,1)S(1)}, u32[]{:S(2)}, u32[]{:S(2)}) collective-permute-start(bf16[208,512]{1,0:T(8,128)(2,1)S(1)} %get-tuple-element.210), channel_id=1, source_target_pairs={{0,8},{1,9},{2,10},{3,11},{4,12},{5,13},{6,14},{7,15},{8,16},{9,17... | collective-permute-start | bytes 638984 | tf_op jit(solution)/shard_map/ppermute | solution.py:854
  372.5 17.4 %collective-permute-start.52 = (bf16[208,512]{1,0:T(8,128)(2,1)S(1)}, bf16[208,512]{1,0:T(8,128)(2,1)S(1)}, u32[]{:S(2)}, u32[]{:S(2)}) collective-permute-start(bf16[208,512]{1,0:T(8,128)(2,1)S(1)} %get-tuple-element.212), channel_id=1, source_target_pairs={{0,16},{1,17},{2,18},{3,19},{4,20},{5,21},{6,22},{7,23},{8,24},{9,... | collective-permute-start | bytes 638984 | tf_op jit(solution)/shard_map/ppermute | solution.py:854
  375.6 19.3 %collective-permute-start.53 = (bf16[208,512]{1,0:T(8,128)(2,1)S(1)}, bf16[208,512]{1,0:T(8,128)(2,1)S(1)}, u32[]{:S(2)}, u32[]{:S(2)}) collective-permute-start(bf16[208,512]{1,0:T(8,128)(2,1)S(1)} %get-tuple-element.211), channel_id=1, source_target_pairs={{0,24},{1,25},{2,26},{3,27},{4,28},{5,29},{6,30},{7,31},{8,0},{9,1... | collective-permute-start | bytes 638984 | tf_op jit(solution)/shard_map/ppermute | solution.py:854
  (47 other events, 272.4 us)
